TPU v7x, 32 devices: a whole 2x2x4 slice. The times are simulated.
32 devices in a mesh: seq: 16 (over z, y, core), pair: 2 (over x).
Axes of the slice: x: 2, y: 2, z: 4, core: 2. Of those that a mesh axis runs over, the one named last changes fastest.
Arguments:
- student: float32 [10240, 1408], P('seq'), may hold values from -640 to 640
- teacher: float32 [10240, 1408], P('seq'), may hold values from -640 to 640
Outputs:
- student_grad: float32 [10240, 1408], P('seq')
All inputs are finite; a program needn't handle non-finite values.
Results may differ from a plain program's by a relative error of at most 0.0059.
Values may be sent and summed in bfloat16 or wider, within the bound.
No kernel may reach another device: no remote copies, remote signals or barrier semaphores. Data moves between devices by JAX's collectives and lax.ppermute only.
A program may use at most 64 MiB of HBM per device.

v0:
```python
import functools
import math

import jax
import jax.numpy as jnp
from jax import lax
from jax.experimental import pallas as pl
from jax.experimental.pallas import tpu as pltpu
from jax.sharding import PartitionSpec as P

CORES = 2
ROW_TILE = 16
VMEM_LIMIT = 32 * 1024 * 1024


def normalized(values):
    width = values.shape[1]
    scale = lax.rsqrt(jnp.sum(values * values, axis=1, keepdims=True) + width * 1e-06)
    return scale, (values * scale).astype(jnp.bfloat16)


def own_kernel(student, teacher, half, scale):
    scale[...], half[0] = normalized(student[...])
    _, half[1] = normalized(teacher[...])


def normalize_own(student, teacher):
    rows, width = student.shape
    block = rows // 4
    by_row = pl.BlockSpec((block, width), lambda i: (i, 0))
    return pl.pallas_call(
        own_kernel,
        grid=(rows // block,),
        in_specs=[by_row, by_row],
        out_specs=[
            pl.BlockSpec((2, block, width), lambda i: (0, i, 0)),
            pl.BlockSpec((block, 1), lambda i: (i, 0)),
        ],
        out_shape=[
            jax.ShapeDtypeStruct((2, rows, width), jnp.bfloat16),
            jax.ShapeDtypeStruct((rows, 1), jnp.float32),
        ],
        compiler_params=pltpu.CompilerParams(vmem_limit_bytes=VMEM_LIMIT),
        cost_estimate=pl.CostEstimate(
            flops=6 * rows * width, bytes_accessed=12 * rows * width, transcendentals=2 * rows
        ),
    )(student, teacher)


def pack_kernel(counts, which, student, teacher, *packed):
    at = 0
    for out, count in zip(packed, counts):
        out[:count, :] = normalized(student[at : at + count, :])[1]
        out[count:, :] = normalized(teacher[at : at + count, :])[1]
        at += count


def pack_share(student, teacher, pair_index, counts):
    share, width = sum(counts), student.shape[1]
    mine = pl.BlockSpec((share, width), lambda i, which: (which[0], 0))
    return pl.pallas_call(
        functools.partial(pack_kernel, counts),
        grid_spec=pltpu.PrefetchScalarGridSpec(
            num_scalar_prefetch=1,
            grid=(1,),
            in_specs=[mine, mine],
            out_specs=[pl.BlockSpec((2 * n, width), lambda i, which: (0, 0)) for n in counts],
        ),
        out_shape=[jax.ShapeDtypeStruct((2 * n, width), jnp.bfloat16) for n in counts],
        compiler_params=pltpu.CompilerParams(vmem_limit_bytes=VMEM_LIMIT),
        cost_estimate=pl.CostEstimate(
            flops=6 * share * width, bytes_accessed=12 * share * width, transcendentals=2 * share
        ),
    )(jnp.reshape(pair_index, (1,)).astype(jnp.int32), student, teacher)


def relation_kernel(margin, weight, counts, terms, project, *refs):
    refs = list(refs)
    rows = refs.pop(0)
    partners = [refs.pop(0) for _ in counts]
    added = [refs.pop(0) for _ in range(terms)]
    student, scale = (refs.pop(0), refs.pop(0)) if project else (None, None)
    out, all_s, all_t = refs

    @pl.when(pl.program_id(0) == 0)
    def _():
        at = 0
        for partner, count in zip(partners, counts):
            all_s[at : at + count, :] = partner[:count, :]
            all_t[at : at + count, :] = partner[count:, :]
            at += count

    contract = (((1,), (1,)), ((), ()))
    s_rel = lax.dot_general(rows[0], all_s[...], contract, preferred_element_type=jnp.float32)
    t_rel = lax.dot_general(rows[1], all_t[...], contract, preferred_element_type=jnp.float32)
    delta = s_rel - t_rel
    shrink = jnp.maximum(delta - margin, 0.0) + jnp.minimum(delta + margin, 0.0)
    relation = (weight * shrink).astype(jnp.bfloat16)
    grad = jnp.dot(relation, all_s[...], preferred_element_type=jnp.float32)
    for term in added:
        grad = term[...] + grad
    if project:
        unit = student[...] * scale[...]
        grad = grad - unit * jnp.sum(unit * grad, axis=1, keepdims=True)
    out[...] = grad.astype(out.dtype)


def add_relation(half, partners, terms, margin, weight, project=None, dtype=jnp.float32):
    _, rows, width = half.shape
    block = rows // 2
    counts = tuple(x.shape[0] // 2 for x in partners)
    tokens = sum(counts)
    by_row = pl.BlockSpec((block, width), lambda i: (i, 0))
    operands = [half] + list(partners) + list(terms)
    specs = [pl.BlockSpec((2, block, width), lambda i: (0, i, 0))]
    specs += [pl.BlockSpec(x.shape, lambda i: (0, 0), pipeline_mode=pl.Buffered(1)) for x in partners]
    specs += [by_row] * len(terms)
    aliases = {1 + len(partners): 0} if terms and dtype == terms[0].dtype else {}
    if project is not None:
        operands += list(project)
        specs += [by_row, pl.BlockSpec((block, 1), lambda i: (i, 0))]
    return pl.pallas_call(
        functools.partial(relation_kernel, margin, weight, counts, len(terms), project is not None),
        grid=(rows // block,),
        in_specs=specs,
        out_specs=by_row,
        out_shape=jax.ShapeDtypeStruct((rows, width), dtype),
        scratch_shapes=[pltpu.VMEM((tokens, width), jnp.bfloat16)] * 2,
        input_output_aliases=aliases,
        compiler_params=pltpu.CompilerParams(vmem_limit_bytes=VMEM_LIMIT),
        cost_estimate=pl.CostEstimate(
            flops=6 * rows * tokens * width,
            bytes_accessed=(12 * rows + 4 * tokens) * width,
            transcendentals=0,
        ),
    )(*operands)


def ring_routes(count):
    chips = count // CORES
    order = list(range(0, chips, 2)) + list(range(1, chips, 2))[::-1]
    onward, back = [], []
    for place, chip in enumerate(order):
        following = order[(place + 1) % chips]
        for core in range(CORES):
            onward.append((chip * CORES + core, following * CORES + core))
            back.append((following * CORES + core, chip * CORES + core))
    swap = [(i, i ^ 1) for i in range(count)]
    return onward, back, swap


def halves(tokens):
    first = -(-tokens // (2 * ROW_TILE)) * ROW_TILE
    return first, tokens - first


def after(x, *values):
    return lax.optimization_barrier((x, *values))[0]


def local(student, teacher):
    rows, width = student.shape
    seq_count = lax.axis_size("seq")
    pair_count = lax.axis_size("pair")
    pair_index = lax.axis_index("pair")
    margin = 0.75 / math.sqrt(width)
    weight = 64.0 * width / math.sqrt(rows * seq_count)
    onward, back, swap = ring_routes(seq_count)
    hops = seq_count // CORES // 2
    counts = [n for part in halves(rows // pair_count) for n in halves(part)]
    pieces = pack_share(student, teacher, pair_index, counts)
    own_half, s_scale = normalize_own(student, teacher)
    other_half = lax.ppermute(own_half, "seq", swap)
    own, other = None, None

    def add(half, partners, terms, project=None, dtype=jnp.float32):
        return add_relation(half, partners, terms, margin, weight, project, dtype)

    def hop(chains, wait_for=()):
        sent = []
        for k, chain in enumerate(chains):
            if wait_for and k:
                chain = [after(x, *wait_for) for x in chain]
            sent.append([lax.ppermute(chain[0], "seq", onward), lax.ppermute(chain[1], "seq", back)])
        return sent

    def once(chains, arrived):
        return [[after(x, y) for x, y in zip(*both)] for both in zip(chains, arrived)]

    def flat(chains):
        return [x for chain in chains for x in chain]

    def terms(total):
        return [] if total is None else [total]

    far = [[pieces[0], pieces[2]], [pieces[1], pieces[3]]]
    near = [[pieces[2], pieces[0]], [pieces[3], pieces[1]]]
    batch = list(pieces)
    arrivals = []
    for step in range(1, hops):
        far = hop(far, () if own is None else (own, other))
        batch += flat(far)
        if step % 2 == 1 or step == hops - 1:
            other = add(other_half, batch, terms(other))
            own = add(own_half, batch, terms(own))
            batch = []
    near = once(near, far)
    theirs = []
    for k in range(1, pair_count):
        route = [(i, (i + k) % pair_count) for i in range(pair_count)]
        theirs.append([[lax.ppermute(x, "pair", route) for x in chain] for chain in far])
    for step in range(1, hops):
        near = hop(near, (own, other) if step % 2 == 0 else ())
        batch += flat(near)
        if step % 2 == 0 and step < hops - 1:
            other = add(other_half, batch, terms(other))
            own = add(own_half, batch, terms(own))
            batch = []
    far = hop(once(far, near), (own, other))
    other = add(other_half, batch, terms(other))
    moved = lax.ppermute(other, "seq", swap)
    partial_grad = add(own_half, batch, [own, moved], (student, s_scale), jnp.bfloat16)
    summed = partial_grad
    distance = 1
    while distance < pair_count:
        half = summed.astype(jnp.bfloat16)
        arrived = lax.ppermute(half, "pair", [(i, i ^ distance) for i in range(pair_count)])
        summed = half.astype(jnp.float32) + arrived.astype(jnp.float32)
        distance *= 2
    own, other = None, None
    for chains in theirs:
        batch = flat(far)
        far = hop(once(chains, far), (partial_grad,))
        other = add(other_half, batch, terms(other))
        own = add(own_half, batch, terms(own))
    batch = flat(far)
    other = add(other_half, batch, terms(other))
    moved = lax.ppermute(other, "seq", swap)
    total = add(own_half, batch, terms(own) + [moved], (student, s_scale))
    return s_scale * (summed + total)


def solution(mesh):
    placed = (P("seq", None), P("seq", None))
    return jax.shard_map(
        local, mesh=mesh, in_specs=placed, out_specs=P("seq", None), check_vma=False
    )
```

profile of v0, /device:TPU:0, one launch (start us, length us, event | category | flops | bytes accessed | tf_op | source)
XLA Modules:
  0.0 255.5 jit_solution(7269756975883100504)
XLA Ops:
  0.0 2.0 copy-done
  2.0 2.0 copy-done.4
  4.0 2.6 %shard_map.28 = (bf16[2,640,1408]{2,1,0:T(8,128)(2,1)}, f32[640,1]{1,0:T(8,128)S(1)}) custom-call(f32[640,1408]{1,0:T(8,128)S(1)} %copy-done, f32[640,1408]{1,0:T(8,128)S(1)} %copy-done.4), custom_call_target="tpu_custom_call" | custom-call | flops 5406720 | bytes 10813440 | tf_op jit(solution)/shard_map/pallas_call | solution.py:31
  7.1 2.0 copy-done.1
  11.6 2.6 %collective-permute-start = (bf16[160,1408]{1,0:T(8,128)(2,1)S(1)}, bf16[160,1408]{1,0:T(8,128)(2,1)S(1)}, u32[]{:S(2)}, u32[]{:S(2)}) collective-permute-start(bf16[160,1408]{1,0:T(8,128)(2,1)S(1)} %get-tuple-element.38.refs_1_), channel_id=1, source_target_pairs={{0,8},{2,10},{8,16},{10,18},{16,24},{18,26},{24,28},{26,30},{28,20... | collective-permute-start | bytes 1351688 | tf_op jit(solution)/shard_map/ppermute | solution.py:184
  16.2 9.1 %collective-permute-done.refs_5_ = bf16[160,1408]{1,0:T(8,128)(2,1)S(1)} collective-permute-done((bf16[160,1408]{1,0:T(8,128)(2,1)S(1)}, bf16[160,1408]{1,0:T(8,128)(2,1)S(1)}, u32[]{:S(2)}, u32[]{:S(2)}) %collective-permute-start) | collective-permute-done | bytes 450592 | tf_op jit(solution)/shard_map/ppermute | solution.py:184
  27.4 7.6 %collective-permute-done.12.refs_7_ = bf16[160,1408]{1,0:T(8,128)(2,1)S(1)} collective-permute-done((bf16[160,1408]{1,0:T(8,128)(2,1)S(1)}, bf16[160,1408]{1,0:T(8,128)(2,1)S(1)}, u32[]{:S(2)}, u32[]{:S(2)}) %collective-permute-start.12) | collective-permute-done | bytes 450592 | tf_op jit(solution)/shard_map/ppermute | solution.py:184
  35.0 2.0 collective-permute-done.13.refs_8_
  37.0 6.7 %shard_map.30.refs_9_ = f32[640,1408]{1,0:T(8,128)S(1)} custom-call(bf16[2,640,1408]{2,1,0:T(8,128)(2,1)} %get-tuple-element.34.refs_0_, bf16[160,1408]{1,0:T(8,128)(2,1)S(1)} %get-tuple-element.38.refs_1_, bf16[160,1408]{1,0:T(8,128)(2,1)S(1)} %get-tuple-element.47.refs_2_, bf16[160,1408]{1,0:T(8,128)(2,1)S(1)} %get-tuple-element.37.refs_3_, ...), custom_call_target="tpu_custom_call" | custom-call | flops 3460300800 | bytes 14417920 | tf_op jit(solution)/shard_map/pallas_call | solution.py:122
  46.5 6.7 %shard_map.31.refs_9_ = f32[640,1408]{1,0:T(8,128)S(1)} custom-call(bf16[2,640,1408]{2,1,0:T(8,128)(2,1)} %collective-permute-done.14.refs_0_, bf16[160,1408]{1,0:T(8,128)(2,1)S(1)} %get-tuple-element.38.refs_1_, bf16[160,1408]{1,0:T(8,128)(2,1)S(1)} %get-tuple-element.47.refs_2_, bf16[160,1408]{1,0:T(8,128)(2,1)S(1)} %get-tuple-element.37.refs_3_, ...), custom_call_target="tpu_custom_call" | custom-call | flops 3460300800 | bytes 14417920 | tf_op jit(solution)/shard_map/pallas_call | solution.py:122
  55.3 4.3 %collective-permute-done.8.refs_6_ = bf16[160,1408]{1,0:T(8,128)(2,1)S(1)} collective-permute-done((bf16[160,1408]{1,0:T(8,128)(2,1)S(1)}, bf16[160,1408]{1,0:T(8,128)(2,1)S(1)}, u32[]{:S(2)}, u32[]{:S(2)}) %collective-permute-start.8) | collective-permute-done | bytes 450592 | tf_op jit(solution)/shard_map/ppermute | solution.py:184
  61.6 7.6 %collective-permute-done.18.refs_4_ = bf16[160,1408]{1,0:T(8,128)(2,1)S(1)} collective-permute-done((bf16[160,1408]{1,0:T(8,128)(2,1)S(1)}, bf16[160,1408]{1,0:T(8,128)(2,1)S(1)}, u32[]{:S(2)}, u32[]{:S(2)}) %collective-permute-start.18) | collective-permute-done | bytes 450592 | tf_op jit(solution)/shard_map/ppermute | solution.py:184
  71.2 7.6 %collective-permute-done.9.refs_2_ = bf16[160,1408]{1,0:T(8,128)(2,1)S(1)} collective-permute-done((bf16[160,1408]{1,0:T(8,128)(2,1)S(1)}, bf16[160,1408]{1,0:T(8,128)(2,1)S(1)}, u32[]{:S(2)}, u32[]{:S(2)}) %collective-permute-start.9) | collective-permute-done | bytes 450592 | tf_op jit(solution)/shard_map/ppermute | solution.py:184
  80.9 7.6 %collective-permute-done.19.refs_8_ = bf16[160,1408]{1,0:T(8,128)(2,1)S(1)} collective-permute-done((bf16[160,1408]{1,0:T(8,128)(2,1)S(1)}, bf16[160,1408]{1,0:T(8,128)(2,1)S(1)}, u32[]{:S(2)}, u32[]{:S(2)}) %collective-permute-start.19) | collective-permute-done | bytes 450592 | tf_op jit(solution)/shard_map/ppermute | solution.py:184
  90.5 6.9 %shard_map.33.refs_9_ = f32[640,1408]{1,0:T(8,128)S(1)} custom-call(bf16[2,640,1408]{2,1,0:T(8,128)(2,1)} %collective-permute-done.14.refs_0_, bf16[160,1408]{1,0:T(8,128)(2,1)S(1)} %collective-permute-done.1.refs_1_, bf16[160,1408]{1,0:T(8,128)(2,1)S(1)} %collective-permute-done.7.refs_2_, ...), custom_call_target="tpu_custom_call", output_to_operand_aliasing={{}: (9, {})} | custom-call | flops 3460300800 | bytes 14417920 | tf_op jit(solution)/shard_map/pallas_call | solution.py:122
  97.4 6.9 %shard_map.32.refs_9_ = f32[640,1408]{1,0:T(8,128)S(1)} custom-call(bf16[2,640,1408]{2,1,0:T(8,128)(2,1)} %get-tuple-element.34.refs_0_, bf16[160,1408]{1,0:T(8,128)(2,1)S(1)} %collective-permute-done.1.refs_1_, bf16[160,1408]{1,0:T(8,128)(2,1)S(1)} %collective-permute-done.7.refs_2_, ...), custom_call_target="tpu_custom_call", output_to_operand_aliasing={{}: (9, {})} | custom-call | flops 3460300800 | bytes 14417920 | tf_op jit(solution)/shard_map/pallas_call | solution.py:122
  110.3 9.2 %collective-permute-done.23.refs_8_ = bf16[160,1408]{1,0:T(8,128)(2,1)S(1)} collective-permute-done((bf16[160,1408]{1,0:T(8,128)(2,1)S(1)}, bf16[160,1408]{1,0:T(8,128)(2,1)S(1)}, u32[]{:S(2)}, u32[]{:S(2)}) %collective-permute-start.23) | collective-permute-done | bytes 450592 | tf_op jit(solution)/shard_map/ppermute | solution.py:184
  121.5 6.9 %shard_map.35.refs_5_ = f32[640,1408]{1,0:T(8,128)S(1)} custom-call(bf16[2,640,1408]{2,1,0:T(8,128)(2,1)} %collective-permute-done.14.refs_0_, bf16[160,1408]{1,0:T(8,128)(2,1)S(1)} %collective-permute-done.3.refs_1_, bf16[160,1408]{1,0:T(8,128)(2,1)S(1)} %collective-permute-done.9.refs_2_, ...), custom_call_target="tpu_custom_call", output_to_operand_aliasing={{}: (9, {})} | custom-call | flops 3460300800 | bytes 14417920 | tf_op jit(solution)/shard_map/pallas_call | solution.py:122
  128.5 6.9 %shard_map.34.refs_5_ = f32[640,1408]{1,0:T(8,128)S(1)} custom-call(bf16[2,640,1408]{2,1,0:T(8,128)(2,1)} %get-tuple-element.34.refs_0_, bf16[160,1408]{1,0:T(8,128)(2,1)S(1)} %collective-permute-done.3.refs_1_, bf16[160,1408]{1,0:T(8,128)(2,1)S(1)} %collective-permute-done.9.refs_2_, ...), custom_call_target="tpu_custom_call", output_to_operand_aliasing={{}: (9, {})} | custom-call | flops 3460300800 | bytes 14417920 | tf_op jit(solution)/shard_map/pallas_call | solution.py:122
  136.7 5.2 %shard_map.36 = f32[640,1408]{1,0:T(8,128)S(1)} custom-call(bf16[2,640,1408]{2,1,0:T(8,128)(2,1)} %collective-permute-done.14.refs_0_, bf16[160,1408]{1,0:T(8,128)(2,1)S(1)} %collective-permute-done.5.refs_1_, bf16[160,1408]{1,0:T(8,128)(2,1)S(1)} %collective-permute-done.11.refs_2_, ...), custom_call_target="tpu_custom_call", output_to_operand_aliasing={{}: (5, {})} | custom-call | flops 1730150400 | bytes 12615680 | tf_op jit(solution)/shard_map/pallas_call | solution.py:122
  146.1 9.1 %collective-permute-done.30 = bf16[160,1408]{1,0:T(8,128)(2,1)S(1)} collective-permute-done((bf16[160,1408]{1,0:T(8,128)(2,1)S(1)}, bf16[160,1408]{1,0:T(8,128)(2,1)S(1)}, u32[]{:S(2)}, u32[]{:S(2)}) %collective-permute-start.30) | collective-permute-done | bytes 450592 | tf_op jit(solution)/shard_map/ppermute | solution.py:211
  156.5 8.4 %collective-permute-done.27 = bf16[160,1408]{1,0:T(8,128)(2,1)S(1)} collective-permute-done((bf16[160,1408]{1,0:T(8,128)(2,1)S(1)}, bf16[160,1408]{1,0:T(8,128)(2,1)S(1)}, u32[]{:S(2)}, u32[]{:S(2)}) %collective-permute-start.27) | collective-permute-done | bytes 450592 | tf_op jit(solution)/shard_map/ppermute | solution.py:211
  168.2 6.3 %collective-permute-done.36 = bf16[160,1408]{1,0:T(8,128)(2,1)S(1)} collective-permute-done((bf16[160,1408]{1,0:T(8,128)(2,1)S(1)}, bf16[160,1408]{1,0:T(8,128)(2,1)S(1)}, u32[]{:S(2)}, u32[]{:S(2)}) %collective-permute-start.36) | collective-permute-done | bytes 450592 | tf_op jit(solution)/shard_map/ppermute | solution.py:211
  177.7 6.0 %collective-permute-done.33 = bf16[160,1408]{1,0:T(8,128)(2,1)S(1)} collective-permute-done((bf16[160,1408]{1,0:T(8,128)(2,1)S(1)}, bf16[160,1408]{1,0:T(8,128)(2,1)S(1)}, u32[]{:S(2)}, u32[]{:S(2)}) %collective-permute-start.33) | collective-permute-done | bytes 450592 | tf_op jit(solution)/shard_map/ppermute | solution.py:211
  183.8 5.9 %shard_map.37 = bf16[640,1408]{1,0:T(8,128)(2,1)S(1)} custom-call(bf16[2,640,1408]{2,1,0:T(8,128)(2,1)} %get-tuple-element.34.refs_0_, bf16[160,1408]{1,0:T(8,128)(2,1)S(1)} %collective-permute-done.5.refs_1_, bf16[160,1408]{1,0:T(8,128)(2,1)S(1)} %collective-permute-done.11.refs_2_, bf16[160,1408]{1,0:T(8,128)(2,1)S(1)} %collective-permute-done.21.refs_3_, ...), custom_call_target="tpu_custom_call" | custom-call | flops 1730150400 | bytes 12615680 | tf_op jit(solution)/shard_map/pallas_call | solution.py:122
  191.8 6.3 %shard_map.39.refs_5_ = f32[640,1408]{1,0:T(8,128)} custom-call(bf16[2,640,1408]{2,1,0:T(8,128)(2,1)} %collective-permute-done.14.refs_0_, bf16[160,1408]{1,0:T(8,128)(2,1)S(1)} %collective-permute-done.28.refs_1_, bf16[160,1408]{1,0:T(8,128)(2,1)S(1)} %collective-permute-done.31.refs_2_, bf16[160,1408]{1,0:T(8,128)(2,1)S(1)} %collective-permute-done.34.refs_3_, ...), custom_call_target="tpu_custom_call" | custom-call | flops 1730150400 | bytes 12615680 | tf_op jit(solution)/shard_map/pallas_call | solution.py:122
  198.1 3.5 %collective-permute-done.38.refs_4_ = bf16[160,1408]{1,0:T(8,128)(2,1)S(1)} collective-permute-done((bf16[160,1408]{1,0:T(8,128)(2,1)S(1)}, bf16[160,1408]{1,0:T(8,128)(2,1)S(1)}, u32[]{:S(2)}, u32[]{:S(2)}) %collective-permute-start.38) | collective-permute-done | bytes 450592 | tf_op jit(solution)/shard_map/ppermute | solution.py:184
  202.7 7.0 %shard_map.40 = f32[640,1408]{1,0:T(8,128)} custom-call(bf16[2,640,1408]{2,1,0:T(8,128)(2,1)} %collective-permute-done.14.refs_0_, bf16[160,1408]{1,0:T(8,128)(2,1)S(1)} %collective-permute-done.29.refs_1_, bf16[160,1408]{1,0:T(8,128)(2,1)S(1)} %collective-permute-done.32.refs_2_, ...), custom_call_target="tpu_custom_call", output_to_operand_aliasing={{}: (5, {})} | custom-call | flops 1730150400 | bytes 12615680 | tf_op jit(solution)/shard_map/pallas_call | solution.py:122
  215.5 5.3 %shard_map.38.refs_5_ = f32[640,1408]{1,0:T(8,128)S(1)} custom-call(bf16[2,640,1408]{2,1,0:T(8,128)(2,1)} %get-tuple-element.34.refs_0_, bf16[160,1408]{1,0:T(8,128)(2,1)S(1)} %copy-done.11, bf16[160,1408]{1,0:T(8,128)(2,1)S(1)} %copy-done.9, bf16[160,1408]{1,0:T(8,128)(2,1)S(1)} %copy-done.15, bf16[160,1408]{1,0:T(8,128)(2,1)S(1)} %copy-done.13), custom_call_target="tpu_custom_call" | custom-call | flops 1730150400 | bytes 12615680 | tf_op jit(solution)/shard_map/pallas_call | solution.py:122
  220.8 6.4 %shard_map.41 = f32[640,1408]{1,0:T(8,128)S(1)} custom-call(bf16[2,640,1408]{2,1,0:T(8,128)(2,1)} %get-tuple-element.34.refs_0_, bf16[160,1408]{1,0:T(8,128)(2,1)S(1)} %collective-permute-done.29.refs_1_, bf16[160,1408]{1,0:T(8,128)(2,1)S(1)} %collective-permute-done.32.refs_2_, bf16[160,1408]{1,0:T(8,128)(2,1)S(1)} %copy-done.7, ...), custom_call_target="tpu_custom_call", output_to_operand_aliasing={{}: (5, {})} | custom-call | flops 1730150400 | bytes 12615680 | tf_op jit(solution)/shard_map/pallas_call | solution.py:122
  227.2 24.3 %collective-permute-done.26 = bf16[640,1408]{1,0:T(8,128)(2,1)} collective-permute-done((bf16[640,1408]{1,0:T(8,128)(2,1)S(1)}, bf16[640,1408]{1,0:T(8,128)(2,1)}, u32[]{:S(2)}, u32[]{:S(2)}) %collective-permute-start.26) | collective-permute-done | bytes 1802272 | tf_op jit(solution)/shard_map/ppermute | solution.py:227
  251.6 3.9 %add_multiply_fusion = f32[640,1408]{1,0:T(8,128)} fusion(f32[640,1408]{1,0:T(8,128)S(1)} %shard_map.41, bf16[640,1408]{1,0:T(8,128)(2,1)} %collective-permute-done.26, bf16[640,1408]{1,0:T(8,128)(2,1)S(1)} %shard_map.37, f32[640]{0:T(1024)S(1)} %reduce), kind=kLoop, calls=%fused_computation | loop fusion | flops 4505600 | bytes 10816000 | tf_op jit(solution)/shard_map/mul | solution.py:240
  (96 shorter events, 50.1 us)
Async XLA Ops:
  6.6 39.9 %collective-permute-start.14 = (bf16[2,640,1408]{2,1,0:T(8,128)(2,1)}, bf16[2,640,1408]{2,1,0:T(8,128)(2,1)}, u32[]{:S(2)}, u32[]{:S(2)}) collective-permute-start(bf16[2,640,1408]{2,1,0:T(8,128)(2,1)} %get-tuple-element.34.refs_0_), channel_id=1, source_target_pairs={{0,2},{2,0},{4,6},{6,4},{8,10},{10,8},{12,14},{14,12},{16,18},{18,... | collective-permute-start | bytes 10813448 | tf_op jit(solution)/shard_map/ppermute | solution.py:173
  11.6 13.8 %collective-permute-start = (bf16[160,1408]{1,0:T(8,128)(2,1)S(1)}, bf16[160,1408]{1,0:T(8,128)(2,1)S(1)}, u32[]{:S(2)}, u32[]{:S(2)}) collective-permute-start(bf16[160,1408]{1,0:T(8,128)(2,1)S(1)} %get-tuple-element.38.refs_1_), channel_id=1, source_target_pairs={{0,8},{2,10},{8,16},{10,18},{16,24},{18,26},{24,28},{26,30},{28,20... | collective-permute-start | bytes 1351688 | tf_op jit(solution)/shard_map/ppermute | solution.py:184
  14.2 20.8 %collective-permute-start.12 = (bf16[160,1408]{1,0:T(8,128)(2,1)S(1)}, bf16[160,1408]{1,0:T(8,128)(2,1)S(1)}, u32[]{:S(2)}, u32[]{:S(2)}) collective-permute-start(bf16[160,1408]{1,0:T(8,128)(2,1)S(1)} %get-tuple-element.47.refs_2_), channel_id=1, source_target_pairs={{0,8},{2,10},{8,16},{10,18},{16,24},{18,26},{24,28},{26,30},{28,20... | collective-permute-start | bytes 1351688 | tf_op jit(solution)/shard_map/ppermute | solution.py:184
  16.2 20.8 %collective-permute-start.13 = (bf16[160,1408]{1,0:T(8,128)(2,1)S(1)}, bf16[160,1408]{1,0:T(8,128)(2,1)S(1)}, u32[]{:S(2)}, u32[]{:S(2)}) collective-permute-start(bf16[160,1408]{1,0:T(8,128)(2,1)S(1)} %get-tuple-element.43.refs_4_), channel_id=1, source_target_pairs={{8,0},{10,2},{16,8},{18,10},{24,16},{26,18},{28,24},{30,26},{20,28... | collective-permute-start | bytes 1351688 | tf_op jit(solution)/shard_map/ppermute | solution.py:184
  25.3 19.1 %collective-permute-start.1 = (bf16[160,1408]{1,0:T(8,128)(2,1)S(1)}, bf16[160,1408]{1,0:T(8,128)(2,1)S(1)}, u32[]{:S(2)}, u32[]{:S(2)}) collective-permute-start(bf16[160,1408]{1,0:T(8,128)(2,1)S(1)} %collective-permute-done.refs_5_), channel_id=1, source_target_pairs={{0,8},{2,10},{8,16},{10,18},{16,24},{18,26},{24,28},{26,30},{28,20... | collective-permute-start | bytes 1351688 | tf_op jit(solution)/shard_map/ppermute | solution.py:184
  27.4 18.9 %collective-permute-start.7 = (bf16[160,1408]{1,0:T(8,128)(2,1)S(1)}, bf16[160,1408]{1,0:T(8,128)(2,1)S(1)}, u32[]{:S(2)}, u32[]{:S(2)}) collective-permute-start(bf16[160,1408]{1,0:T(8,128)(2,1)S(1)} %collective-permute-done.6.refs_6_), channel_id=1, source_target_pairs={{8,0},{10,2},{16,8},{18,10},{24,16},{26,18},{28,24},{30,26},{20,28... | collective-permute-start | bytes 1351688 | tf_op jit(solution)/shard_map/ppermute | solution.py:184
  44.5 15.3 %collective-permute-start.2 = (bf16[160,1408]{1,0:T(8,128)(2,1)S(1)}, bf16[160,1408]{1,0:T(8,128)(2,1)S(1)}, u32[]{:S(2)}, u32[]{:S(2)}) collective-permute-start(bf16[160,1408]{1,0:T(8,128)(2,1)S(1)} %collective-permute-done.1.refs_1_), channel_id=1, source_target_pairs={{0,8},{2,10},{8,16},{10,18},{16,24},{18,26},{24,28},{26,30},{28,20... | collective-permute-start | bytes 1351688 | tf_op jit(solution)/shard_map/ppermute | solution.py:184
  53.2 16.0 %collective-permute-start.18 = (bf16[160,1408]{1,0:T(8,128)(2,1)S(1)}, bf16[160,1408]{1,0:T(8,128)(2,1)S(1)}, u32[]{:S(2)}, u32[]{:S(2)}) collective-permute-start(bf16[160,1408]{1,0:T(8,128)(2,1)S(1)} %collective-permute-done.13.refs_8_), channel_id=1, source_target_pairs={{8,0},{10,2},{16,8},{18,10},{24,16},{26,18},{28,24},{30,26},{20,28... | collective-permute-start | bytes 1351688 | tf_op jit(solution)/shard_map/ppermute | solution.py:184
  55.0 14.4 %collective-permute-start.15 = (bf16[160,1408]{1,0:T(8,128)(2,1)S(1)}, bf16[160,1408]{1,0:T(8,128)(2,1)S(1)}, u32[]{:S(2)}, u32[]{:S(2)}) collective-permute-start(bf16[160,1408]{1,0:T(8,128)(2,1)S(1)} %collective-permute-done.12.refs_7_), channel_id=1, source_target_pairs={{0,8},{2,10},{8,16},{10,18},{16,24},{18,26},{24,28},{26,30},{28,20... | collective-permute-start | bytes 1351688 | tf_op jit(solution)/shard_map/ppermute | solution.py:184
  59.5 19.3 %collective-permute-start.9 = (bf16[160,1408]{1,0:T(8,128)(2,1)S(1)}, bf16[160,1408]{1,0:T(8,128)(2,1)S(1)}, u32[]{:S(2)}, u32[]{:S(2)}) collective-permute-start(bf16[160,1408]{1,0:T(8,128)(2,1)S(1)} %get-tuple-element.38.refs_1_), channel_id=1, source_target_pairs={{8,0},{10,2},{16,8},{18,10},{24,16},{26,18},{28,24},{30,26},{20,28... | collective-permute-start | bytes 1351688 | tf_op jit(solution)/shard_map/ppermute | solution.py:184
  59.8 19.3 %collective-permute-start.3 = (bf16[160,1408]{1,0:T(8,128)(2,1)S(1)}, bf16[160,1408]{1,0:T(8,128)(2,1)S(1)}, u32[]{:S(2)}, u32[]{:S(2)}) collective-permute-start(bf16[160,1408]{1,0:T(8,128)(2,1)S(1)} %get-tuple-element.37.refs_3_), channel_id=1, source_target_pairs={{0,8},{2,10},{8,16},{10,18},{16,24},{18,26},{24,28},{26,30},{28,20... | collective-permute-start | bytes 1351688 | tf_op jit(solution)/shard_map/ppermute | solution.py:184
  69.2 19.3 %collective-permute-start.19 = (bf16[160,1408]{1,0:T(8,128)(2,1)S(1)}, bf16[160,1408]{1,0:T(8,128)(2,1)S(1)}, u32[]{:S(2)}, u32[]{:S(2)}) collective-permute-start(bf16[160,1408]{1,0:T(8,128)(2,1)S(1)} %collective-permute-done.18.refs_4_), channel_id=1, source_target_pairs={{8,0},{10,2},{16,8},{18,10},{24,16},{26,18},{28,24},{30,26},{20,28... | collective-permute-start | bytes 1351688 | tf_op jit(solution)/shard_map/ppermute | solution.py:184
  69.4 19.3 %collective-permute-start.16 = (bf16[160,1408]{1,0:T(8,128)(2,1)S(1)}, bf16[160,1408]{1,0:T(8,128)(2,1)S(1)}, u32[]{:S(2)}, u32[]{:S(2)}) collective-permute-start(bf16[160,1408]{1,0:T(8,128)(2,1)S(1)} %collective-permute-done.15.refs_3_), channel_id=1, source_target_pairs={{0,8},{2,10},{8,16},{10,18},{16,24},{18,26},{24,28},{26,30},{28,20... | collective-permute-start | bytes 1351688 | tf_op jit(solution)/shard_map/ppermute | solution.py:184
  78.9 29.4 %collective-permute-start.10 = (bf16[160,1408]{1,0:T(8,128)(2,1)S(1)}, bf16[160,1408]{1,0:T(8,128)(2,1)S(1)}, u32[]{:S(2)}, u32[]{:S(2)}) collective-permute-start(bf16[160,1408]{1,0:T(8,128)(2,1)S(1)} %collective-permute-done.9.refs_2_), channel_id=1, source_target_pairs={{8,0},{10,2},{16,8},{18,10},{24,16},{26,18},{28,24},{30,26},{20,28... | collective-permute-start | bytes 1351688 | tf_op jit(solution)/shard_map/ppermute | solution.py:184
  79.1 29.6 %collective-permute-start.4 = (bf16[160,1408]{1,0:T(8,128)(2,1)S(1)}, bf16[160,1408]{1,0:T(8,128)(2,1)S(1)}, u32[]{:S(2)}, u32[]{:S(2)}) collective-permute-start(bf16[160,1408]{1,0:T(8,128)(2,1)S(1)} %collective-permute-done.3.refs_1_), channel_id=1, source_target_pairs={{0,8},{2,10},{8,16},{10,18},{16,24},{18,26},{24,28},{26,30},{28,20... | collective-permute-start | bytes 1351688 | tf_op jit(solution)/shard_map/ppermute | solution.py:184
  88.5 17.7 %collective-permute-start.22 = (bf16[160,1408]{1,0:T(8,128)(2,1)S(1)}, bf16[160,1408]{1,0:T(8,128)(2,1)S(1)}, u32[]{:S(2)}, u32[]{:S(2)}) collective-permute-start(bf16[160,1408]{1,0:T(8,128)(2,1)S(1)} %get-tuple-element.47.refs_2_), channel_id=1, source_target_pairs={{8,0},{10,2},{16,8},{18,10},{24,16},{26,18},{28,24},{30,26},{20,28... | collective-permute-start | bytes 1351688 | tf_op jit(solution)/shard_map/ppermute | solution.py:184
  88.7 17.9 %collective-permute-start.17 = (bf16[160,1408]{1,0:T(8,128)(2,1)S(1)}, bf16[160,1408]{1,0:T(8,128)(2,1)S(1)}, u32[]{:S(2)}, u32[]{:S(2)}) collective-permute-start(bf16[160,1408]{1,0:T(8,128)(2,1)S(1)} %get-tuple-element.43.refs_4_), channel_id=1, source_target_pairs={{0,8},{2,10},{8,16},{10,18},{16,24},{18,26},{24,28},{26,30},{28,20... | collective-permute-start | bytes 1351688 | tf_op jit(solution)/shard_map/ppermute | solution.py:184
  106.7 13.3 %collective-permute-start.20 = (bf16[160,1408]{1,0:T(8,128)(2,1)S(1)}, bf16[160,1408]{1,0:T(8,128)(2,1)S(1)}, u32[]{:S(2)}, u32[]{:S(2)}) collective-permute-start(bf16[160,1408]{1,0:T(8,128)(2,1)S(1)} %collective-permute-done.17.refs_3_), channel_id=1, source_target_pairs={{0,8},{2,10},{8,16},{10,18},{16,24},{18,26},{24,28},{26,30},{28,20... | collective-permute-start | bytes 1351688 | tf_op jit(solution)/shard_map/ppermute | solution.py:184
  108.3 28.4 %collective-permute-start.11 = (bf16[160,1408]{1,0:T(8,128)(2,1)S(1)}, bf16[160,1408]{1,0:T(8,128)(2,1)S(1)}, u32[]{:S(2)}, u32[]{:S(2)}) collective-permute-start(bf16[160,1408]{1,0:T(8,128)(2,1)S(1)} %collective-permute-done.10.refs_6_), channel_id=1, source_target_pairs={{8,0},{10,2},{16,8},{18,10},{24,16},{26,18},{28,24},{30,26},{20,28... | collective-permute-start | bytes 1351688 | tf_op jit(solution)/shard_map/ppermute | solution.py:184
  108.7 28.0 %collective-permute-start.5 = (bf16[160,1408]{1,0:T(8,128)(2,1)S(1)}, bf16[160,1408]{1,0:T(8,128)(2,1)S(1)}, u32[]{:S(2)}, u32[]{:S(2)}) collective-permute-start(bf16[160,1408]{1,0:T(8,128)(2,1)S(1)} %collective-permute-done.4.refs_5_), channel_id=1, source_target_pairs={{0,8},{2,10},{8,16},{10,18},{16,24},{18,26},{24,28},{26,30},{28,20... | collective-permute-start | bytes 1351688 | tf_op jit(solution)/shard_map/ppermute | solution.py:184
  119.5 16.8 %collective-permute-start.24 = (bf16[160,1408]{1,0:T(8,128)(2,1)S(1)}, bf16[160,1408]{1,0:T(8,128)(2,1)S(1)}, u32[]{:S(2)}, u32[]{:S(2)}) collective-permute-start(bf16[160,1408]{1,0:T(8,128)(2,1)S(1)} %collective-permute-done.23.refs_8_), channel_id=1, source_target_pairs={{8,0},{10,2},{16,8},{18,10},{24,16},{26,18},{28,24},{30,26},{20,28... | collective-permute-start | bytes 1351688 | tf_op jit(solution)/shard_map/ppermute | solution.py:184
  120.0 16.7 %collective-permute-start.21 = (bf16[160,1408]{1,0:T(8,128)(2,1)S(1)}, bf16[160,1408]{1,0:T(8,128)(2,1)S(1)}, u32[]{:S(2)}, u32[]{:S(2)}) collective-permute-start(bf16[160,1408]{1,0:T(8,128)(2,1)S(1)} %collective-permute-done.20.refs_7_), channel_id=1, source_target_pairs={{0,8},{2,10},{8,16},{10,18},{16,24},{18,26},{24,28},{26,30},{28,20... | collective-permute-start | bytes 1351688 | tf_op jit(solution)/shard_map/ppermute | solution.py:184
  141.9 41.8 %collective-permute-start.25 = (f32[640,1408]{1,0:T(8,128)S(1)}, f32[640,1408]{1,0:T(8,128)S(1)}, u32[]{:S(2)}, u32[]{:S(2)}) collective-permute-start(f32[640,1408]{1,0:T(8,128)S(1)} %shard_map.36), channel_id=1, source_target_pairs={{0,2},{2,0},{4,6},{6,4},{8,10},{10,8},{12,14},{14,12},{16,18},{18,... | collective-permute-start | bytes 10813448 | tf_op jit(solution)/shard_map/ppermute | solution.py:221
  143.4 21.5 %collective-permute-start.27 = (bf16[160,1408]{1,0:T(8,128)(2,1)S(1)}, bf16[160,1408]{1,0:T(8,128)(2,1)S(1)}, u32[]{:S(2)}, u32[]{:S(2)}) collective-permute-start(bf16[160,1408]{1,0:T(8,128)(2,1)S(1)} %collective-permute-done.2.refs_5_), channel_id=1, source_target_pairs={{0,1},{1,0},{2,3},{3,2},{4,5},{5,4},{6,7},{7,6},{8,9},{9,8},{10,11... | collective-permute-start | bytes 1351688 | tf_op jit(solution)/shard_map/ppermute | solution.py:211
  144.1 22.1 %collective-permute-start.31 = (bf16[160,1408]{1,0:T(8,128)(2,1)S(1)}, bf16[160,1408]{1,0:T(8,128)(2,1)S(1)}, u32[]{:S(2)}, u32[]{:S(2)}) collective-permute-start(bf16[160,1408]{1,0:T(8,128)(2,1)S(1)} %collective-permute-done.8.refs_6_), channel_id=1, source_target_pairs={{8,0},{10,2},{16,8},{18,10},{24,16},{26,18},{28,24},{30,26},{20,28... | collective-permute-start | bytes 1351688 | tf_op jit(solution)/shard_map/ppermute | solution.py:184
  145.4 22.3 %collective-permute-start.28 = (bf16[160,1408]{1,0:T(8,128)(2,1)S(1)}, bf16[160,1408]{1,0:T(8,128)(2,1)S(1)}, u32[]{:S(2)}, u32[]{:S(2)}) collective-permute-start(bf16[160,1408]{1,0:T(8,128)(2,1)S(1)} %collective-permute-done.2.refs_5_), channel_id=1, source_target_pairs={{0,8},{2,10},{8,16},{10,18},{16,24},{18,26},{24,28},{26,30},{28,20... | collective-permute-start | bytes 1351688 | tf_op jit(solution)/shard_map/ppermute | solution.py:184
  155.2 19.3 %collective-permute-start.36 = (bf16[160,1408]{1,0:T(8,128)(2,1)S(1)}, bf16[160,1408]{1,0:T(8,128)(2,1)S(1)}, u32[]{:S(2)}, u32[]{:S(2)}) collective-permute-start(bf16[160,1408]{1,0:T(8,128)(2,1)S(1)} %collective-permute-done.19.refs_8_), channel_id=1, source_target_pairs={{0,1},{1,0},{2,3},{3,2},{4,5},{5,4},{6,7},{7,6},{8,9},{9,8},{10,11... | collective-permute-start | bytes 1351688 | tf_op jit(solution)/shard_map/ppermute | solution.py:211
  166.2 17.5 %collective-permute-start.33 = (bf16[160,1408]{1,0:T(8,128)(2,1)S(1)}, bf16[160,1408]{1,0:T(8,128)(2,1)S(1)}, u32[]{:S(2)}, u32[]{:S(2)}) collective-permute-start(bf16[160,1408]{1,0:T(8,128)(2,1)S(1)} %collective-permute-done.16.refs_7_), channel_id=1, source_target_pairs={{0,1},{1,0},{2,3},{3,2},{4,5},{5,4},{6,7},{7,6},{8,9},{9,8},{10,11... | collective-permute-start | bytes 1351688 | tf_op jit(solution)/shard_map/ppermute | solution.py:211
  167.7 16.0 %collective-permute-start.34 = (bf16[160,1408]{1,0:T(8,128)(2,1)S(1)}, bf16[160,1408]{1,0:T(8,128)(2,1)S(1)}, u32[]{:S(2)}, u32[]{:S(2)}) collective-permute-start(bf16[160,1408]{1,0:T(8,128)(2,1)S(1)} %collective-permute-done.16.refs_7_), channel_id=1, source_target_pairs={{0,8},{2,10},{8,16},{10,18},{16,24},{18,26},{24,28},{26,30},{28,20... | collective-permute-start | bytes 1351688 | tf_op jit(solution)/shard_map/ppermute | solution.py:184
  174.5 23.6 %collective-permute-start.32 = (bf16[160,1408]{1,0:T(8,128)(2,1)S(1)}, bf16[160,1408]{1,0:T(8,128)(2,1)S(1)}, u32[]{:S(2)}, u32[]{:S(2)}) collective-permute-start(bf16[160,1408]{1,0:T(8,128)(2,1)S(1)} %collective-permute-done.30), channel_id=1, source_target_pairs={{8,0},{10,2},{16,8},{18,10},{24,16},{26,18},{28,24},{30,26},{20,28... | collective-permute-start | bytes 1351688 | tf_op jit(solution)/shard_map/ppermute | solution.py:184
  176.3 21.8 %collective-permute-start.29 = (bf16[160,1408]{1,0:T(8,128)(2,1)S(1)}, bf16[160,1408]{1,0:T(8,128)(2,1)S(1)}, u32[]{:S(2)}, u32[]{:S(2)}) collective-permute-start(bf16[160,1408]{1,0:T(8,128)(2,1)S(1)} %collective-permute-done.27), channel_id=1, source_target_pairs={{0,8},{2,10},{8,16},{10,18},{16,24},{18,26},{24,28},{26,30},{28,20... | collective-permute-start | bytes 1351688 | tf_op jit(solution)/shard_map/ppermute | solution.py:184
  209.7 41.8 %collective-permute-start.26 = (bf16[640,1408]{1,0:T(8,128)(2,1)S(1)}, bf16[640,1408]{1,0:T(8,128)(2,1)}, u32[]{:S(2)}, u32[]{:S(2)}) collective-permute-start(bf16[640,1408]{1,0:T(8,128)(2,1)S(1)} %shard_map.37), channel_id=1, source_target_pairs={{0,1},{1,0},{2,3},{3,2},{4,5},{5,4},{6,7},{7,6},{8,9},{9,8},{10,11... | collective-permute-start | bytes 5406728 | tf_op jit(solution)/shard_map/ppermute | solution.py:227
  (24 other events, 250.4 us)
where the time goes:
time: 256 us; the launch traced here: 255 us
  waiting for transfers between devices  118 us (46%)
  Pallas kernels  80.2 us (31%)
  starting transfers between devices  40.5 us (16%)
  local copies, waits for them, and re-layouts  12.2 us (5%)
  other arithmetic  4.08 us (2%)
    pallas_call x12, Pallas kernels, add_relation(): pl.pallas_call(functools.partial(relation_kernel, margin, weight, counts,...  77.2 us
    ppermute x16, waiting for transfers between devices, hop(): lax.ppermute(chain[1], 'seq', back)  45.3 us
    ppermute x4, waiting for transfers between devices, local(): lax.ppermute(x, 'pair', route)  29.8 us
    ppermute x1, waiting for transfers between devices, local(): lax.ppermute(half, 'pair', [(i, i ^ distance) for i in range(pair_count)])  24.3 us
    ppermute x16, starting transfers between devices, hop(): lax.ppermute(chain[0], 'seq', onward)  24.1 us
    ppermute x16, waiting for transfers between devices, hop(): lax.ppermute(chain[0], 'seq', onward)  18.9 us
    unnamed x32, local copies, waits for them, and re-layouts  12.2 us
    ppermute x16, starting transfers between devices, hop(): lax.ppermute(chain[1], 'seq', back)  9.45 us
  transfers between devices with their start and end apart: 40, of which 20 were waited for; matrix products, arithmetic and copies ran while one was open for 0% of the time, Pallas kernels for 26%

commit v1 on v0

--- a/solution.py
+++ b/solution.py
@@ -9,8 +9,13 @@
 from jax.sharding import PartitionSpec as P
 
 CORES = 2
+DOUBLED = 0
+TIE_RELAY = (1,)
+TIE_SWAP = (0, 1)
+MERGE_FIRST = True
 ROW_TILE = 16
 VMEM_LIMIT = 32 * 1024 * 1024
+FIRST_VMEM_LIMIT = 58 * 1024 * 1024
 
 
 def normalized(values):
@@ -55,8 +60,8 @@
         at += count
 
 
-def pack_share(student, teacher, pair_index, counts):
-    share, width = sum(counts), student.shape[1]
+def pack_share(student, teacher, pair_index, share, counts):
+    width = student.shape[1]
     mine = pl.BlockSpec((share, width), lambda i, which: (which[0], 0))
     return pl.pallas_call(
         functools.partial(pack_kernel, counts),
@@ -67,19 +72,20 @@
             out_specs=[pl.BlockSpec((2 * n, width), lambda i, which: (0, 0)) for n in counts],
         ),
         out_shape=[jax.ShapeDtypeStruct((2 * n, width), jnp.bfloat16) for n in counts],
-        compiler_params=pltpu.CompilerParams(vmem_limit_bytes=VMEM_LIMIT),
+        compiler_params=pltpu.CompilerParams(vmem_limit_bytes=FIRST_VMEM_LIMIT),
         cost_estimate=pl.CostEstimate(
             flops=6 * share * width, bytes_accessed=12 * share * width, transcendentals=2 * share
         ),
     )(jnp.reshape(pair_index, (1,)).astype(jnp.int32), student, teacher)
 
 
-def relation_kernel(margin, weight, counts, terms, project, *refs):
+def relation_kernel(margin, weight, counts, terms, project, halves, *refs):
     refs = list(refs)
     rows = refs.pop(0)
     partners = [refs.pop(0) for _ in counts]
     added = [refs.pop(0) for _ in range(terms)]
     student, scale = (refs.pop(0), refs.pop(0)) if project else (None, None)
+    summands = [refs.pop(0) for _ in range(halves)]
     out, all_s, all_t = refs
 
     @pl.when(pl.program_id(0) == 0)
@@ -98,14 +104,17 @@
     relation = (weight * shrink).astype(jnp.bfloat16)
     grad = jnp.dot(relation, all_s[...], preferred_element_type=jnp.float32)
     for term in added:
-        grad = term[...] + grad
+        grad = grad + term[...].astype(jnp.float32)
     if project:
         unit = student[...] * scale[...]
         grad = grad - unit * jnp.sum(unit * grad, axis=1, keepdims=True)
+    if summands:
+        others = [x[...].astype(jnp.float32) for x in summands]
+        grad = scale[...] * (sum(others[1:], others[0]) + grad)
     out[...] = grad.astype(out.dtype)
 
 
-def add_relation(half, partners, terms, margin, weight, project=None, dtype=jnp.float32):
+def add_relation(half, partners, terms, margin, weight, project=None, summands=(), dtype=jnp.float32):
     _, rows, width = half.shape
     block = rows // 2
     counts = tuple(x.shape[0] // 2 for x in partners)
@@ -119,8 +128,12 @@
     if project is not None:
         operands += list(project)
         specs += [by_row, pl.BlockSpec((block, 1), lambda i: (i, 0))]
+    operands += list(summands)
+    specs += [by_row] * len(summands)
     return pl.pallas_call(
-        functools.partial(relation_kernel, margin, weight, counts, len(terms), project is not None),
+        functools.partial(
+            relation_kernel, margin, weight, counts, len(terms), project is not None, len(summands)
+        ),
         grid=(rows // block,),
         in_specs=specs,
         out_specs=by_row,
@@ -149,13 +162,18 @@
     return onward, back, swap
 
 
-def halves(tokens):
-    first = -(-tokens // (2 * ROW_TILE)) * ROW_TILE
-    return first, tokens - first
+def split(tokens, parts):
+    tiles = tokens // ROW_TILE
+    return [ROW_TILE * (tiles // parts + (k < tiles % parts)) for k in range(parts)]
 
 
 def after(x, *values):
-    return lax.optimization_barrier((x, *values))[0]
+    return lax.optimization_barrier((x, *values))[0] if values else x
+
+
+def cut(piece, start, count):
+    tokens = piece.shape[0] // 2
+    return jnp.concatenate([piece[start : start + count], piece[tokens + start : tokens + start + count]])
 
 
 def local(student, teacher):
@@ -167,77 +185,78 @@
     weight = 64.0 * width / math.sqrt(rows * seq_count)
     onward, back, swap = ring_routes(seq_count)
     hops = seq_count // CORES // 2
-    counts = [n for part in halves(rows // pair_count) for n in halves(part)]
-    pieces = pack_share(student, teacher, pair_index, counts)
-    own_half, s_scale = normalize_own(student, teacher)
-    other_half = lax.ppermute(own_half, "seq", swap)
-    own, other = None, None
-
-    def add(half, partners, terms, project=None, dtype=jnp.float32):
-        return add_relation(half, partners, terms, margin, weight, project, dtype)
+    share = rows // pair_count
+    doubled = max(1, round(DOUBLED * share / ROW_TILE)) * ROW_TILE if pair_count == 2 and DOUBLED else 0
+    pieces = pack_share(student, teacher, pair_index, share, split(share - doubled, 2))
+    own_half, s_scale = normalize_own(after(student, *pieces), teacher)
+
+    def add(batch, total, **options):
+        return add_relation(own_half, batch, [] if total is None else [total], margin, weight, **options)
 
     def hop(chains, wait_for=()):
         sent = []
-        for k, chain in enumerate(chains):
-            if wait_for and k:
-                chain = [after(x, *wait_for) for x in chain]
-            sent.append([lax.ppermute(chain[0], "seq", onward), lax.ppermute(chain[1], "seq", back)])
+        for k, (onto, off) in enumerate(chains):
+            if k in TIE_RELAY:
+                onto, off = after(onto, *wait_for), after(off, *wait_for)
+            sent.append((lax.ppermute(onto, "seq", onward), lax.ppermute(off, "seq", back)))
         return sent
 
-    def once(chains, arrived):
-        return [[after(x, y) for x, y in zip(*both)] for both in zip(chains, arrived)]
+    def swapped(chains, wait_for=()):
+        return [
+            lax.ppermute(after(x, *wait_for) if k in TIE_SWAP else x, "seq", swap)
+            for k, chain in enumerate(chains)
+            for x in chain
+        ]
 
     def flat(chains):
         return [x for chain in chains for x in chain]
 
-    def terms(total):
-        return [] if total is None else [total]
-
-    far = [[pieces[0], pieces[2]], [pieces[1], pieces[3]]]
-    near = [[pieces[2], pieces[0]], [pieces[3], pieces[1]]]
-    batch = list(pieces)
-    arrivals = []
-    for step in range(1, hops):
-        far = hop(far, () if own is None else (own, other))
-        batch += flat(far)
-        if step % 2 == 1 or step == hops - 1:
-            other = add(other_half, batch, terms(other))
-            own = add(own_half, batch, terms(own))
-            batch = []
-    near = once(near, far)
-    theirs = []
-    for k in range(1, pair_count):
-        route = [(i, (i + k) % pair_count) for i in range(pair_count)]
-        theirs.append([[lax.ppermute(x, "pair", route) for x in chain] for chain in far])
-    for step in range(1, hops):
-        near = hop(near, (own, other) if step % 2 == 0 else ())
-        batch += flat(near)
-        if step % 2 == 0 and step < hops - 1:
-            other = add(other_half, batch, terms(other))
-            own = add(own_half, batch, terms(own))
-            batch = []
-    far = hop(once(far, near), (own, other))
-    other = add(other_half, batch, terms(other))
-    moved = lax.ppermute(other, "seq", swap)
-    partial_grad = add(own_half, batch, [own, moved], (student, s_scale), jnp.bfloat16)
-    summed = partial_grad
+    def last_cut(chains):
+        cuts = []
+        for k, (onto, off) in enumerate(chains):
+            first, second = split(onto.shape[0] // 2, 2)
+            if k % 2:
+                first, second = second, first
+            cuts.append((cut(onto, 0, first), cut(off, first, second)))
+        return cuts
+
+    def around(pieces, began, before, **options):
+        chains = [(x, x) for x in pieces]
+        batch = list(pieces) + [lax.ppermute(x, "seq", swap) for x in pieces]
+        if began:
+            chains = [(after(on, done[0]), after(off, done[1])) for (on, off), done in zip(chains, began)]
+        total = None
+        older = before
+        for step in range(1, hops + 1):
+            if step == hops:
+                chains = last_cut(chains)
+            chains = hop(chains, older)
+            older = () if total is None else (total,)
+            if batch and (step > 1 or not MERGE_FIRST):
+                total = add(batch, total)
+                batch = []
+            batch += flat(chains) + swapped(chains, older if total is None else (total,))
+        return chains, (total,), add(batch, total, **options)
+
+    arrived, before, own = around(pieces, None, (), project=(student, s_scale), dtype=jnp.bfloat16)
     distance = 1
+    summands = (own,)
     while distance < pair_count:
-        half = summed.astype(jnp.bfloat16)
-        arrived = lax.ppermute(half, "pair", [(i, i ^ distance) for i in range(pair_count)])
-        summed = half.astype(jnp.float32) + arrived.astype(jnp.float32)
+        value = sum(x.astype(jnp.float32) for x in summands).astype(jnp.bfloat16)
+        route = [(i, i ^ distance) for i in range(pair_count)]
+        summands = (value, lax.ppermute(value, "pair", route))
         distance *= 2
-    own, other = None, None
-    for chains in theirs:
-        batch = flat(far)
-        far = hop(once(chains, far), (partial_grad,))
-        other = add(other_half, batch, terms(other))
-        own = add(own_half, batch, terms(own))
-    batch = flat(far)
-    other = add(other_half, batch, terms(other))
-    moved = lax.ppermute(other, "seq", swap)
-    total = add(own_half, batch, terms(own) + [moved], (student, s_scale))
-    return s_scale * (summed + total)
+    if not doubled:
+        return s_scale * sum(x.astype(jnp.float32) for x in summands)
+
+    ends = own_half.reshape(2, pair_count, share, width)[:, :, share - doubled :]
+    lasts, at = [], 0
+    for n in split(doubled, 2):
+        if n:
+            lasts.append(ends[:, :, at : at + n].reshape(2 * pair_count * n, width))
+        at += n
+    _, _, result = around(lasts, arrived, (own,), project=(student, s_scale), summands=summands)
+    return result
 
 
 def solution(mesh):

time: 256 us -> 209 us (0.82)
  Pallas kernels: 80.2 us -> 43.6 us
  starting transfers between devices: 40.5 us -> 20.5 us
  waiting for transfers between devices: 118 us -> 138 us
  local copies, waits for them, and re-layouts: 12.2 us -> 2.16 us
    pallas_call x12 -> x4, Pallas kernels: 77.2 us -> 38.7 us  [add_relation(): pl.pallas_call(functools.partial(relation_kernel, margin, weight, counts,...]
    ppermute x40 -> x35, waiting for transfers between devices: 118 us -> 138 us  [the longest x8 54 us: hop(): lax.ppermute(off, 'seq', back)]
    ppermute x40 -> x35, starting transfers between devices: 40.5 us -> 20.5 us  [the longest x8 11.1 us: hop(): lax.ppermute(onto, 'seq', onward)]
    unnamed x32 -> x8, local copies, waits for them, and re-layouts: 12.2 us -> 2.03 us
    pallas_call x1, Pallas kernels: 0.44 us -> 3.74 us  [pack_share(): pl.pallas_call(functools.partial(pack_kernel, counts), grid_spec=pltpu.Pr...]
  transfers between devices with their start and end apart: 40 -> 35, of which waited for: 20 -> 15; matrix products, arithmetic and copies ran while one was open for 0% -> 0% of each run, Pallas kernels for 26% -> 16%
where the time goes in v1:
time: 209 us
  waiting for transfers between devices  138 us (66%)
  Pallas kernels  43.6 us (21%)
  starting transfers between devices  20.5 us (10%)
  other arithmetic  4.1 us (2%)
  local copies, waits for them, and re-layouts  2.16 us (1%)
    ppermute x8, waiting for transfers between devices, hop(): lax.ppermute(off, 'seq', back)  54 us
    ppermute x8, waiting for transfers between devices, hop(): lax.ppermute(onto, 'seq', onward)  42.6 us
    ppermute x1, waiting for transfers between devices, local(): summands = (value, lax.ppermute(value, 'pair', route))  39.8 us
    pallas_call x4, Pallas kernels, add_relation(): pl.pallas_call(functools.partial(relation_kernel, margin, weight, counts,...  38.7 us
    ppermute x8, starting transfers between devices, hop(): lax.ppermute(onto, 'seq', onward)  11.1 us
    ppermute x8, starting transfers between devices, hop(): lax.ppermute(off, 'seq', back)  6.53 us
  transfers between devices with their start and end apart: 35, of which 15 were waited for; matrix products, arithmetic and copies ran while one was open for 0% of the time, Pallas kernels for 16%

profile of v1, /device:TPU:0, one launch (start us, length us, event | category | flops | bytes accessed | tf_op | source)
XLA Modules:
  0.0 208.9 jit_solution(15520696542374509566)
XLA Ops:
  0.0 3.7 %shard_map.28 = (bf16[320,1408]{1,0:T(8,128)(2,1)}, bf16[320,1408]{1,0:T(8,128)(2,1)}) custom-call(s32[1]{0:T(128)} %bitcast.which, f32[640,1408]{1,0:T(8,128)} %refs_10_.1, f32[640,1408]{1,0:T(8,128)} %teacher.3), custom_call_target="tpu_custom_call" | custom-call | flops 2703360 | bytes 5406720 | tf_op jit(solution)/shard_map/pallas_call | solution.py:66
  3.7 3.0 %collective-permute-start = (bf16[320,1408]{1,0:T(8,128)(2,1)}, bf16[320,1408]{1,0:T(8,128)(2,1)S(1)}, u32[]{:S(2)}, u32[]{:S(2)}) collective-permute-start(bf16[320,1408]{1,0:T(8,128)(2,1)} %get-tuple-element.24.refs_1_), channel_id=1, source_target_pairs={{0,8},{2,10},{8,16},{10,18},{16,24},{18,26},{24,28},{26,30},{28,20... | collective-permute-start | bytes 2703368 | tf_op jit(solution)/shard_map/ppermute | solution.py:201
  6.8 2.0 collective-permute-start.8
  8.8 18.9 %collective-permute-done.refs_5_ = bf16[320,1408]{1,0:T(8,128)(2,1)S(1)} collective-permute-done((bf16[320,1408]{1,0:T(8,128)(2,1)}, bf16[320,1408]{1,0:T(8,128)(2,1)S(1)}, u32[]{:S(2)}, u32[]{:S(2)}) %collective-permute-start) | collective-permute-done | bytes 901152 | tf_op jit(solution)/shard_map/ppermute | solution.py:201
  27.7 2.2 %collective-permute-done.4.refs_6_ = bf16[320,1408]{1,0:T(8,128)(2,1)S(1)} collective-permute-done((bf16[320,1408]{1,0:T(8,128)(2,1)}, bf16[320,1408]{1,0:T(8,128)(2,1)S(1)}, u32[]{:S(2)}, u32[]{:S(2)}) %collective-permute-start.4) | collective-permute-done | bytes 901152 | tf_op jit(solution)/shard_map/ppermute | solution.py:201
  29.9 16.3 %collective-permute-done.8.refs_7_ = bf16[320,1408]{1,0:T(8,128)(2,1)S(1)} collective-permute-done((bf16[320,1408]{1,0:T(8,128)(2,1)}, bf16[320,1408]{1,0:T(8,128)(2,1)S(1)}, u32[]{:S(2)}, u32[]{:S(2)}) %collective-permute-start.8) | collective-permute-done | bytes 901152 | tf_op jit(solution)/shard_map/ppermute | solution.py:201
  46.2 1.5 collective-permute-done.13.refs_8_
  47.8 0.7 collective-permute-start.19
  48.5 1.3 collective-permute-start.9
  49.8 2.0 copy-done.1
  51.8 1.2 shard_map.29
  53.1 1.6 collective-permute-start.1
  55.1 15.4 %collective-permute-done.19.refs_4_ = bf16[320,1408]{1,0:T(8,128)(2,1)S(1)} collective-permute-done((bf16[320,1408]{1,0:T(8,128)(2,1)S(1)}, bf16[320,1408]{1,0:T(8,128)(2,1)S(1)}, u32[]{:S(2)}, u32[]{:S(2)}) %collective-permute-start.19) | collective-permute-done | bytes 901152 | tf_op jit(solution)/shard_map/ppermute | solution.py:201
  70.6 0.8 collective-permute-start.20
  71.4 1.2 collective-permute-start.10
  72.6 13.8 %shard_map.30.refs_9_ = f32[640,1408]{1,0:T(8,128)S(1)} custom-call(bf16[2,640,1408]{2,1,0:T(8,128)(2,1)S(1)} %get-tuple-element.28.refs_0_, bf16[320,1408]{1,0:T(8,128)(2,1)S(1)} %copy-done.2, bf16[320,1408]{1,0:T(8,128)(2,1)S(1)} %copy-done.3, bf16[320,1408]{1,0:T(8,128)(2,1)S(1)} %collective-permute-done.11.refs_3_, ...), custom_call_target="tpu_custom_call" | custom-call | flops 10380902400 | bytes 21626880 | tf_op jit(solution)/shard_map/pallas_call | solution.py:133
  86.4 4.3 %collective-permute-done.1.refs_1_ = bf16[320,1408]{1,0:T(8,128)(2,1)S(1)} collective-permute-done((bf16[320,1408]{1,0:T(8,128)(2,1)S(1)}, bf16[320,1408]{1,0:T(8,128)(2,1)S(1)}, u32[]{:S(2)}, u32[]{:S(2)}) %collective-permute-start.1) | collective-permute-done | bytes 901152 | tf_op jit(solution)/shard_map/ppermute | solution.py:201
  91.2 17.6 %collective-permute-done.20.refs_4_ = bf16[320,1408]{1,0:T(8,128)(2,1)S(1)} collective-permute-done((bf16[320,1408]{1,0:T(8,128)(2,1)S(1)}, bf16[320,1408]{1,0:T(8,128)(2,1)S(1)}, u32[]{:S(2)}, u32[]{:S(2)}) %collective-permute-start.20) | collective-permute-done | bytes 901152 | tf_op jit(solution)/shard_map/ppermute | solution.py:201
  108.8 1.6 collective-permute-start.6
  111.3 9.4 %shard_map.31.refs_9_ = f32[640,1408]{1,0:T(8,128)S(1)} custom-call(bf16[2,640,1408]{2,1,0:T(8,128)(2,1)S(1)} %get-tuple-element.28.refs_0_, bf16[320,1408]{1,0:T(8,128)(2,1)S(1)} %collective-permute-done.1.refs_1_, bf16[320,1408]{1,0:T(8,128)(2,1)S(1)} %collective-permute-done.5.refs_2_, ...), custom_call_target="tpu_custom_call", output_to_operand_aliasing={{}: (9, {})} | custom-call | flops 6920601600 | bytes 18022400 | tf_op jit(solution)/shard_map/pallas_call | solution.py:133
  121.3 10.0 %collective-permute-done.6.refs_2_ = bf16[320,1408]{1,0:T(8,128)(2,1)S(1)} collective-permute-done((bf16[320,1408]{1,0:T(8,128)(2,1)S(1)}, bf16[320,1408]{1,0:T(8,128)(2,1)S(1)}, u32[]{:S(2)}, u32[]{:S(2)}) %collective-permute-start.6) | collective-permute-done | bytes 901152 | tf_op jit(solution)/shard_map/ppermute | solution.py:201
  131.8 1.5 collective-permute-start.21
  134.1 1.5 collective-permute-start.7
  136.1 9.4 %shard_map.32.refs_9_ = f32[640,1408]{1,0:T(8,128)S(1)} custom-call(bf16[2,640,1408]{2,1,0:T(8,128)(2,1)S(1)} %get-tuple-element.28.refs_0_, bf16[320,1408]{1,0:T(8,128)(2,1)S(1)} %collective-permute-done.2.refs_1_, bf16[320,1408]{1,0:T(8,128)(2,1)S(1)} %collective-permute-done.6.refs_2_, ...), custom_call_target="tpu_custom_call", output_to_operand_aliasing={{}: (9, {})} | custom-call | flops 6920601600 | bytes 18022400 | tf_op jit(solution)/shard_map/pallas_call | solution.py:133
  145.6 1.1 collective-permute-done.18.refs_3_
  146.7 7.3 %collective-permute-done.7.refs_2_ = bf16[160,1408]{1,0:T(8,128)(2,1)S(1)} collective-permute-done((bf16[160,1408]{1,0:T(8,128)(2,1)S(1)}, bf16[160,1408]{1,0:T(8,128)(2,1)S(1)}, u32[]{:S(2)}, u32[]{:S(2)}) %collective-permute-start.7) | collective-permute-done | bytes 450592 | tf_op jit(solution)/shard_map/ppermute | solution.py:201
  154.0 1.6 collective-permute-done.3.refs_1_
  155.8 1.6 collective-permute-done.30.refs_5_
  157.4 6.2 %shard_map.33 = bf16[640,1408]{1,0:T(8,128)(2,1)S(1)} custom-call(bf16[2,640,1408]{2,1,0:T(8,128)(2,1)S(1)} %get-tuple-element.28.refs_0_, bf16[160,1408]{1,0:T(8,128)(2,1)S(1)} %collective-permute-done.3.refs_1_, bf16[160,1408]{1,0:T(8,128)(2,1)S(1)} %collective-permute-done.7.refs_2_, bf16[160,1408]{1,0:T(8,128)(2,1)S(1)} %collective-permute-done.18.refs_3_, ...), custom_call_target="tpu_custom_call" | custom-call | flops 3460300800 | bytes 14417920 | tf_op jit(solution)/shard_map/pallas_call | solution.py:133
  163.6 1.6 collective-permute-start.34
  165.4 39.8 %collective-permute-done.34 = bf16[640,1408]{1,0:T(8,128)(2,1)} collective-permute-done((bf16[640,1408]{1,0:T(8,128)(2,1)S(1)}, bf16[640,1408]{1,0:T(8,128)(2,1)}, u32[]{:S(2)}, u32[]{:S(2)}) %collective-permute-start.34) | collective-permute-done | bytes 1802272 | tf_op jit(solution)/shard_map/ppermute | solution.py:247
  205.1 3.8 %add_multiply_fusion = f32[640,1408]{1,0:T(8,128)} fusion(bf16[640,1408]{1,0:T(8,128)(2,1)} %collective-permute-done.34, bf16[640,1408]{1,0:T(8,128)(2,1)S(1)} %shard_map.33, f32[640]{0:T(1024)S(1)} %reduce), kind=kLoop, calls=%fused_computation | loop fusion | flops 3604480 | bytes 7211520 | tf_op jit(solution)/shard_map/mul | solution.py:250
  (62 shorter events, 4.8 us)
Async XLA Ops:
  3.7 24.0 %collective-permute-start = (bf16[320,1408]{1,0:T(8,128)(2,1)}, bf16[320,1408]{1,0:T(8,128)(2,1)S(1)}, u32[]{:S(2)}, u32[]{:S(2)}) collective-permute-start(bf16[320,1408]{1,0:T(8,128)(2,1)} %get-tuple-element.24.refs_1_), channel_id=1, source_target_pairs={{0,8},{2,10},{8,16},{10,18},{16,24},{18,26},{24,28},{26,30},{28,20... | collective-permute-start | bytes 2703368 | tf_op jit(solution)/shard_map/ppermute | solution.py:201
  6.8 23.1 %collective-permute-start.4 = (bf16[320,1408]{1,0:T(8,128)(2,1)}, bf16[320,1408]{1,0:T(8,128)(2,1)S(1)}, u32[]{:S(2)}, u32[]{:S(2)}) collective-permute-start(bf16[320,1408]{1,0:T(8,128)(2,1)} %get-tuple-element.24.refs_1_), channel_id=1, source_target_pairs={{8,0},{10,2},{16,8},{18,10},{24,16},{26,18},{28,24},{30,26},{20,28... | collective-permute-start | bytes 2703368 | tf_op jit(solution)/shard_map/ppermute | solution.py:201
  6.8 39.5 %collective-permute-start.8 = (bf16[320,1408]{1,0:T(8,128)(2,1)}, bf16[320,1408]{1,0:T(8,128)(2,1)S(1)}, u32[]{:S(2)}, u32[]{:S(2)}) collective-permute-start(bf16[320,1408]{1,0:T(8,128)(2,1)} %get-tuple-element.25.refs_2_), channel_id=1, source_target_pairs={{0,8},{2,10},{8,16},{10,18},{16,24},{18,26},{24,28},{26,30},{28,20... | collective-permute-start | bytes 2703368 | tf_op jit(solution)/shard_map/ppermute | solution.py:201
  8.8 39.0 %collective-permute-start.13 = (bf16[320,1408]{1,0:T(8,128)(2,1)}, bf16[320,1408]{1,0:T(8,128)(2,1)S(1)}, u32[]{:S(2)}, u32[]{:S(2)}) collective-permute-start(bf16[320,1408]{1,0:T(8,128)(2,1)} %get-tuple-element.25.refs_2_), channel_id=1, source_target_pairs={{8,0},{10,2},{16,8},{18,10},{24,16},{26,18},{28,24},{30,26},{20,28... | collective-permute-start | bytes 2703368 | tf_op jit(solution)/shard_map/ppermute | solution.py:201
  8.8 39.0 %collective-permute-start.11 = (bf16[320,1408]{1,0:T(8,128)(2,1)}, bf16[320,1408]{1,0:T(8,128)(2,1)S(1)}, u32[]{:S(2)}, u32[]{:S(2)}) collective-permute-start(bf16[320,1408]{1,0:T(8,128)(2,1)} %get-tuple-element.24.refs_1_), channel_id=1, source_target_pairs={{0,2},{2,0},{4,6},{6,4},{8,10},{10,8},{12,14},{14,12},{16,18},{18,... | collective-permute-start | bytes 2703368 | tf_op jit(solution)/shard_map/ppermute | solution.py:225
  27.7 20.7 %collective-permute-start.12 = (bf16[320,1408]{1,0:T(8,128)(2,1)}, bf16[320,1408]{1,0:T(8,128)(2,1)S(1)}, u32[]{:S(2)}, u32[]{:S(2)}) collective-permute-start(bf16[320,1408]{1,0:T(8,128)(2,1)} %get-tuple-element.25.refs_2_), channel_id=1, source_target_pairs={{0,2},{2,0},{4,6},{6,4},{8,10},{10,8},{12,14},{14,12},{16,18},{18,... | collective-permute-start | bytes 2703368 | tf_op jit(solution)/shard_map/ppermute | solution.py:225
  29.9 19.9 %collective-permute-start.14 = (bf16[320,1408]{1,0:T(8,128)(2,1)S(1)}, bf16[320,1408]{1,0:T(8,128)(2,1)S(1)}, u32[]{:S(2)}, u32[]{:S(2)}) collective-permute-start(bf16[320,1408]{1,0:T(8,128)(2,1)S(1)} %collective-permute-done.refs_5_), channel_id=1, source_target_pairs={{0,2},{2,0},{4,6},{6,4},{8,10},{10,8},{12,14},{14,12},{16,18},{18,... | collective-permute-start | bytes 2703368 | tf_op jit(solution)/shard_map/ppermute | solution.py:206
  46.2 6.8 %collective-permute-start.15 = (bf16[320,1408]{1,0:T(8,128)(2,1)S(1)}, bf16[320,1408]{1,0:T(8,128)(2,1)S(1)}, u32[]{:S(2)}, u32[]{:S(2)}) collective-permute-start(bf16[320,1408]{1,0:T(8,128)(2,1)S(1)} %collective-permute-done.4.refs_6_), channel_id=1, source_target_pairs={{0,2},{2,0},{4,6},{6,4},{8,10},{10,8},{12,14},{14,12},{16,18},{18,... | collective-permute-start | bytes 2703368 | tf_op jit(solution)/shard_map/ppermute | solution.py:206
  47.7 6.9 %collective-permute-start.16 = (bf16[320,1408]{1,0:T(8,128)(2,1)S(1)}, bf16[320,1408]{1,0:T(8,128)(2,1)S(1)}, u32[]{:S(2)}, u32[]{:S(2)}) collective-permute-start(bf16[320,1408]{1,0:T(8,128)(2,1)S(1)} %collective-permute-done.8.refs_7_), channel_id=1, source_target_pairs={{0,2},{2,0},{4,6},{6,4},{8,10},{10,8},{12,14},{14,12},{16,18},{18,... | collective-permute-start | bytes 2703368 | tf_op jit(solution)/shard_map/ppermute | solution.py:206
  47.8 22.8 %collective-permute-start.19 = (bf16[320,1408]{1,0:T(8,128)(2,1)S(1)}, bf16[320,1408]{1,0:T(8,128)(2,1)S(1)}, u32[]{:S(2)}, u32[]{:S(2)}) collective-permute-start(bf16[320,1408]{1,0:T(8,128)(2,1)S(1)} %collective-permute-done.13.refs_8_), channel_id=1, source_target_pairs={{8,0},{10,2},{16,8},{18,10},{24,16},{26,18},{28,24},{30,26},{20,28... | collective-permute-start | bytes 2703368 | tf_op jit(solution)/shard_map/ppermute | solution.py:201
  48.5 22.9 %collective-permute-start.9 = (bf16[320,1408]{1,0:T(8,128)(2,1)S(1)}, bf16[320,1408]{1,0:T(8,128)(2,1)S(1)}, u32[]{:S(2)}, u32[]{:S(2)}) collective-permute-start(bf16[320,1408]{1,0:T(8,128)(2,1)S(1)} %collective-permute-done.8.refs_7_), channel_id=1, source_target_pairs={{0,8},{2,10},{8,16},{10,18},{16,24},{18,26},{24,28},{26,30},{28,20... | collective-permute-start | bytes 2703368 | tf_op jit(solution)/shard_map/ppermute | solution.py:201
  49.8 22.8 %collective-permute-start.17 = (bf16[320,1408]{1,0:T(8,128)(2,1)S(1)}, bf16[320,1408]{1,0:T(8,128)(2,1)S(1)}, u32[]{:S(2)}, u32[]{:S(2)}) collective-permute-start(bf16[320,1408]{1,0:T(8,128)(2,1)S(1)} %collective-permute-done.13.refs_8_), channel_id=1, source_target_pairs={{0,2},{2,0},{4,6},{6,4},{8,10},{10,8},{12,14},{14,12},{16,18},{18,... | collective-permute-start | bytes 2703368 | tf_op jit(solution)/shard_map/ppermute | solution.py:206
  53.1 37.6 %collective-permute-start.1 = (bf16[320,1408]{1,0:T(8,128)(2,1)S(1)}, bf16[320,1408]{1,0:T(8,128)(2,1)S(1)}, u32[]{:S(2)}, u32[]{:S(2)}) collective-permute-start(bf16[320,1408]{1,0:T(8,128)(2,1)S(1)} %collective-permute-done.refs_5_), channel_id=1, source_target_pairs={{0,8},{2,10},{8,16},{10,18},{16,24},{18,26},{24,28},{26,30},{28,20... | collective-permute-start | bytes 2703368 | tf_op jit(solution)/shard_map/ppermute | solution.py:201
  54.7 36.0 %collective-permute-start.5 = (bf16[320,1408]{1,0:T(8,128)(2,1)S(1)}, bf16[320,1408]{1,0:T(8,128)(2,1)S(1)}, u32[]{:S(2)}, u32[]{:S(2)}) collective-permute-start(bf16[320,1408]{1,0:T(8,128)(2,1)S(1)} %collective-permute-done.4.refs_6_), channel_id=1, source_target_pairs={{8,0},{10,2},{16,8},{18,10},{24,16},{26,18},{28,24},{30,26},{20,28... | collective-permute-start | bytes 2703368 | tf_op jit(solution)/shard_map/ppermute | solution.py:201
  70.6 38.2 %collective-permute-start.20 = (bf16[320,1408]{1,0:T(8,128)(2,1)S(1)}, bf16[320,1408]{1,0:T(8,128)(2,1)S(1)}, u32[]{:S(2)}, u32[]{:S(2)}) collective-permute-start(bf16[320,1408]{1,0:T(8,128)(2,1)S(1)} %collective-permute-done.19.refs_4_), channel_id=1, source_target_pairs={{8,0},{10,2},{16,8},{18,10},{24,16},{26,18},{28,24},{30,26},{20,28... | collective-permute-start | bytes 2703368 | tf_op jit(solution)/shard_map/ppermute | solution.py:201
  71.4 37.5 %collective-permute-start.10 = (bf16[320,1408]{1,0:T(8,128)(2,1)S(1)}, bf16[320,1408]{1,0:T(8,128)(2,1)S(1)}, u32[]{:S(2)}, u32[]{:S(2)}) collective-permute-start(bf16[320,1408]{1,0:T(8,128)(2,1)S(1)} %collective-permute-done.9.refs_3_), channel_id=1, source_target_pairs={{0,8},{2,10},{8,16},{10,18},{16,24},{18,26},{24,28},{26,30},{28,20... | collective-permute-start | bytes 2703368 | tf_op jit(solution)/shard_map/ppermute | solution.py:201
  90.7 19.8 %collective-permute-start.22 = (bf16[320,1408]{1,0:T(8,128)(2,1)S(1)}, bf16[320,1408]{1,0:T(8,128)(2,1)S(1)}, u32[]{:S(2)}, u32[]{:S(2)}) collective-permute-start(bf16[320,1408]{1,0:T(8,128)(2,1)S(1)} %collective-permute-done.1.refs_1_), channel_id=1, source_target_pairs={{0,2},{2,0},{4,6},{6,4},{8,10},{10,8},{12,14},{14,12},{16,18},{18,... | collective-permute-start | bytes 2703368 | tf_op jit(solution)/shard_map/ppermute | solution.py:206
  90.7 20.6 %collective-permute-start.23 = (bf16[320,1408]{1,0:T(8,128)(2,1)S(1)}, bf16[320,1408]{1,0:T(8,128)(2,1)S(1)}, u32[]{:S(2)}, u32[]{:S(2)}) collective-permute-start(bf16[320,1408]{1,0:T(8,128)(2,1)S(1)} %collective-permute-done.5.refs_2_), channel_id=1, source_target_pairs={{0,2},{2,0},{4,6},{6,4},{8,10},{10,8},{12,14},{14,12},{16,18},{18,... | collective-permute-start | bytes 2703368 | tf_op jit(solution)/shard_map/ppermute | solution.py:206
  91.2 20.1 %collective-permute-start.24 = (bf16[320,1408]{1,0:T(8,128)(2,1)S(1)}, bf16[320,1408]{1,0:T(8,128)(2,1)S(1)}, u32[]{:S(2)}, u32[]{:S(2)}) collective-permute-start(bf16[320,1408]{1,0:T(8,128)(2,1)S(1)} %collective-permute-done.9.refs_3_), channel_id=1, source_target_pairs={{0,2},{2,0},{4,6},{6,4},{8,10},{10,8},{12,14},{14,12},{16,18},{18,... | collective-permute-start | bytes 2703368 | tf_op jit(solution)/shard_map/ppermute | solution.py:206
  108.8 22.5 %collective-permute-start.6 = (bf16[320,1408]{1,0:T(8,128)(2,1)S(1)}, bf16[320,1408]{1,0:T(8,128)(2,1)S(1)}, u32[]{:S(2)}, u32[]{:S(2)}) collective-permute-start(bf16[320,1408]{1,0:T(8,128)(2,1)S(1)} %collective-permute-done.5.refs_2_), channel_id=1, source_target_pairs={{8,0},{10,2},{16,8},{18,10},{24,16},{26,18},{28,24},{30,26},{20,28... | collective-permute-start | bytes 2703368 | tf_op jit(solution)/shard_map/ppermute | solution.py:201
  110.5 21.1 %collective-permute-start.2 = (bf16[320,1408]{1,0:T(8,128)(2,1)S(1)}, bf16[320,1408]{1,0:T(8,128)(2,1)S(1)}, u32[]{:S(2)}, u32[]{:S(2)}) collective-permute-start(bf16[320,1408]{1,0:T(8,128)(2,1)S(1)} %collective-permute-done.1.refs_1_), channel_id=1, source_target_pairs={{0,8},{2,10},{8,16},{10,18},{16,24},{18,26},{24,28},{26,30},{28,20... | collective-permute-start | bytes 2703368 | tf_op jit(solution)/shard_map/ppermute | solution.py:201
  120.7 12.8 %collective-permute-start.29 = (bf16[320,1408]{1,0:T(8,128)(2,1)S(1)}, bf16[320,1408]{1,0:T(8,128)(2,1)S(1)}, u32[]{:S(2)}, u32[]{:S(2)}) collective-permute-start(bf16[320,1408]{1,0:T(8,128)(2,1)S(1)} %collective-permute-done.20.refs_4_), channel_id=1, source_target_pairs={{0,2},{2,0},{4,6},{6,4},{8,10},{10,8},{12,14},{14,12},{16,18},{18,... | collective-permute-start | bytes 2703368 | tf_op jit(solution)/shard_map/ppermute | solution.py:206
  120.8 13.3 %collective-permute-start.28 = (bf16[320,1408]{1,0:T(8,128)(2,1)S(1)}, bf16[320,1408]{1,0:T(8,128)(2,1)S(1)}, u32[]{:S(2)}, u32[]{:S(2)}) collective-permute-start(bf16[320,1408]{1,0:T(8,128)(2,1)S(1)} %collective-permute-done.10.refs_3_), channel_id=1, source_target_pairs={{0,2},{2,0},{4,6},{6,4},{8,10},{10,8},{12,14},{14,12},{16,18},{18,... | collective-permute-start | bytes 2703368 | tf_op jit(solution)/shard_map/ppermute | solution.py:206
  131.3 4.2 %collective-permute-start.27 = (bf16[320,1408]{1,0:T(8,128)(2,1)S(1)}, bf16[320,1408]{1,0:T(8,128)(2,1)S(1)}, u32[]{:S(2)}, u32[]{:S(2)}) collective-permute-start(bf16[320,1408]{1,0:T(8,128)(2,1)S(1)} %collective-permute-done.6.refs_2_), channel_id=1, source_target_pairs={{0,2},{2,0},{4,6},{6,4},{8,10},{10,8},{12,14},{14,12},{16,18},{18,... | collective-permute-start | bytes 2703368 | tf_op jit(solution)/shard_map/ppermute | solution.py:206
  131.6 4.5 %collective-permute-start.26 = (bf16[320,1408]{1,0:T(8,128)(2,1)S(1)}, bf16[320,1408]{1,0:T(8,128)(2,1)S(1)}, u32[]{:S(2)}, u32[]{:S(2)}) collective-permute-start(bf16[320,1408]{1,0:T(8,128)(2,1)S(1)} %collective-permute-done.2.refs_1_), channel_id=1, source_target_pairs={{0,2},{2,0},{4,6},{6,4},{8,10},{10,8},{12,14},{14,12},{16,18},{18,... | collective-permute-start | bytes 2703368 | tf_op jit(solution)/shard_map/ppermute | solution.py:206
  131.8 13.7 %collective-permute-start.21 = (bf16[160,1408]{1,0:T(8,128)(2,1)S(1)}, bf16[160,1408]{1,0:T(8,128)(2,1)S(1)}, u32[]{:S(2)}, u32[]{:S(2)}) collective-permute-start(bf16[160,1408]{1,0:T(8,128)(2,1)S(1)} %pad_maximum_fusion.3), channel_id=1, source_target_pairs={{8,0},{10,2},{16,8},{18,10},{24,16},{26,18},{28,24},{30,26},{20,28... | collective-permute-start | bytes 1351688 | tf_op jit(solution)/shard_map/ppermute | solution.py:201
  133.5 13.2 %collective-permute-start.18 = (bf16[160,1408]{1,0:T(8,128)(2,1)S(1)}, bf16[160,1408]{1,0:T(8,128)(2,1)S(1)}, u32[]{:S(2)}, u32[]{:S(2)}) collective-permute-start(bf16[160,1408]{1,0:T(8,128)(2,1)S(1)} %pad_maximum_fusion.2), channel_id=1, source_target_pairs={{0,8},{2,10},{8,16},{10,18},{16,24},{18,26},{24,28},{26,30},{28,20... | collective-permute-start | bytes 1351688 | tf_op jit(solution)/shard_map/ppermute | solution.py:201
  134.1 20.0 %collective-permute-start.7 = (bf16[160,1408]{1,0:T(8,128)(2,1)S(1)}, bf16[160,1408]{1,0:T(8,128)(2,1)S(1)}, u32[]{:S(2)}, u32[]{:S(2)}) collective-permute-start(bf16[160,1408]{1,0:T(8,128)(2,1)S(1)} %pad_maximum_fusion.1), channel_id=1, source_target_pairs={{8,0},{10,2},{16,8},{18,10},{24,16},{26,18},{28,24},{30,26},{20,28... | collective-permute-start | bytes 1351688 | tf_op jit(solution)/shard_map/ppermute | solution.py:201
  135.5 20.1 %collective-permute-start.3 = (bf16[160,1408]{1,0:T(8,128)(2,1)S(1)}, bf16[160,1408]{1,0:T(8,128)(2,1)S(1)}, u32[]{:S(2)}, u32[]{:S(2)}) collective-permute-start(bf16[160,1408]{1,0:T(8,128)(2,1)S(1)} %pad_maximum_fusion), channel_id=1, source_target_pairs={{0,8},{2,10},{8,16},{10,18},{16,24},{18,26},{24,28},{26,30},{28,20... | collective-permute-start | bytes 1351688 | tf_op jit(solution)/shard_map/ppermute | solution.py:201
  145.5 10.2 %collective-permute-start.33 = (bf16[160,1408]{1,0:T(8,128)(2,1)S(1)}, bf16[160,1408]{1,0:T(8,128)(2,1)S(1)}, u32[]{:S(2)}, u32[]{:S(2)}) collective-permute-start(bf16[160,1408]{1,0:T(8,128)(2,1)S(1)} %collective-permute-done.21.refs_4_), channel_id=1, source_target_pairs={{0,2},{2,0},{4,6},{6,4},{8,10},{10,8},{12,14},{14,12},{16,18},{18,... | collective-permute-start | bytes 1351688 | tf_op jit(solution)/shard_map/ppermute | solution.py:206
  146.7 9.0 %collective-permute-start.32 = (bf16[160,1408]{1,0:T(8,128)(2,1)S(1)}, bf16[160,1408]{1,0:T(8,128)(2,1)S(1)}, u32[]{:S(2)}, u32[]{:S(2)}) collective-permute-start(bf16[160,1408]{1,0:T(8,128)(2,1)S(1)} %collective-permute-done.18.refs_3_), channel_id=1, source_target_pairs={{0,2},{2,0},{4,6},{6,4},{8,10},{10,8},{12,14},{14,12},{16,18},{18,... | collective-permute-start | bytes 1351688 | tf_op jit(solution)/shard_map/ppermute | solution.py:206
  163.6 41.5 %collective-permute-start.34 = (bf16[640,1408]{1,0:T(8,128)(2,1)S(1)}, bf16[640,1408]{1,0:T(8,128)(2,1)}, u32[]{:S(2)}, u32[]{:S(2)}) collective-permute-start(bf16[640,1408]{1,0:T(8,128)(2,1)S(1)} %shard_map.33), channel_id=1, source_target_pairs={{0,1},{1,0},{2,3},{3,2},{4,5},{5,4},{6,7},{7,6},{8,9},{9,8},{10,11... | collective-permute-start | bytes 5406728 | tf_op jit(solution)/shard_map/ppermute | solution.py:247
  (7 other events, 99.6 us)

commit v2 on v1

--- a/solution.py
+++ b/solution.py
@@ -9,10 +9,12 @@
 from jax.sharding import PartitionSpec as P
 
 CORES = 2
-DOUBLED = 0
-TIE_RELAY = (1,)
-TIE_SWAP = (0, 1)
-MERGE_FIRST = True
+PARTS = 4
+CHAINS = 2
+LAG = 2
+SLAG = 1
+FIRST = 2
+COSTW = 1.0
 ROW_TILE = 16
 VMEM_LIMIT = 32 * 1024 * 1024
 FIRST_VMEM_LIMIT = 58 * 1024 * 1024
@@ -152,14 +154,12 @@
 def ring_routes(count):
     chips = count // CORES
     order = list(range(0, chips, 2)) + list(range(1, chips, 2))[::-1]
-    onward, back = [], []
+    around = []
     for place, chip in enumerate(order):
         following = order[(place + 1) % chips]
-        for core in range(CORES):
-            onward.append((chip * CORES + core, following * CORES + core))
-            back.append((following * CORES + core, chip * CORES + core))
-    swap = [(i, i ^ 1) for i in range(count)]
-    return onward, back, swap
+        around.append((chip * CORES, following * CORES))
+        around.append((following * CORES + 1, chip * CORES + 1))
+    return around, [(to, of) for of, to in around], [(i, i ^ 1) for i in range(count)]
 
 
 def split(tokens, parts):
@@ -169,11 +169,6 @@
 
 def after(x, *values):
     return lax.optimization_barrier((x, *values))[0] if values else x
-
-
-def cut(piece, start, count):
-    tokens = piece.shape[0] // 2
-    return jnp.concatenate([piece[start : start + count], piece[tokens + start : tokens + start + count]])
 
 
 def local(student, teacher):
@@ -183,62 +178,33 @@
     pair_index = lax.axis_index("pair")
     margin = 0.75 / math.sqrt(width)
     weight = 64.0 * width / math.sqrt(rows * seq_count)
-    onward, back, swap = ring_routes(seq_count)
-    hops = seq_count // CORES // 2
+    around, reverse, swap = ring_routes(seq_count)
+    hops = seq_count // CORES - 2
     share = rows // pair_count
-    doubled = max(1, round(DOUBLED * share / ROW_TILE)) * ROW_TILE if pair_count == 2 and DOUBLED else 0
-    pieces = pack_share(student, teacher, pair_index, share, split(share - doubled, 2))
+    pieces = list(pack_share(student, teacher, pair_index, share, split(share, CHAINS)))
     own_half, s_scale = normalize_own(after(student, *pieces), teacher)
 
     def add(batch, total, **options):
         return add_relation(own_half, batch, [] if total is None else [total], margin, weight, **options)
 
-    def hop(chains, wait_for=()):
-        sent = []
-        for k, (onto, off) in enumerate(chains):
-            if k in TIE_RELAY:
-                onto, off = after(onto, *wait_for), after(off, *wait_for)
-            sent.append((lax.ppermute(onto, "seq", onward), lax.ppermute(off, "seq", back)))
-        return sent
-
-    def swapped(chains, wait_for=()):
-        return [
-            lax.ppermute(after(x, *wait_for) if k in TIE_SWAP else x, "seq", swap)
-            for k, chain in enumerate(chains)
-            for x in chain
-        ]
-
-    def flat(chains):
-        return [x for chain in chains for x in chain]
-
-    def last_cut(chains):
-        cuts = []
-        for k, (onto, off) in enumerate(chains):
-            first, second = split(onto.shape[0] // 2, 2)
-            if k % 2:
-                first, second = second, first
-            cuts.append((cut(onto, 0, first), cut(off, first, second)))
-        return cuts
-
-    def around(pieces, began, before, **options):
-        chains = [(x, x) for x in pieces]
-        batch = list(pieces) + [lax.ppermute(x, "seq", swap) for x in pieces]
-        if began:
-            chains = [(after(on, done[0]), after(off, done[1])) for (on, off), done in zip(chains, began)]
-        total = None
-        older = before
-        for step in range(1, hops + 1):
-            if step == hops:
-                chains = last_cut(chains)
-            chains = hop(chains, older)
-            older = () if total is None else (total,)
-            if batch and (step > 1 or not MERGE_FIRST):
-                total = add(batch, total)
-                batch = []
-            batch += flat(chains) + swapped(chains, older if total is None else (total,))
-        return chains, (total,), add(batch, total, **options)
-
-    arrived, before, own = around(pieces, None, (), project=(student, s_scale), dtype=jnp.bfloat16)
+    def move(x, route, *wait_for):
+        return lax.ppermute(after(x, *wait_for), "seq", route)
+
+    batch = pieces + [move(x, swap) for x in pieces]
+    totals = []
+    held = list(pieces)
+    doubled = pair_count == 2
+    for event in range(CHAINS * hops):
+        k = event % CHAINS
+        held[k] = move(held[k], around, *(totals[-1 - LAG :][:1] if len(totals) > LAG else []))
+        if event >= FIRST:
+            totals.append(add(batch, totals[-1] if totals else None))
+            batch = []
+        batch += [held[k], move(held[k], swap, *totals[len(totals) - 1 - SLAG :][:1] if len(totals) > SLAG else [])]
+    if not doubled:
+        nearest = [move(x, reverse) for x in pieces]
+        batch += nearest + [move(x, swap) for x in nearest]
+    own = add(batch, totals[-1], project=(student, s_scale), dtype=jnp.bfloat16)
     distance = 1
     summands = (own,)
     while distance < pair_count:
@@ -246,17 +212,22 @@
         route = [(i, i ^ distance) for i in range(pair_count)]
         summands = (value, lax.ppermute(value, "pair", route))
         distance *= 2
+    summed = sum(x.astype(jnp.float32) for x in summands)
     if not doubled:
-        return s_scale * sum(x.astype(jnp.float32) for x in summands)
-
-    ends = own_half.reshape(2, pair_count, share, width)[:, :, share - doubled :]
-    lasts, at = [], 0
-    for n in split(doubled, 2):
-        if n:
-            lasts.append(ends[:, :, at : at + n].reshape(2 * pair_count * n, width))
+        return s_scale * summed
+
+    total, at, batch = None, 0, []
+    nearest = []
+    for k, n in enumerate(split(rows, PARTS)):
+        part = own_half[:, at : at + n].reshape(2 * n, width)
+        nearest.append(move(part, reverse, *([own] if k == PARTS - 1 else [held[k % CHAINS]])))
         at += n
-    _, _, result = around(lasts, arrived, (own,), project=(student, s_scale), summands=summands)
-    return result
+    for x in nearest[:-1]:
+        batch += [x, move(x, swap, own)]
+    total = add(batch, None)
+    batch = [nearest[-1], move(nearest[-1], swap, total, summands[-1])]
+    total = add(batch, total, project=(student, s_scale))
+    return s_scale * (summed + total)
 
 
 def solution(mesh):

time: 209 us -> 198 us (0.947)
  waiting for transfers between devices: 138 us -> 81.4 us
  Pallas kernels: 43.6 us -> 67.5 us
  starting transfers between devices: 20.5 us -> 34.3 us
  local copies, waits for them, and re-layouts: 2.16 us -> 11.4 us
    ppermute x1, waiting for transfers between devices: 39.8 us -> 8.93 us  [local(): summands = (value, lax.ppermute(value, 'pair', route))]
    ppermute x34, waiting for transfers between devices: 98.5 us -> 72.5 us  [move(): return lax.ppermute(after(x, *wait_for), 'seq', route)]
    pallas_call x4 -> x13, Pallas kernels: 38.7 us -> 62.5 us  [add_relation(): pl.pallas_call(functools.partial(relation_kernel, margin, weight, counts,...]
    ppermute x34, starting transfers between devices: 19 us -> 32.8 us  [move(): return lax.ppermute(after(x, *wait_for), 'seq', route)]
    unnamed x8 -> x22, local copies, waits for them, and re-layouts: 2.03 us -> 11.1 us
  transfers between devices with their start and end apart: 35 -> 35, of which waited for: 15 -> 17; matrix products, arithmetic and copies ran while one was open for 0% -> 0% of each run, Pallas kernels for 16% -> 29%
where the time goes in v2:
time: 198 us; the launch traced here: 197 us
  waiting for transfers between devices  81.4 us (41%)
  Pallas kernels  67.5 us (34%)
  starting transfers between devices  34.3 us (17%)
  local copies, waits for them, and re-layouts  11.4 us (6%)
  other arithmetic  2.6 us (1%)
    ppermute x34, waiting for transfers between devices, move(): return lax.ppermute(after(x, *wait_for), 'seq', route)  72.5 us
    pallas_call x13, Pallas kernels, add_relation(): pl.pallas_call(functools.partial(relation_kernel, margin, weight, counts,...  62.5 us
    ppermute x34, starting transfers between devices, move(): return lax.ppermute(after(x, *wait_for), 'seq', route)  32.8 us
    unnamed x22, local copies, waits for them, and re-layouts  11.1 us
    ppermute x1, waiting for transfers between devices, local(): summands = (value, lax.ppermute(value, 'pair', route))  8.93 us
  transfers between devices with their start and end apart: 35, of which 17 were waited for; matrix products, arithmetic and copies ran while one was open for 0% of the time, Pallas kernels for 29%

profile of v2, /device:TPU:0, one launch (start us, length us, event | category | flops | bytes accessed | tf_op | source)
XLA Modules:
  0.0 197.5 jit_solution(8090571170619663597)
XLA Ops:
  0.0 3.8 %shard_map.28 = (bf16[320,1408]{1,0:T(8,128)(2,1)}, bf16[320,1408]{1,0:T(8,128)(2,1)}) custom-call(s32[1]{0:T(128)} %bitcast.which, f32[640,1408]{1,0:T(8,128)} %refs_4_.3, f32[640,1408]{1,0:T(8,128)} %teacher.3), custom_call_target="tpu_custom_call" | custom-call | flops 2703360 | bytes 5406720 | tf_op jit(solution)/shard_map/pallas_call | solution.py:68
  3.8 3.0 %collective-permute-start.4 = (bf16[320,1408]{1,0:T(8,128)(2,1)}, bf16[320,1408]{1,0:T(8,128)(2,1)S(1)}, u32[]{:S(2)}, u32[]{:S(2)}) collective-permute-start(bf16[320,1408]{1,0:T(8,128)(2,1)} %get-tuple-element.27.refs_1_), channel_id=1, source_target_pairs={{0,8},{10,2},{8,16},{18,10},{16,24},{26,18},{24,28},{30,26},{28,20... | collective-permute-start | bytes 2703368 | tf_op jit(solution)/shard_map/ppermute | solution.py:191
  8.4 9.8 %collective-permute-done.4.refs_5_ = bf16[320,1408]{1,0:T(8,128)(2,1)S(1)} collective-permute-done((bf16[320,1408]{1,0:T(8,128)(2,1)}, bf16[320,1408]{1,0:T(8,128)(2,1)S(1)}, u32[]{:S(2)}, u32[]{:S(2)}) %collective-permute-start.4) | collective-permute-done | bytes 901152 | tf_op jit(solution)/shard_map/ppermute | solution.py:191
  20.7 7.1 %collective-permute-done.refs_7_ = bf16[320,1408]{1,0:T(8,128)(2,1)S(1)} collective-permute-done((bf16[320,1408]{1,0:T(8,128)(2,1)}, bf16[320,1408]{1,0:T(8,128)(2,1)S(1)}, u32[]{:S(2)}, u32[]{:S(2)}) %collective-permute-start) | collective-permute-done | bytes 901152 | tf_op jit(solution)/shard_map/ppermute | solution.py:191
  27.8 2.1 %collective-permute-start.1 = (bf16[320,1408]{1,0:T(8,128)(2,1)S(1)}, bf16[320,1408]{1,0:T(8,128)(2,1)S(1)}, u32[]{:S(2)}, u32[]{:S(2)}) collective-permute-start(bf16[320,1408]{1,0:T(8,128)(2,1)S(1)} %collective-permute-done.refs_7_), channel_id=1, source_target_pairs={{0,8},{10,2},{8,16},{18,10},{16,24},{26,18},{24,28},{30,26},{28,20... | collective-permute-start | bytes 2703368 | tf_op jit(solution)/shard_map/ppermute | solution.py:191
  33.2 4.3 %collective-permute-done.9.refs_1_ = bf16[320,1408]{1,0:T(8,128)(2,1)S(1)} collective-permute-done((bf16[320,1408]{1,0:T(8,128)(2,1)S(1)}, bf16[320,1408]{1,0:T(8,128)(2,1)S(1)}, u32[]{:S(2)}, u32[]{:S(2)}) %collective-permute-start.9) | collective-permute-done | bytes 901152 | tf_op jit(solution)/shard_map/ppermute | solution.py:191
  39.6 9.0 %shard_map.30.refs_3_ = f32[640,1408]{1,0:T(8,128)S(1)} custom-call(bf16[2,640,1408]{2,1,0:T(8,128)(2,1)S(1)} %get-tuple-element.31.refs_0_, bf16[320,1408]{1,0:T(8,128)(2,1)S(1)} %copy-done.7, bf16[320,1408]{1,0:T(8,128)(2,1)S(1)} %copy-done.8, bf16[320,1408]{1,0:T(8,128)(2,1)S(1)} %collective-permute-done.2.refs_3_, ...), custom_call_target="tpu_custom_call" | custom-call | flops 6920601600 | bytes 18022400 | tf_op jit(solution)/shard_map/pallas_call | solution.py:135
  50.3 4.0 %shard_map.31.refs_3_ = f32[640,1408]{1,0:T(8,128)S(1)} custom-call(bf16[2,640,1408]{2,1,0:T(8,128)(2,1)S(1)} %get-tuple-element.31.refs_0_, bf16[320,1408]{1,0:T(8,128)(2,1)S(1)} %collective-permute-done.9.refs_1_, bf16[320,1408]{1,0:T(8,128)(2,1)S(1)} %collective-permute-done.10.refs_2_, ...), custom_call_target="tpu_custom_call", output_to_operand_aliasing={{}: (3, {})} | custom-call | flops 1730150400 | bytes 12615680 | tf_op jit(solution)/shard_map/pallas_call | solution.py:135
  54.3 2.4 %collective-permute-done.13.refs_1_ = bf16[320,1408]{1,0:T(8,128)(2,1)S(1)} collective-permute-done((bf16[320,1408]{1,0:T(8,128)(2,1)S(1)}, bf16[320,1408]{1,0:T(8,128)(2,1)S(1)}, u32[]{:S(2)}, u32[]{:S(2)}) %collective-permute-start.13) | collective-permute-done | bytes 901152 | tf_op jit(solution)/shard_map/ppermute | solution.py:191
  58.9 4.0 %shard_map.32.refs_3_ = f32[640,1408]{1,0:T(8,128)S(1)} custom-call(bf16[2,640,1408]{2,1,0:T(8,128)(2,1)S(1)} %get-tuple-element.31.refs_0_, bf16[320,1408]{1,0:T(8,128)(2,1)S(1)} %collective-permute-done.1.refs_1_, bf16[320,1408]{1,0:T(8,128)(2,1)S(1)} %collective-permute-done.8.refs_2_, ...), custom_call_target="tpu_custom_call", output_to_operand_aliasing={{}: (3, {})} | custom-call | flops 1730150400 | bytes 12615680 | tf_op jit(solution)/shard_map/pallas_call | solution.py:135
  62.9 3.6 %collective-permute-done.7.refs_1_ = bf16[320,1408]{1,0:T(8,128)(2,1)S(1)} collective-permute-done((bf16[320,1408]{1,0:T(8,128)(2,1)S(1)}, bf16[320,1408]{1,0:T(8,128)(2,1)S(1)}, u32[]{:S(2)}, u32[]{:S(2)}) %collective-permute-start.7) | collective-permute-done | bytes 901152 | tf_op jit(solution)/shard_map/ppermute | solution.py:191
  68.5 4.0 %shard_map.33.refs_3_ = f32[640,1408]{1,0:T(8,128)S(1)} custom-call(bf16[2,640,1408]{2,1,0:T(8,128)(2,1)S(1)} %get-tuple-element.31.refs_0_, bf16[320,1408]{1,0:T(8,128)(2,1)S(1)} %collective-permute-done.13.refs_1_, bf16[320,1408]{1,0:T(8,128)(2,1)S(1)} %collective-permute-done.14.refs_2_, ...), custom_call_target="tpu_custom_call", output_to_operand_aliasing={{}: (3, {})} | custom-call | flops 1730150400 | bytes 12615680 | tf_op jit(solution)/shard_map/pallas_call | solution.py:135
  72.5 3.6 %collective-permute-done.17.refs_1_ = bf16[320,1408]{1,0:T(8,128)(2,1)S(1)} collective-permute-done((bf16[320,1408]{1,0:T(8,128)(2,1)S(1)}, bf16[320,1408]{1,0:T(8,128)(2,1)S(1)}, u32[]{:S(2)}, u32[]{:S(2)}) %collective-permute-start.17) | collective-permute-done | bytes 901152 | tf_op jit(solution)/shard_map/ppermute | solution.py:191
  78.2 4.0 %shard_map.34.refs_3_ = f32[640,1408]{1,0:T(8,128)S(1)} custom-call(bf16[2,640,1408]{2,1,0:T(8,128)(2,1)S(1)} %get-tuple-element.31.refs_0_, bf16[320,1408]{1,0:T(8,128)(2,1)S(1)} %collective-permute-done.7.refs_1_, bf16[320,1408]{1,0:T(8,128)(2,1)S(1)} %collective-permute-done.12.refs_2_, ...), custom_call_target="tpu_custom_call", output_to_operand_aliasing={{}: (3, {})} | custom-call | flops 1730150400 | bytes 12615680 | tf_op jit(solution)/shard_map/pallas_call | solution.py:135
  82.2 3.6 %collective-permute-done.11.refs_1_ = bf16[320,1408]{1,0:T(8,128)(2,1)S(1)} collective-permute-done((bf16[320,1408]{1,0:T(8,128)(2,1)S(1)}, bf16[320,1408]{1,0:T(8,128)(2,1)S(1)}, u32[]{:S(2)}, u32[]{:S(2)}) %collective-permute-start.11) | collective-permute-done | bytes 901152 | tf_op jit(solution)/shard_map/ppermute | solution.py:191
  87.8 4.0 %shard_map.35.refs_3_ = f32[640,1408]{1,0:T(8,128)S(1)} custom-call(bf16[2,640,1408]{2,1,0:T(8,128)(2,1)S(1)} %get-tuple-element.31.refs_0_, bf16[320,1408]{1,0:T(8,128)(2,1)S(1)} %collective-permute-done.17.refs_1_, bf16[320,1408]{1,0:T(8,128)(2,1)S(1)} %collective-permute-done.18.refs_2_, ...), custom_call_target="tpu_custom_call", output_to_operand_aliasing={{}: (3, {})} | custom-call | flops 1730150400 | bytes 12615680 | tf_op jit(solution)/shard_map/pallas_call | solution.py:135
  91.8 3.6 %collective-permute-done.21.refs_1_ = bf16[320,1408]{1,0:T(8,128)(2,1)S(1)} collective-permute-done((bf16[320,1408]{1,0:T(8,128)(2,1)S(1)}, bf16[320,1408]{1,0:T(8,128)(2,1)S(1)}, u32[]{:S(2)}, u32[]{:S(2)}) %collective-permute-start.21) | collective-permute-done | bytes 901152 | tf_op jit(solution)/shard_map/ppermute | solution.py:191
  97.5 4.0 %shard_map.36.refs_3_ = f32[640,1408]{1,0:T(8,128)S(1)} custom-call(bf16[2,640,1408]{2,1,0:T(8,128)(2,1)S(1)} %get-tuple-element.31.refs_0_, bf16[320,1408]{1,0:T(8,128)(2,1)S(1)} %collective-permute-done.11.refs_1_, bf16[320,1408]{1,0:T(8,128)(2,1)S(1)} %collective-permute-done.16.refs_2_, ...), custom_call_target="tpu_custom_call", output_to_operand_aliasing={{}: (3, {})} | custom-call | flops 1730150400 | bytes 12615680 | tf_op jit(solution)/shard_map/pallas_call | solution.py:135
  101.5 3.6 %collective-permute-done.15.refs_1_ = bf16[320,1408]{1,0:T(8,128)(2,1)S(1)} collective-permute-done((bf16[320,1408]{1,0:T(8,128)(2,1)S(1)}, bf16[320,1408]{1,0:T(8,128)(2,1)S(1)}, u32[]{:S(2)}, u32[]{:S(2)}) %collective-permute-start.15) | collective-permute-done | bytes 901152 | tf_op jit(solution)/shard_map/ppermute | solution.py:191
  107.1 4.0 %shard_map.37.refs_3_ = f32[640,1408]{1,0:T(8,128)S(1)} custom-call(bf16[2,640,1408]{2,1,0:T(8,128)(2,1)S(1)} %get-tuple-element.31.refs_0_, bf16[320,1408]{1,0:T(8,128)(2,1)S(1)} %collective-permute-done.21.refs_1_, bf16[320,1408]{1,0:T(8,128)(2,1)S(1)} %collective-permute-done.22.refs_2_, ...), custom_call_target="tpu_custom_call", output_to_operand_aliasing={{}: (3, {})} | custom-call | flops 1730150400 | bytes 12615680 | tf_op jit(solution)/shard_map/pallas_call | solution.py:135
  111.1 3.6 %collective-permute-done.24.refs_1_ = bf16[320,1408]{1,0:T(8,128)(2,1)S(1)} collective-permute-done((bf16[320,1408]{1,0:T(8,128)(2,1)S(1)}, bf16[320,1408]{1,0:T(8,128)(2,1)S(1)}, u32[]{:S(2)}, u32[]{:S(2)}) %collective-permute-start.24) | collective-permute-done | bytes 901152 | tf_op jit(solution)/shard_map/ppermute | solution.py:191
  114.7 4.0 %shard_map.38.refs_3_ = f32[640,1408]{1,0:T(8,128)S(1)} custom-call(bf16[2,640,1408]{2,1,0:T(8,128)(2,1)S(1)} %get-tuple-element.31.refs_0_, bf16[320,1408]{1,0:T(8,128)(2,1)S(1)} %collective-permute-done.15.refs_1_, bf16[320,1408]{1,0:T(8,128)(2,1)S(1)} %collective-permute-done.20.refs_2_, ...), custom_call_target="tpu_custom_call", output_to_operand_aliasing={{}: (3, {})} | custom-call | flops 1730150400 | bytes 12615680 | tf_op jit(solution)/shard_map/pallas_call | solution.py:135
  118.7 5.7 %collective-permute-done.19.refs_1_ = bf16[320,1408]{1,0:T(8,128)(2,1)S(1)} collective-permute-done((bf16[320,1408]{1,0:T(8,128)(2,1)S(1)}, bf16[320,1408]{1,0:T(8,128)(2,1)S(1)}, u32[]{:S(2)}, u32[]{:S(2)}) %collective-permute-start.19) | collective-permute-done | bytes 901152 | tf_op jit(solution)/shard_map/ppermute | solution.py:191
  129.9 4.0 %shard_map.39.refs_3_ = f32[640,1408]{1,0:T(8,128)S(1)} custom-call(bf16[2,640,1408]{2,1,0:T(8,128)(2,1)S(1)} %get-tuple-element.31.refs_0_, bf16[320,1408]{1,0:T(8,128)(2,1)S(1)} %collective-permute-done.24.refs_1_, bf16[320,1408]{1,0:T(8,128)(2,1)S(1)} %collective-permute-done.25.refs_2_, ...), custom_call_target="tpu_custom_call", output_to_operand_aliasing={{}: (3, {})} | custom-call | flops 1730150400 | bytes 12615680 | tf_op jit(solution)/shard_map/pallas_call | solution.py:135
  133.9 4.5 %shard_map.40 = bf16[640,1408]{1,0:T(8,128)(2,1)S(1)} custom-call(bf16[2,640,1408]{2,1,0:T(8,128)(2,1)S(1)} %get-tuple-element.31.refs_0_, bf16[320,1408]{1,0:T(8,128)(2,1)S(1)} %collective-permute-done.19.refs_1_, bf16[320,1408]{1,0:T(8,128)(2,1)S(1)} %collective-permute-done.23.refs_2_, f32[640,1408]{1,0:T(8,128)S(1)} %shard_map.39.refs_3_, ...), custom_call_target="tpu_custom_call" | custom-call | flops 1730150400 | bytes 12615680 | tf_op jit(solution)/shard_map/pallas_call | solution.py:135
  140.0 7.6 %collective-permute-done.30.refs_3_ = bf16[320,1408]{1,0:T(8,128)(2,1)S(1)} collective-permute-done((bf16[320,1408]{1,0:T(8,128)(2,1)S(1)}, bf16[320,1408]{1,0:T(8,128)(2,1)S(1)}, u32[]{:S(2)}, u32[]{:S(2)}) %collective-permute-start.30) | collective-permute-done | bytes 901152 | tf_op jit(solution)/shard_map/ppermute | solution.py:191
  147.6 9.7 %collective-permute-done.28.refs_1_ = bf16[320,1408]{1,0:T(8,128)(2,1)S(1)} collective-permute-done((bf16[320,1408]{1,0:T(8,128)(2,1)S(1)}, bf16[320,1408]{1,0:T(8,128)(2,1)S(1)}, u32[]{:S(2)}, u32[]{:S(2)}) %collective-permute-start.28) | collective-permute-done | bytes 901152 | tf_op jit(solution)/shard_map/ppermute | solution.py:191
  159.7 7.3 %shard_map.41.refs_3_ = f32[640,1408]{1,0:T(8,128)S(1)} custom-call(bf16[2,640,1408]{2,1,0:T(8,128)(2,1)S(1)} %get-tuple-element.31.refs_0_, bf16[320,1408]{1,0:T(8,128)(2,1)S(1)} %collective-permute-done.28.refs_1_, bf16[320,1408]{1,0:T(8,128)(2,1)S(1)} %collective-permute-done.29.refs_2_, bf16[320,1408]{1,0:T(8,128)(2,1)S(1)} %collective-permute-done.30.refs_3_, ...), custom_call_target="tpu_custom_call" | custom-call | flops 5190451200 | bytes 16220160 | tf_op jit(solution)/shard_map/pallas_call | solution.py:135
  170.5 8.9 %collective-permute-done.26 = bf16[640,1408]{1,0:T(8,128)(2,1)S(1)} collective-permute-done((bf16[640,1408]{1,0:T(8,128)(2,1)S(1)}, bf16[640,1408]{1,0:T(8,128)(2,1)S(1)}, u32[]{:S(2)}, u32[]{:S(2)}) %collective-permute-start.26) | collective-permute-done | bytes 1802272 | tf_op jit(solution)/shard_map/ppermute | solution.py:213
  180.9 2.4 %collective-permute-done.34.refs_2_ = bf16[320,1408]{1,0:T(8,128)(2,1)} collective-permute-done((bf16[320,1408]{1,0:T(8,128)(2,1)S(1)}, bf16[320,1408]{1,0:T(8,128)(2,1)}, u32[]{:S(2)}, u32[]{:S(2)}) %collective-permute-start.34) | collective-permute-done | bytes 901152 | tf_op jit(solution)/shard_map/ppermute | solution.py:191
  189.3 5.7 %shard_map.42 = f32[640,1408]{1,0:T(8,128)S(1)} custom-call(bf16[2,640,1408]{2,1,0:T(8,128)(2,1)S(1)} %copy-done.1, bf16[320,1408]{1,0:T(8,128)(2,1)S(1)} %collective-permute-done.27.refs_1_, bf16[320,1408]{1,0:T(8,128)(2,1)} %collective-permute-done.34.refs_2_, f32[640,1408]{1,0:T(8,128)S(1)} %copy-done.6, ...), custom_call_target="tpu_custom_call", output_to_operand_aliasing={{}: (3, {})} | custom-call | flops 1730150400 | bytes 12615680 | tf_op jit(solution)/shard_map/pallas_call | solution.py:135
  195.1 2.4 %add_multiply_fusion = f32[640,1408]{1,0:T(8,128)} fusion(f32[640,1408]{1,0:T(8,128)S(1)} %shard_map.42, bf16[640,1408]{1,0:T(8,128)(2,1)S(1)} %copy-done.10, bf16[640,1408]{1,0:T(8,128)(2,1)S(1)} %shard_map.40, f32[640]{0:T(1024)S(1)} %reduce), kind=kLoop, calls=%fused_computation | loop fusion | flops 4505600 | bytes 10816000 | tf_op jit(solution)/shard_map/mul | solution.py:230
  (78 shorter events, 44.2 us)
Async XLA Ops:
  3.8 14.4 %collective-permute-start.4 = (bf16[320,1408]{1,0:T(8,128)(2,1)}, bf16[320,1408]{1,0:T(8,128)(2,1)S(1)}, u32[]{:S(2)}, u32[]{:S(2)}) collective-permute-start(bf16[320,1408]{1,0:T(8,128)(2,1)} %get-tuple-element.27.refs_1_), channel_id=1, source_target_pairs={{0,8},{10,2},{8,16},{18,10},{16,24},{26,18},{24,28},{30,26},{28,20... | collective-permute-start | bytes 2703368 | tf_op jit(solution)/shard_map/ppermute | solution.py:191
  6.8 21.0 %collective-permute-start = (bf16[320,1408]{1,0:T(8,128)(2,1)}, bf16[320,1408]{1,0:T(8,128)(2,1)S(1)}, u32[]{:S(2)}, u32[]{:S(2)}) collective-permute-start(bf16[320,1408]{1,0:T(8,128)(2,1)} %get-tuple-element.28.refs_2_), channel_id=1, source_target_pairs={{0,8},{10,2},{8,16},{18,10},{16,24},{26,18},{24,28},{30,26},{28,20... | collective-permute-start | bytes 2703368 | tf_op jit(solution)/shard_map/ppermute | solution.py:191
  8.4 19.4 %collective-permute-start.2 = (bf16[320,1408]{1,0:T(8,128)(2,1)}, bf16[320,1408]{1,0:T(8,128)(2,1)S(1)}, u32[]{:S(2)}, u32[]{:S(2)}) collective-permute-start(bf16[320,1408]{1,0:T(8,128)(2,1)} %get-tuple-element.27.refs_1_), channel_id=1, source_target_pairs={{0,2},{2,0},{4,6},{6,4},{8,10},{10,8},{12,14},{14,12},{16,18},{18,... | collective-permute-start | bytes 2703368 | tf_op jit(solution)/shard_map/ppermute | solution.py:191
  18.1 19.3 %collective-permute-start.9 = (bf16[320,1408]{1,0:T(8,128)(2,1)S(1)}, bf16[320,1408]{1,0:T(8,128)(2,1)S(1)}, u32[]{:S(2)}, u32[]{:S(2)}) collective-permute-start(bf16[320,1408]{1,0:T(8,128)(2,1)S(1)} %collective-permute-done.4.refs_5_), channel_id=1, source_target_pairs={{0,8},{10,2},{8,16},{18,10},{16,24},{26,18},{24,28},{30,26},{28,20... | collective-permute-start | bytes 2703368 | tf_op jit(solution)/shard_map/ppermute | solution.py:191
  20.2 17.2 %collective-permute-start.3 = (bf16[320,1408]{1,0:T(8,128)(2,1)}, bf16[320,1408]{1,0:T(8,128)(2,1)S(1)}, u32[]{:S(2)}, u32[]{:S(2)}) collective-permute-start(bf16[320,1408]{1,0:T(8,128)(2,1)} %get-tuple-element.28.refs_2_), channel_id=1, source_target_pairs={{0,2},{2,0},{4,6},{6,4},{8,10},{10,8},{12,14},{14,12},{16,18},{18,... | collective-permute-start | bytes 2703368 | tf_op jit(solution)/shard_map/ppermute | solution.py:191
  20.2 19.3 %collective-permute-start.5 = (bf16[320,1408]{1,0:T(8,128)(2,1)S(1)}, bf16[320,1408]{1,0:T(8,128)(2,1)S(1)}, u32[]{:S(2)}, u32[]{:S(2)}) collective-permute-start(bf16[320,1408]{1,0:T(8,128)(2,1)S(1)} %collective-permute-done.4.refs_5_), channel_id=1, source_target_pairs={{0,2},{2,0},{4,6},{6,4},{8,10},{10,8},{12,14},{14,12},{16,18},{18,... | collective-permute-start | bytes 2703368 | tf_op jit(solution)/shard_map/ppermute | solution.py:191
  27.8 11.7 %collective-permute-start.6 = (bf16[320,1408]{1,0:T(8,128)(2,1)S(1)}, bf16[320,1408]{1,0:T(8,128)(2,1)S(1)}, u32[]{:S(2)}, u32[]{:S(2)}) collective-permute-start(bf16[320,1408]{1,0:T(8,128)(2,1)S(1)} %collective-permute-done.refs_7_), channel_id=1, source_target_pairs={{0,2},{2,0},{4,6},{6,4},{8,10},{10,8},{12,14},{14,12},{16,18},{18,... | collective-permute-start | bytes 2703368 | tf_op jit(solution)/shard_map/ppermute | solution.py:191
  27.8 20.8 %collective-permute-start.1 = (bf16[320,1408]{1,0:T(8,128)(2,1)S(1)}, bf16[320,1408]{1,0:T(8,128)(2,1)S(1)}, u32[]{:S(2)}, u32[]{:S(2)}) collective-permute-start(bf16[320,1408]{1,0:T(8,128)(2,1)S(1)} %collective-permute-done.refs_7_), channel_id=1, source_target_pairs={{0,8},{10,2},{8,16},{18,10},{16,24},{26,18},{24,28},{30,26},{28,20... | collective-permute-start | bytes 2703368 | tf_op jit(solution)/shard_map/ppermute | solution.py:191
  37.5 12.9 %collective-permute-start.10 = (bf16[320,1408]{1,0:T(8,128)(2,1)S(1)}, bf16[320,1408]{1,0:T(8,128)(2,1)S(1)}, u32[]{:S(2)}, u32[]{:S(2)}) collective-permute-start(bf16[320,1408]{1,0:T(8,128)(2,1)S(1)} %collective-permute-done.9.refs_1_), channel_id=1, source_target_pairs={{0,2},{2,0},{4,6},{6,4},{8,10},{10,8},{12,14},{14,12},{16,18},{18,... | collective-permute-start | bytes 2703368 | tf_op jit(solution)/shard_map/ppermute | solution.py:191
  37.5 19.3 %collective-permute-start.13 = (bf16[320,1408]{1,0:T(8,128)(2,1)S(1)}, bf16[320,1408]{1,0:T(8,128)(2,1)S(1)}, u32[]{:S(2)}, u32[]{:S(2)}) collective-permute-start(bf16[320,1408]{1,0:T(8,128)(2,1)S(1)} %collective-permute-done.9.refs_1_), channel_id=1, source_target_pairs={{0,8},{10,2},{8,16},{18,10},{16,24},{26,18},{24,28},{30,26},{28,20... | collective-permute-start | bytes 2703368 | tf_op jit(solution)/shard_map/ppermute | solution.py:191
  48.6 10.2 %collective-permute-start.8 = (bf16[320,1408]{1,0:T(8,128)(2,1)S(1)}, bf16[320,1408]{1,0:T(8,128)(2,1)S(1)}, u32[]{:S(2)}, u32[]{:S(2)}) collective-permute-start(bf16[320,1408]{1,0:T(8,128)(2,1)S(1)} %collective-permute-done.1.refs_1_), channel_id=1, source_target_pairs={{0,2},{2,0},{4,6},{6,4},{8,10},{10,8},{12,14},{14,12},{16,18},{18,... | collective-permute-start | bytes 2703368 | tf_op jit(solution)/shard_map/ppermute | solution.py:191
  48.9 17.6 %collective-permute-start.7 = (bf16[320,1408]{1,0:T(8,128)(2,1)S(1)}, bf16[320,1408]{1,0:T(8,128)(2,1)S(1)}, u32[]{:S(2)}, u32[]{:S(2)}) collective-permute-start(bf16[320,1408]{1,0:T(8,128)(2,1)S(1)} %collective-permute-done.1.refs_1_), channel_id=1, source_target_pairs={{0,8},{10,2},{8,16},{18,10},{16,24},{26,18},{24,28},{30,26},{28,20... | collective-permute-start | bytes 2703368 | tf_op jit(solution)/shard_map/ppermute | solution.py:191
  56.8 11.7 %collective-permute-start.14 = (bf16[320,1408]{1,0:T(8,128)(2,1)S(1)}, bf16[320,1408]{1,0:T(8,128)(2,1)S(1)}, u32[]{:S(2)}, u32[]{:S(2)}) collective-permute-start(bf16[320,1408]{1,0:T(8,128)(2,1)S(1)} %collective-permute-done.13.refs_1_), channel_id=1, source_target_pairs={{0,2},{2,0},{4,6},{6,4},{8,10},{10,8},{12,14},{14,12},{16,18},{18,... | collective-permute-start | bytes 2703368 | tf_op jit(solution)/shard_map/ppermute | solution.py:191
  56.8 19.3 %collective-permute-start.17 = (bf16[320,1408]{1,0:T(8,128)(2,1)S(1)}, bf16[320,1408]{1,0:T(8,128)(2,1)S(1)}, u32[]{:S(2)}, u32[]{:S(2)}) collective-permute-start(bf16[320,1408]{1,0:T(8,128)(2,1)S(1)} %collective-permute-done.13.refs_1_), channel_id=1, source_target_pairs={{0,8},{10,2},{8,16},{18,10},{16,24},{26,18},{24,28},{30,26},{28,20... | collective-permute-start | bytes 2703368 | tf_op jit(solution)/shard_map/ppermute | solution.py:191
  66.4 11.7 %collective-permute-start.12 = (bf16[320,1408]{1,0:T(8,128)(2,1)S(1)}, bf16[320,1408]{1,0:T(8,128)(2,1)S(1)}, u32[]{:S(2)}, u32[]{:S(2)}) collective-permute-start(bf16[320,1408]{1,0:T(8,128)(2,1)S(1)} %collective-permute-done.7.refs_1_), channel_id=1, source_target_pairs={{0,2},{2,0},{4,6},{6,4},{8,10},{10,8},{12,14},{14,12},{16,18},{18,... | collective-permute-start | bytes 2703368 | tf_op jit(solution)/shard_map/ppermute | solution.py:191
  66.4 19.3 %collective-permute-start.11 = (bf16[320,1408]{1,0:T(8,128)(2,1)S(1)}, bf16[320,1408]{1,0:T(8,128)(2,1)S(1)}, u32[]{:S(2)}, u32[]{:S(2)}) collective-permute-start(bf16[320,1408]{1,0:T(8,128)(2,1)S(1)} %collective-permute-done.7.refs_1_), channel_id=1, source_target_pairs={{0,8},{10,2},{8,16},{18,10},{16,24},{26,18},{24,28},{30,26},{28,20... | collective-permute-start | bytes 2703368 | tf_op jit(solution)/shard_map/ppermute | solution.py:191
  76.1 11.7 %collective-permute-start.18 = (bf16[320,1408]{1,0:T(8,128)(2,1)S(1)}, bf16[320,1408]{1,0:T(8,128)(2,1)S(1)}, u32[]{:S(2)}, u32[]{:S(2)}) collective-permute-start(bf16[320,1408]{1,0:T(8,128)(2,1)S(1)} %collective-permute-done.17.refs_1_), channel_id=1, source_target_pairs={{0,2},{2,0},{4,6},{6,4},{8,10},{10,8},{12,14},{14,12},{16,18},{18,... | collective-permute-start | bytes 2703368 | tf_op jit(solution)/shard_map/ppermute | solution.py:191
  76.1 19.3 %collective-permute-start.21 = (bf16[320,1408]{1,0:T(8,128)(2,1)S(1)}, bf16[320,1408]{1,0:T(8,128)(2,1)S(1)}, u32[]{:S(2)}, u32[]{:S(2)}) collective-permute-start(bf16[320,1408]{1,0:T(8,128)(2,1)S(1)} %collective-permute-done.17.refs_1_), channel_id=1, source_target_pairs={{0,8},{10,2},{8,16},{18,10},{16,24},{26,18},{24,28},{30,26},{28,20... | collective-permute-start | bytes 2703368 | tf_op jit(solution)/shard_map/ppermute | solution.py:191
  85.7 11.7 %collective-permute-start.16 = (bf16[320,1408]{1,0:T(8,128)(2,1)S(1)}, bf16[320,1408]{1,0:T(8,128)(2,1)S(1)}, u32[]{:S(2)}, u32[]{:S(2)}) collective-permute-start(bf16[320,1408]{1,0:T(8,128)(2,1)S(1)} %collective-permute-done.11.refs_1_), channel_id=1, source_target_pairs={{0,2},{2,0},{4,6},{6,4},{8,10},{10,8},{12,14},{14,12},{16,18},{18,... | collective-permute-start | bytes 2703368 | tf_op jit(solution)/shard_map/ppermute | solution.py:191
  85.7 19.3 %collective-permute-start.15 = (bf16[320,1408]{1,0:T(8,128)(2,1)S(1)}, bf16[320,1408]{1,0:T(8,128)(2,1)S(1)}, u32[]{:S(2)}, u32[]{:S(2)}) collective-permute-start(bf16[320,1408]{1,0:T(8,128)(2,1)S(1)} %collective-permute-done.11.refs_1_), channel_id=1, source_target_pairs={{0,8},{10,2},{8,16},{18,10},{16,24},{26,18},{24,28},{30,26},{28,20... | collective-permute-start | bytes 2703368 | tf_op jit(solution)/shard_map/ppermute | solution.py:191
  95.4 11.7 %collective-permute-start.22 = (bf16[320,1408]{1,0:T(8,128)(2,1)S(1)}, bf16[320,1408]{1,0:T(8,128)(2,1)S(1)}, u32[]{:S(2)}, u32[]{:S(2)}) collective-permute-start(bf16[320,1408]{1,0:T(8,128)(2,1)S(1)} %collective-permute-done.21.refs_1_), channel_id=1, source_target_pairs={{0,2},{2,0},{4,6},{6,4},{8,10},{10,8},{12,14},{14,12},{16,18},{18,... | collective-permute-start | bytes 2703368 | tf_op jit(solution)/shard_map/ppermute | solution.py:191
  95.4 19.3 %collective-permute-start.24 = (bf16[320,1408]{1,0:T(8,128)(2,1)S(1)}, bf16[320,1408]{1,0:T(8,128)(2,1)S(1)}, u32[]{:S(2)}, u32[]{:S(2)}) collective-permute-start(bf16[320,1408]{1,0:T(8,128)(2,1)S(1)} %collective-permute-done.21.refs_1_), channel_id=1, source_target_pairs={{0,8},{10,2},{8,16},{18,10},{16,24},{26,18},{24,28},{30,26},{28,20... | collective-permute-start | bytes 2703368 | tf_op jit(solution)/shard_map/ppermute | solution.py:191
  105.0 9.7 %collective-permute-start.20 = (bf16[320,1408]{1,0:T(8,128)(2,1)S(1)}, bf16[320,1408]{1,0:T(8,128)(2,1)S(1)}, u32[]{:S(2)}, u32[]{:S(2)}) collective-permute-start(bf16[320,1408]{1,0:T(8,128)(2,1)S(1)} %collective-permute-done.15.refs_1_), channel_id=1, source_target_pairs={{0,2},{2,0},{4,6},{6,4},{8,10},{10,8},{12,14},{14,12},{16,18},{18,... | collective-permute-start | bytes 2703368 | tf_op jit(solution)/shard_map/ppermute | solution.py:191
  105.0 19.3 %collective-permute-start.19 = (bf16[320,1408]{1,0:T(8,128)(2,1)S(1)}, bf16[320,1408]{1,0:T(8,128)(2,1)S(1)}, u32[]{:S(2)}, u32[]{:S(2)}) collective-permute-start(bf16[320,1408]{1,0:T(8,128)(2,1)S(1)} %collective-permute-done.15.refs_1_), channel_id=1, source_target_pairs={{0,8},{10,2},{8,16},{18,10},{16,24},{26,18},{24,28},{30,26},{28,20... | collective-permute-start | bytes 2703368 | tf_op jit(solution)/shard_map/ppermute | solution.py:191
  114.7 15.2 %collective-permute-start.25 = (bf16[320,1408]{1,0:T(8,128)(2,1)S(1)}, bf16[320,1408]{1,0:T(8,128)(2,1)S(1)}, u32[]{:S(2)}, u32[]{:S(2)}) collective-permute-start(bf16[320,1408]{1,0:T(8,128)(2,1)S(1)} %collective-permute-done.24.refs_1_), channel_id=1, source_target_pairs={{0,2},{2,0},{4,6},{6,4},{8,10},{10,8},{12,14},{14,12},{16,18},{18,... | collective-permute-start | bytes 2703368 | tf_op jit(solution)/shard_map/ppermute | solution.py:191
  124.6 15.3 %collective-permute-start.32 = (bf16[320,1408]{1,0:T(8,128)(2,1)S(1)}, bf16[320,1408]{1,0:T(8,128)(2,1)S(1)}, u32[]{:S(2)}, u32[]{:S(2)}) collective-permute-start(bf16[320,1408]{1,0:T(8,128)(2,1)S(1)} %bitcast.8), channel_id=1, source_target_pairs={{8,0},{2,10},{16,8},{10,18},{24,16},{18,26},{28,24},{26,30},{20,28... | collective-permute-start | bytes 2703368 | tf_op jit(solution)/shard_map/ppermute | solution.py:191
  126.7 20.9 %collective-permute-start.30 = (bf16[320,1408]{1,0:T(8,128)(2,1)S(1)}, bf16[320,1408]{1,0:T(8,128)(2,1)S(1)}, u32[]{:S(2)}, u32[]{:S(2)}) collective-permute-start(bf16[320,1408]{1,0:T(8,128)(2,1)S(1)} %bitcast.7), channel_id=1, source_target_pairs={{8,0},{2,10},{16,8},{10,18},{24,16},{18,26},{28,24},{26,30},{20,28... | collective-permute-start | bytes 2703368 | tf_op jit(solution)/shard_map/ppermute | solution.py:191
  128.3 29.0 %collective-permute-start.28 = (bf16[320,1408]{1,0:T(8,128)(2,1)S(1)}, bf16[320,1408]{1,0:T(8,128)(2,1)S(1)}, u32[]{:S(2)}, u32[]{:S(2)}) collective-permute-start(bf16[320,1408]{1,0:T(8,128)(2,1)S(1)} %bitcast.6), channel_id=1, source_target_pairs={{8,0},{2,10},{16,8},{10,18},{24,16},{18,26},{28,24},{26,30},{20,28... | collective-permute-start | bytes 2703368 | tf_op jit(solution)/shard_map/ppermute | solution.py:191
  138.4 41.0 %collective-permute-start.26 = (bf16[640,1408]{1,0:T(8,128)(2,1)S(1)}, bf16[640,1408]{1,0:T(8,128)(2,1)S(1)}, u32[]{:S(2)}, u32[]{:S(2)}) collective-permute-start(bf16[640,1408]{1,0:T(8,128)(2,1)S(1)} %shard_map.40), channel_id=1, source_target_pairs={{0,1},{1,0},{2,3},{3,2},{4,5},{5,4},{6,7},{7,6},{8,9},{9,8},{10,11... | collective-permute-start | bytes 5406728 | tf_op jit(solution)/shard_map/ppermute | solution.py:213
  140.0 19.3 %collective-permute-start.33 = (bf16[320,1408]{1,0:T(8,128)(2,1)S(1)}, bf16[320,1408]{1,0:T(8,128)(2,1)S(1)}, u32[]{:S(2)}, u32[]{:S(2)}) collective-permute-start(bf16[320,1408]{1,0:T(8,128)(2,1)S(1)} %collective-permute-done.32.refs_5_), channel_id=1, source_target_pairs={{0,2},{2,0},{4,6},{6,4},{8,10},{10,8},{12,14},{14,12},{16,18},{18,... | collective-permute-start | bytes 2703368 | tf_op jit(solution)/shard_map/ppermute | solution.py:191
  147.6 11.6 %collective-permute-start.31 = (bf16[320,1408]{1,0:T(8,128)(2,1)S(1)}, bf16[320,1408]{1,0:T(8,128)(2,1)S(1)}, u32[]{:S(2)}, u32[]{:S(2)}) collective-permute-start(bf16[320,1408]{1,0:T(8,128)(2,1)S(1)} %collective-permute-done.30.refs_3_), channel_id=1, source_target_pairs={{0,2},{2,0},{4,6},{6,4},{8,10},{10,8},{12,14},{14,12},{16,18},{18,... | collective-permute-start | bytes 2703368 | tf_op jit(solution)/shard_map/ppermute | solution.py:191
  157.3 13.2 %collective-permute-start.27 = (bf16[320,1408]{1,0:T(8,128)(2,1)S(1)}, bf16[320,1408]{1,0:T(8,128)(2,1)S(1)}, u32[]{:S(2)}, u32[]{:S(2)}) collective-permute-start(bf16[320,1408]{1,0:T(8,128)(2,1)S(1)} %bitcast.5), channel_id=1, source_target_pairs={{8,0},{2,10},{16,8},{10,18},{24,16},{18,26},{28,24},{26,30},{20,28... | collective-permute-start | bytes 2703368 | tf_op jit(solution)/shard_map/ppermute | solution.py:191
  (14 other events, 203.1 us)

commit v3 on v2

--- a/solution.py
+++ b/solution.py
@@ -200,13 +200,13 @@
         if event >= FIRST:
             totals.append(add(batch, totals[-1] if totals else None))
             batch = []
-        batch += [held[k], move(held[k], swap, *totals[len(totals) - 1 - SLAG :][:1] if len(totals) > SLAG else [])]
+        slag = SLAG
+        batch += [held[k], move(held[k], swap, *totals[len(totals) - 1 - slag :][:1] if len(totals) > slag else [])]
     if not doubled:
         nearest = [move(x, reverse) for x in pieces]
         batch += nearest + [move(x, swap) for x in nearest]
     own = add(batch, totals[-1], project=(student, s_scale), dtype=jnp.bfloat16)
-    distance = 1
-    summands = (own,)
+    summands, distance = (own,), 1
     while distance < pair_count:
         value = sum(x.astype(jnp.float32) for x in summands).astype(jnp.bfloat16)
         route = [(i, i ^ distance) for i in range(pair_count)]
@@ -216,16 +216,16 @@
     if not doubled:
         return s_scale * summed
 
-    total, at, batch = None, 0, []
-    nearest = []
+    nearest, at = [], 0
     for k, n in enumerate(split(rows, PARTS)):
-        part = own_half[:, at : at + n].reshape(2 * n, width)
-        nearest.append(move(part, reverse, *([own] if k == PARTS - 1 else [held[k % CHAINS]])))
+        piece = own_half[:, at : at + n].reshape(2 * n, width)
+        nearest.append(move(piece, reverse, own if k else held[0]))
         at += n
+    batch = []
     for x in nearest[:-1]:
         batch += [x, move(x, swap, own)]
     total = add(batch, None)
-    batch = [nearest[-1], move(nearest[-1], swap, total, summands[-1])]
+    batch = [nearest[-1], move(nearest[-1], swap)]
     total = add(batch, total, project=(student, s_scale))
     return s_scale * (summed + total)
 

time: 198 us -> 190 us (0.960)
  local copies, waits for them, and re-layouts: 11.4 us -> 4.33 us
  waiting for transfers between devices: 81.4 us -> 77 us
  Pallas kernels: 67.5 us -> 70 us
    ppermute x1, waiting for transfers between devices: 8.93 us -> 0.01 us  [local(): summands = (value, lax.ppermute(value, 'pair', route))]
    unnamed x22 -> x16, local copies, waits for them, and re-layouts: 11.1 us -> 4.06 us
    ppermute x34, waiting for transfers between devices: 72.5 us -> 77 us  [move(): return lax.ppermute(after(x, *wait_for), 'seq', route)]
    pallas_call x13, Pallas kernels: 62.5 us -> 65 us  [add_relation(): pl.pallas_call(functools.partial(relation_kernel, margin, weight, counts,...]
  transfers between devices with their start and end apart: 35 -> 35, of which waited for: 17 -> 14; matrix products, arithmetic and copies ran while one was open for 0% -> 0% of each run, Pallas kernels for 29% -> 35%
where the time goes in v3:
time: 190 us
  waiting for transfers between devices  77 us (41%)
  Pallas kernels  70 us (37%)
  starting transfers between devices  34.1 us (18%)
  local copies, waits for them, and re-layouts  4.33 us (2%)
  other arithmetic  4.08 us (2%)
    ppermute x34, waiting for transfers between devices, move(): return lax.ppermute(after(x, *wait_for), 'seq', route)  77 us
    pallas_call x13, Pallas kernels, add_relation(): pl.pallas_call(functools.partial(relation_kernel, margin, weight, counts,...  65 us
    ppermute x34, starting transfers between devices, move(): return lax.ppermute(after(x, *wait_for), 'seq', route)  32.7 us
    unnamed x16, local copies, waits for them, and re-layouts  4.06 us
    mul x1, other arithmetic, local(): return s_scale * (summed + total)  3.91 us
  transfers between devices with their start and end apart: 35, of which 14 were waited for; matrix products, arithmetic and copies ran while one was open for 0% of the time, Pallas kernels for 35%

profile of v3, /device:TPU:0, one launch (start us, length us, event | category | flops | bytes accessed | tf_op | source)
XLA Modules:
  0.0 189.8 jit_solution(17238634283600526906)
XLA Ops:
  0.0 3.8 %shard_map.28 = (bf16[320,1408]{1,0:T(8,128)(2,1)}, bf16[320,1408]{1,0:T(8,128)(2,1)}) custom-call(s32[1]{0:T(128)} %bitcast.which, f32[640,1408]{1,0:T(8,128)} %refs_4_.3, f32[640,1408]{1,0:T(8,128)} %teacher.3), custom_call_target="tpu_custom_call" | custom-call | flops 2703360 | bytes 5406720 | tf_op jit(solution)/shard_map/pallas_call | solution.py:68
  3.8 3.0 %collective-permute-start.4 = (bf16[320,1408]{1,0:T(8,128)(2,1)}, bf16[320,1408]{1,0:T(8,128)(2,1)S(1)}, u32[]{:S(2)}, u32[]{:S(2)}) collective-permute-start(bf16[320,1408]{1,0:T(8,128)(2,1)} %get-tuple-element.26.refs_1_), channel_id=1, source_target_pairs={{0,8},{10,2},{8,16},{18,10},{16,24},{26,18},{24,28},{30,26},{28,20... | collective-permute-start | bytes 2703368 | tf_op jit(solution)/shard_map/ppermute | solution.py:191
  8.4 9.8 %collective-permute-done.4.refs_5_ = bf16[320,1408]{1,0:T(8,128)(2,1)S(1)} collective-permute-done((bf16[320,1408]{1,0:T(8,128)(2,1)}, bf16[320,1408]{1,0:T(8,128)(2,1)S(1)}, u32[]{:S(2)}, u32[]{:S(2)}) %collective-permute-start.4) | collective-permute-done | bytes 901152 | tf_op jit(solution)/shard_map/ppermute | solution.py:191
  20.7 7.1 %collective-permute-done.refs_7_ = bf16[320,1408]{1,0:T(8,128)(2,1)S(1)} collective-permute-done((bf16[320,1408]{1,0:T(8,128)(2,1)}, bf16[320,1408]{1,0:T(8,128)(2,1)S(1)}, u32[]{:S(2)}, u32[]{:S(2)}) %collective-permute-start) | collective-permute-done | bytes 901152 | tf_op jit(solution)/shard_map/ppermute | solution.py:191
  27.8 2.1 %collective-permute-start.1 = (bf16[320,1408]{1,0:T(8,128)(2,1)S(1)}, bf16[320,1408]{1,0:T(8,128)(2,1)S(1)}, u32[]{:S(2)}, u32[]{:S(2)}) collective-permute-start(bf16[320,1408]{1,0:T(8,128)(2,1)S(1)} %collective-permute-done.refs_7_), channel_id=1, source_target_pairs={{0,8},{10,2},{8,16},{18,10},{16,24},{26,18},{24,28},{30,26},{28,20... | collective-permute-start | bytes 2703368 | tf_op jit(solution)/shard_map/ppermute | solution.py:191
  33.1 4.3 %collective-permute-done.9.refs_1_ = bf16[320,1408]{1,0:T(8,128)(2,1)S(1)} collective-permute-done((bf16[320,1408]{1,0:T(8,128)(2,1)S(1)}, bf16[320,1408]{1,0:T(8,128)(2,1)S(1)}, u32[]{:S(2)}, u32[]{:S(2)}) %collective-permute-start.9) | collective-permute-done | bytes 901152 | tf_op jit(solution)/shard_map/ppermute | solution.py:191
  39.6 9.0 %shard_map.30.refs_3_ = f32[640,1408]{1,0:T(8,128)S(1)} custom-call(bf16[2,640,1408]{2,1,0:T(8,128)(2,1)S(1)} %get-tuple-element.30.refs_0_, bf16[320,1408]{1,0:T(8,128)(2,1)S(1)} %copy-done.6, bf16[320,1408]{1,0:T(8,128)(2,1)S(1)} %copy-done.7, bf16[320,1408]{1,0:T(8,128)(2,1)S(1)} %collective-permute-done.2.refs_3_, ...), custom_call_target="tpu_custom_call" | custom-call | flops 6920601600 | bytes 18022400 | tf_op jit(solution)/shard_map/pallas_call | solution.py:135
  50.3 4.0 %shard_map.31.refs_3_ = f32[640,1408]{1,0:T(8,128)S(1)} custom-call(bf16[2,640,1408]{2,1,0:T(8,128)(2,1)S(1)} %get-tuple-element.30.refs_0_, bf16[320,1408]{1,0:T(8,128)(2,1)S(1)} %collective-permute-done.9.refs_1_, bf16[320,1408]{1,0:T(8,128)(2,1)S(1)} %collective-permute-done.10.refs_2_, ...), custom_call_target="tpu_custom_call", output_to_operand_aliasing={{}: (3, {})} | custom-call | flops 1730150400 | bytes 12615680 | tf_op jit(solution)/shard_map/pallas_call | solution.py:135
  54.3 2.4 %collective-permute-done.13.refs_1_ = bf16[320,1408]{1,0:T(8,128)(2,1)S(1)} collective-permute-done((bf16[320,1408]{1,0:T(8,128)(2,1)S(1)}, bf16[320,1408]{1,0:T(8,128)(2,1)S(1)}, u32[]{:S(2)}, u32[]{:S(2)}) %collective-permute-start.13) | collective-permute-done | bytes 901152 | tf_op jit(solution)/shard_map/ppermute | solution.py:191
  58.8 4.0 %shard_map.32.refs_3_ = f32[640,1408]{1,0:T(8,128)S(1)} custom-call(bf16[2,640,1408]{2,1,0:T(8,128)(2,1)S(1)} %get-tuple-element.30.refs_0_, bf16[320,1408]{1,0:T(8,128)(2,1)S(1)} %collective-permute-done.1.refs_1_, bf16[320,1408]{1,0:T(8,128)(2,1)S(1)} %collective-permute-done.8.refs_2_, ...), custom_call_target="tpu_custom_call", output_to_operand_aliasing={{}: (3, {})} | custom-call | flops 1730150400 | bytes 12615680 | tf_op jit(solution)/shard_map/pallas_call | solution.py:135
  62.8 3.6 %collective-permute-done.7.refs_1_ = bf16[320,1408]{1,0:T(8,128)(2,1)S(1)} collective-permute-done((bf16[320,1408]{1,0:T(8,128)(2,1)S(1)}, bf16[320,1408]{1,0:T(8,128)(2,1)S(1)}, u32[]{:S(2)}, u32[]{:S(2)}) %collective-permute-start.7) | collective-permute-done | bytes 901152 | tf_op jit(solution)/shard_map/ppermute | solution.py:191
  68.5 4.0 %shard_map.33.refs_3_ = f32[640,1408]{1,0:T(8,128)S(1)} custom-call(bf16[2,640,1408]{2,1,0:T(8,128)(2,1)S(1)} %get-tuple-element.30.refs_0_, bf16[320,1408]{1,0:T(8,128)(2,1)S(1)} %collective-permute-done.13.refs_1_, bf16[320,1408]{1,0:T(8,128)(2,1)S(1)} %collective-permute-done.14.refs_2_, ...), custom_call_target="tpu_custom_call", output_to_operand_aliasing={{}: (3, {})} | custom-call | flops 1730150400 | bytes 12615680 | tf_op jit(solution)/shard_map/pallas_call | solution.py:135
  72.5 3.6 %collective-permute-done.17.refs_1_ = bf16[320,1408]{1,0:T(8,128)(2,1)S(1)} collective-permute-done((bf16[320,1408]{1,0:T(8,128)(2,1)S(1)}, bf16[320,1408]{1,0:T(8,128)(2,1)S(1)}, u32[]{:S(2)}, u32[]{:S(2)}) %collective-permute-start.17) | collective-permute-done | bytes 901152 | tf_op jit(solution)/shard_map/ppermute | solution.py:191
  78.2 4.0 %shard_map.34.refs_3_ = f32[640,1408]{1,0:T(8,128)S(1)} custom-call(bf16[2,640,1408]{2,1,0:T(8,128)(2,1)S(1)} %get-tuple-element.30.refs_0_, bf16[320,1408]{1,0:T(8,128)(2,1)S(1)} %collective-permute-done.7.refs_1_, bf16[320,1408]{1,0:T(8,128)(2,1)S(1)} %collective-permute-done.12.refs_2_, ...), custom_call_target="tpu_custom_call", output_to_operand_aliasing={{}: (3, {})} | custom-call | flops 1730150400 | bytes 12615680 | tf_op jit(solution)/shard_map/pallas_call | solution.py:135
  82.2 3.6 %collective-permute-done.11.refs_1_ = bf16[320,1408]{1,0:T(8,128)(2,1)S(1)} collective-permute-done((bf16[320,1408]{1,0:T(8,128)(2,1)S(1)}, bf16[320,1408]{1,0:T(8,128)(2,1)S(1)}, u32[]{:S(2)}, u32[]{:S(2)}) %collective-permute-start.11) | collective-permute-done | bytes 901152 | tf_op jit(solution)/shard_map/ppermute | solution.py:191
  87.8 4.0 %shard_map.35.refs_3_ = f32[640,1408]{1,0:T(8,128)S(1)} custom-call(bf16[2,640,1408]{2,1,0:T(8,128)(2,1)S(1)} %get-tuple-element.30.refs_0_, bf16[320,1408]{1,0:T(8,128)(2,1)S(1)} %collective-permute-done.17.refs_1_, bf16[320,1408]{1,0:T(8,128)(2,1)S(1)} %collective-permute-done.18.refs_2_, ...), custom_call_target="tpu_custom_call", output_to_operand_aliasing={{}: (3, {})} | custom-call | flops 1730150400 | bytes 12615680 | tf_op jit(solution)/shard_map/pallas_call | solution.py:135
  91.8 3.6 %collective-permute-done.21.refs_1_ = bf16[320,1408]{1,0:T(8,128)(2,1)S(1)} collective-permute-done((bf16[320,1408]{1,0:T(8,128)(2,1)S(1)}, bf16[320,1408]{1,0:T(8,128)(2,1)S(1)}, u32[]{:S(2)}, u32[]{:S(2)}) %collective-permute-start.21) | collective-permute-done | bytes 901152 | tf_op jit(solution)/shard_map/ppermute | solution.py:191
  97.5 4.0 %shard_map.36.refs_3_ = f32[640,1408]{1,0:T(8,128)S(1)} custom-call(bf16[2,640,1408]{2,1,0:T(8,128)(2,1)S(1)} %get-tuple-element.30.refs_0_, bf16[320,1408]{1,0:T(8,128)(2,1)S(1)} %collective-permute-done.11.refs_1_, bf16[320,1408]{1,0:T(8,128)(2,1)S(1)} %collective-permute-done.16.refs_2_, ...), custom_call_target="tpu_custom_call", output_to_operand_aliasing={{}: (3, {})} | custom-call | flops 1730150400 | bytes 12615680 | tf_op jit(solution)/shard_map/pallas_call | solution.py:135
  101.5 3.6 %collective-permute-done.15.refs_1_ = bf16[320,1408]{1,0:T(8,128)(2,1)S(1)} collective-permute-done((bf16[320,1408]{1,0:T(8,128)(2,1)S(1)}, bf16[320,1408]{1,0:T(8,128)(2,1)S(1)}, u32[]{:S(2)}, u32[]{:S(2)}) %collective-permute-start.15) | collective-permute-done | bytes 901152 | tf_op jit(solution)/shard_map/ppermute | solution.py:191
  107.1 4.0 %shard_map.37.refs_3_ = f32[640,1408]{1,0:T(8,128)S(1)} custom-call(bf16[2,640,1408]{2,1,0:T(8,128)(2,1)S(1)} %get-tuple-element.30.refs_0_, bf16[320,1408]{1,0:T(8,128)(2,1)S(1)} %collective-permute-done.21.refs_1_, bf16[320,1408]{1,0:T(8,128)(2,1)S(1)} %collective-permute-done.22.refs_2_, ...), custom_call_target="tpu_custom_call", output_to_operand_aliasing={{}: (3, {})} | custom-call | flops 1730150400 | bytes 12615680 | tf_op jit(solution)/shard_map/pallas_call | solution.py:135
  111.1 3.6 %collective-permute-done.24.refs_1_ = bf16[320,1408]{1,0:T(8,128)(2,1)S(1)} collective-permute-done((bf16[320,1408]{1,0:T(8,128)(2,1)S(1)}, bf16[320,1408]{1,0:T(8,128)(2,1)S(1)}, u32[]{:S(2)}, u32[]{:S(2)}) %collective-permute-start.24) | collective-permute-done | bytes 901152 | tf_op jit(solution)/shard_map/ppermute | solution.py:191
  114.7 4.0 %shard_map.38.refs_3_ = f32[640,1408]{1,0:T(8,128)S(1)} custom-call(bf16[2,640,1408]{2,1,0:T(8,128)(2,1)S(1)} %get-tuple-element.30.refs_0_, bf16[320,1408]{1,0:T(8,128)(2,1)S(1)} %collective-permute-done.15.refs_1_, bf16[320,1408]{1,0:T(8,128)(2,1)S(1)} %collective-permute-done.20.refs_2_, ...), custom_call_target="tpu_custom_call", output_to_operand_aliasing={{}: (3, {})} | custom-call | flops 1730150400 | bytes 12615680 | tf_op jit(solution)/shard_map/pallas_call | solution.py:135
  118.7 5.6 %collective-permute-done.19.refs_1_ = bf16[320,1408]{1,0:T(8,128)(2,1)S(1)} collective-permute-done((bf16[320,1408]{1,0:T(8,128)(2,1)S(1)}, bf16[320,1408]{1,0:T(8,128)(2,1)S(1)}, u32[]{:S(2)}, u32[]{:S(2)}) %collective-permute-start.19) | collective-permute-done | bytes 901152 | tf_op jit(solution)/shard_map/ppermute | solution.py:191
  124.6 2.3 %collective-permute-start.29 = (bf16[320,1408]{1,0:T(8,128)(2,1)S(1)}, bf16[320,1408]{1,0:T(8,128)(2,1)}, u32[]{:S(2)}, u32[]{:S(2)}) collective-permute-start(bf16[320,1408]{1,0:T(8,128)(2,1)S(1)} %bitcast.8), channel_id=1, source_target_pairs={{8,0},{2,10},{16,8},{10,18},{24,16},{18,26},{28,24},{26,30},{20,28... | collective-permute-start | bytes 2703368 | tf_op jit(solution)/shard_map/ppermute | solution.py:191
  126.9 4.0 %shard_map.39.refs_3_ = f32[640,1408]{1,0:T(8,128)S(1)} custom-call(bf16[2,640,1408]{2,1,0:T(8,128)(2,1)S(1)} %get-tuple-element.30.refs_0_, bf16[320,1408]{1,0:T(8,128)(2,1)S(1)} %collective-permute-done.24.refs_1_, bf16[320,1408]{1,0:T(8,128)(2,1)S(1)} %collective-permute-done.25.refs_2_, ...), custom_call_target="tpu_custom_call", output_to_operand_aliasing={{}: (3, {})} | custom-call | flops 1730150400 | bytes 12615680 | tf_op jit(solution)/shard_map/pallas_call | solution.py:135
  130.9 4.5 %shard_map.40 = bf16[640,1408]{1,0:T(8,128)(2,1)S(1)} custom-call(bf16[2,640,1408]{2,1,0:T(8,128)(2,1)S(1)} %get-tuple-element.30.refs_0_, bf16[320,1408]{1,0:T(8,128)(2,1)S(1)} %collective-permute-done.19.refs_1_, bf16[320,1408]{1,0:T(8,128)(2,1)S(1)} %collective-permute-done.23.refs_2_, f32[640,1408]{1,0:T(8,128)S(1)} %shard_map.39.refs_3_, ...), custom_call_target="tpu_custom_call" | custom-call | flops 1730150400 | bytes 12615680 | tf_op jit(solution)/shard_map/pallas_call | solution.py:135
  141.8 7.1 %collective-permute-done.33.refs_5_ = bf16[320,1408]{1,0:T(8,128)(2,1)} collective-permute-done((bf16[320,1408]{1,0:T(8,128)(2,1)S(1)}, bf16[320,1408]{1,0:T(8,128)(2,1)}, u32[]{:S(2)}, u32[]{:S(2)}) %collective-permute-start.33) | collective-permute-done | bytes 901152 | tf_op jit(solution)/shard_map/ppermute | solution.py:191
  148.9 9.7 %collective-permute-done.31.refs_3_ = bf16[320,1408]{1,0:T(8,128)(2,1)} collective-permute-done((bf16[320,1408]{1,0:T(8,128)(2,1)S(1)}, bf16[320,1408]{1,0:T(8,128)(2,1)}, u32[]{:S(2)}, u32[]{:S(2)}) %collective-permute-start.31) | collective-permute-done | bytes 901152 | tf_op jit(solution)/shard_map/ppermute | solution.py:191
  158.5 9.5 %collective-permute-done.27.refs_1_ = bf16[320,1408]{1,0:T(8,128)(2,1)S(1)} collective-permute-done((bf16[320,1408]{1,0:T(8,128)(2,1)S(1)}, bf16[320,1408]{1,0:T(8,128)(2,1)S(1)}, u32[]{:S(2)}, u32[]{:S(2)}) %collective-permute-start.27) | collective-permute-done | bytes 901152 | tf_op jit(solution)/shard_map/ppermute | solution.py:191
  170.3 9.9 %shard_map.41.refs_3_ = f32[640,1408]{1,0:T(8,128)S(1)} custom-call(bf16[2,640,1408]{2,1,0:T(8,128)(2,1)S(1)} %copy-done.1, bf16[320,1408]{1,0:T(8,128)(2,1)} %collective-permute-done.29.refs_1_, bf16[320,1408]{1,0:T(8,128)(2,1)} %collective-permute-done.30.refs_2_, bf16[320,1408]{1,0:T(8,128)(2,1)} %collective-permute-done.31.refs_3_, ...), custom_call_target="tpu_custom_call" | custom-call | flops 5190451200 | bytes 16220160 | tf_op jit(solution)/shard_map/pallas_call | solution.py:135
  180.3 5.6 %shard_map.42 = f32[640,1408]{1,0:T(8,128)S(1)} custom-call(bf16[2,640,1408]{2,1,0:T(8,128)(2,1)S(1)} %copy-done.2, bf16[320,1408]{1,0:T(8,128)(2,1)S(1)} %collective-permute-done.27.refs_1_, bf16[320,1408]{1,0:T(8,128)(2,1)} %collective-permute-done.28.refs_2_, f32[640,1408]{1,0:T(8,128)S(1)} %shard_map.41.refs_3_, ...), custom_call_target="tpu_custom_call", output_to_operand_aliasing={{}: (3, {})} | custom-call | flops 1730150400 | bytes 12615680 | tf_op jit(solution)/shard_map/pallas_call | solution.py:135
  185.9 3.9 %add_multiply_fusion = f32[640,1408]{1,0:T(8,128)} fusion(f32[640,1408]{1,0:T(8,128)S(1)} %shard_map.42, bf16[640,1408]{1,0:T(8,128)(2,1)} %collective-permute-done.26, bf16[640,1408]{1,0:T(8,128)(2,1)S(1)} %shard_map.40, f32[640]{0:T(1024)S(1)} %reduce), kind=kLoop, calls=%fused_computation | loop fusion | flops 4505600 | bytes 10816000 | tf_op jit(solution)/shard_map/mul | solution.py:230
  (72 shorter events, 32.5 us)
Async XLA Ops:
  3.8 14.4 %collective-permute-start.4 = (bf16[320,1408]{1,0:T(8,128)(2,1)}, bf16[320,1408]{1,0:T(8,128)(2,1)S(1)}, u32[]{:S(2)}, u32[]{:S(2)}) collective-permute-start(bf16[320,1408]{1,0:T(8,128)(2,1)} %get-tuple-element.26.refs_1_), channel_id=1, source_target_pairs={{0,8},{10,2},{8,16},{18,10},{16,24},{26,18},{24,28},{30,26},{28,20... | collective-permute-start | bytes 2703368 | tf_op jit(solution)/shard_map/ppermute | solution.py:191
  6.8 21.0 %collective-permute-start = (bf16[320,1408]{1,0:T(8,128)(2,1)}, bf16[320,1408]{1,0:T(8,128)(2,1)S(1)}, u32[]{:S(2)}, u32[]{:S(2)}) collective-permute-start(bf16[320,1408]{1,0:T(8,128)(2,1)} %get-tuple-element.27.refs_2_), channel_id=1, source_target_pairs={{0,8},{10,2},{8,16},{18,10},{16,24},{26,18},{24,28},{30,26},{28,20... | collective-permute-start | bytes 2703368 | tf_op jit(solution)/shard_map/ppermute | solution.py:191
  8.4 19.4 %collective-permute-start.2 = (bf16[320,1408]{1,0:T(8,128)(2,1)}, bf16[320,1408]{1,0:T(8,128)(2,1)S(1)}, u32[]{:S(2)}, u32[]{:S(2)}) collective-permute-start(bf16[320,1408]{1,0:T(8,128)(2,1)} %get-tuple-element.26.refs_1_), channel_id=1, source_target_pairs={{0,2},{2,0},{4,6},{6,4},{8,10},{10,8},{12,14},{14,12},{16,18},{18,... | collective-permute-start | bytes 2703368 | tf_op jit(solution)/shard_map/ppermute | solution.py:191
  18.1 19.3 %collective-permute-start.9 = (bf16[320,1408]{1,0:T(8,128)(2,1)S(1)}, bf16[320,1408]{1,0:T(8,128)(2,1)S(1)}, u32[]{:S(2)}, u32[]{:S(2)}) collective-permute-start(bf16[320,1408]{1,0:T(8,128)(2,1)S(1)} %collective-permute-done.4.refs_5_), channel_id=1, source_target_pairs={{0,8},{10,2},{8,16},{18,10},{16,24},{26,18},{24,28},{30,26},{28,20... | collective-permute-start | bytes 2703368 | tf_op jit(solution)/shard_map/ppermute | solution.py:191
  20.2 17.2 %collective-permute-start.3 = (bf16[320,1408]{1,0:T(8,128)(2,1)}, bf16[320,1408]{1,0:T(8,128)(2,1)S(1)}, u32[]{:S(2)}, u32[]{:S(2)}) collective-permute-start(bf16[320,1408]{1,0:T(8,128)(2,1)} %get-tuple-element.27.refs_2_), channel_id=1, source_target_pairs={{0,2},{2,0},{4,6},{6,4},{8,10},{10,8},{12,14},{14,12},{16,18},{18,... | collective-permute-start | bytes 2703368 | tf_op jit(solution)/shard_map/ppermute | solution.py:191
  20.2 19.3 %collective-permute-start.5 = (bf16[320,1408]{1,0:T(8,128)(2,1)S(1)}, bf16[320,1408]{1,0:T(8,128)(2,1)S(1)}, u32[]{:S(2)}, u32[]{:S(2)}) collective-permute-start(bf16[320,1408]{1,0:T(8,128)(2,1)S(1)} %collective-permute-done.4.refs_5_), channel_id=1, source_target_pairs={{0,2},{2,0},{4,6},{6,4},{8,10},{10,8},{12,14},{14,12},{16,18},{18,... | collective-permute-start | bytes 2703368 | tf_op jit(solution)/shard_map/ppermute | solution.py:191
  27.8 11.7 %collective-permute-start.6 = (bf16[320,1408]{1,0:T(8,128)(2,1)S(1)}, bf16[320,1408]{1,0:T(8,128)(2,1)S(1)}, u32[]{:S(2)}, u32[]{:S(2)}) collective-permute-start(bf16[320,1408]{1,0:T(8,128)(2,1)S(1)} %collective-permute-done.refs_7_), channel_id=1, source_target_pairs={{0,2},{2,0},{4,6},{6,4},{8,10},{10,8},{12,14},{14,12},{16,18},{18,... | collective-permute-start | bytes 2703368 | tf_op jit(solution)/shard_map/ppermute | solution.py:191
  27.8 20.8 %collective-permute-start.1 = (bf16[320,1408]{1,0:T(8,128)(2,1)S(1)}, bf16[320,1408]{1,0:T(8,128)(2,1)S(1)}, u32[]{:S(2)}, u32[]{:S(2)}) collective-permute-start(bf16[320,1408]{1,0:T(8,128)(2,1)S(1)} %collective-permute-done.refs_7_), channel_id=1, source_target_pairs={{0,8},{10,2},{8,16},{18,10},{16,24},{26,18},{24,28},{30,26},{28,20... | collective-permute-start | bytes 2703368 | tf_op jit(solution)/shard_map/ppermute | solution.py:191
  37.4 12.9 %collective-permute-start.10 = (bf16[320,1408]{1,0:T(8,128)(2,1)S(1)}, bf16[320,1408]{1,0:T(8,128)(2,1)S(1)}, u32[]{:S(2)}, u32[]{:S(2)}) collective-permute-start(bf16[320,1408]{1,0:T(8,128)(2,1)S(1)} %collective-permute-done.9.refs_1_), channel_id=1, source_target_pairs={{0,2},{2,0},{4,6},{6,4},{8,10},{10,8},{12,14},{14,12},{16,18},{18,... | collective-permute-start | bytes 2703368 | tf_op jit(solution)/shard_map/ppermute | solution.py:191
  37.5 19.3 %collective-permute-start.13 = (bf16[320,1408]{1,0:T(8,128)(2,1)S(1)}, bf16[320,1408]{1,0:T(8,128)(2,1)S(1)}, u32[]{:S(2)}, u32[]{:S(2)}) collective-permute-start(bf16[320,1408]{1,0:T(8,128)(2,1)S(1)} %collective-permute-done.9.refs_1_), channel_id=1, source_target_pairs={{0,8},{10,2},{8,16},{18,10},{16,24},{26,18},{24,28},{30,26},{28,20... | collective-permute-start | bytes 2703368 | tf_op jit(solution)/shard_map/ppermute | solution.py:191
  48.6 10.2 %collective-permute-start.8 = (bf16[320,1408]{1,0:T(8,128)(2,1)S(1)}, bf16[320,1408]{1,0:T(8,128)(2,1)S(1)}, u32[]{:S(2)}, u32[]{:S(2)}) collective-permute-start(bf16[320,1408]{1,0:T(8,128)(2,1)S(1)} %collective-permute-done.1.refs_1_), channel_id=1, source_target_pairs={{0,2},{2,0},{4,6},{6,4},{8,10},{10,8},{12,14},{14,12},{16,18},{18,... | collective-permute-start | bytes 2703368 | tf_op jit(solution)/shard_map/ppermute | solution.py:191
  48.8 17.6 %collective-permute-start.7 = (bf16[320,1408]{1,0:T(8,128)(2,1)S(1)}, bf16[320,1408]{1,0:T(8,128)(2,1)S(1)}, u32[]{:S(2)}, u32[]{:S(2)}) collective-permute-start(bf16[320,1408]{1,0:T(8,128)(2,1)S(1)} %collective-permute-done.1.refs_1_), channel_id=1, source_target_pairs={{0,8},{10,2},{8,16},{18,10},{16,24},{26,18},{24,28},{30,26},{28,20... | collective-permute-start | bytes 2703368 | tf_op jit(solution)/shard_map/ppermute | solution.py:191
  56.8 11.7 %collective-permute-start.14 = (bf16[320,1408]{1,0:T(8,128)(2,1)S(1)}, bf16[320,1408]{1,0:T(8,128)(2,1)S(1)}, u32[]{:S(2)}, u32[]{:S(2)}) collective-permute-start(bf16[320,1408]{1,0:T(8,128)(2,1)S(1)} %collective-permute-done.13.refs_1_), channel_id=1, source_target_pairs={{0,2},{2,0},{4,6},{6,4},{8,10},{10,8},{12,14},{14,12},{16,18},{18,... | collective-permute-start | bytes 2703368 | tf_op jit(solution)/shard_map/ppermute | solution.py:191
  56.8 19.3 %collective-permute-start.17 = (bf16[320,1408]{1,0:T(8,128)(2,1)S(1)}, bf16[320,1408]{1,0:T(8,128)(2,1)S(1)}, u32[]{:S(2)}, u32[]{:S(2)}) collective-permute-start(bf16[320,1408]{1,0:T(8,128)(2,1)S(1)} %collective-permute-done.13.refs_1_), channel_id=1, source_target_pairs={{0,8},{10,2},{8,16},{18,10},{16,24},{26,18},{24,28},{30,26},{28,20... | collective-permute-start | bytes 2703368 | tf_op jit(solution)/shard_map/ppermute | solution.py:191
  66.4 11.7 %collective-permute-start.12 = (bf16[320,1408]{1,0:T(8,128)(2,1)S(1)}, bf16[320,1408]{1,0:T(8,128)(2,1)S(1)}, u32[]{:S(2)}, u32[]{:S(2)}) collective-permute-start(bf16[320,1408]{1,0:T(8,128)(2,1)S(1)} %collective-permute-done.7.refs_1_), channel_id=1, source_target_pairs={{0,2},{2,0},{4,6},{6,4},{8,10},{10,8},{12,14},{14,12},{16,18},{18,... | collective-permute-start | bytes 2703368 | tf_op jit(solution)/shard_map/ppermute | solution.py:191
  66.4 19.3 %collective-permute-start.11 = (bf16[320,1408]{1,0:T(8,128)(2,1)S(1)}, bf16[320,1408]{1,0:T(8,128)(2,1)S(1)}, u32[]{:S(2)}, u32[]{:S(2)}) collective-permute-start(bf16[320,1408]{1,0:T(8,128)(2,1)S(1)} %collective-permute-done.7.refs_1_), channel_id=1, source_target_pairs={{0,8},{10,2},{8,16},{18,10},{16,24},{26,18},{24,28},{30,26},{28,20... | collective-permute-start | bytes 2703368 | tf_op jit(solution)/shard_map/ppermute | solution.py:191
  76.1 11.7 %collective-permute-start.18 = (bf16[320,1408]{1,0:T(8,128)(2,1)S(1)}, bf16[320,1408]{1,0:T(8,128)(2,1)S(1)}, u32[]{:S(2)}, u32[]{:S(2)}) collective-permute-start(bf16[320,1408]{1,0:T(8,128)(2,1)S(1)} %collective-permute-done.17.refs_1_), channel_id=1, source_target_pairs={{0,2},{2,0},{4,6},{6,4},{8,10},{10,8},{12,14},{14,12},{16,18},{18,... | collective-permute-start | bytes 2703368 | tf_op jit(solution)/shard_map/ppermute | solution.py:191
  76.1 19.3 %collective-permute-start.21 = (bf16[320,1408]{1,0:T(8,128)(2,1)S(1)}, bf16[320,1408]{1,0:T(8,128)(2,1)S(1)}, u32[]{:S(2)}, u32[]{:S(2)}) collective-permute-start(bf16[320,1408]{1,0:T(8,128)(2,1)S(1)} %collective-permute-done.17.refs_1_), channel_id=1, source_target_pairs={{0,8},{10,2},{8,16},{18,10},{16,24},{26,18},{24,28},{30,26},{28,20... | collective-permute-start | bytes 2703368 | tf_op jit(solution)/shard_map/ppermute | solution.py:191
  85.7 11.7 %collective-permute-start.16 = (bf16[320,1408]{1,0:T(8,128)(2,1)S(1)}, bf16[320,1408]{1,0:T(8,128)(2,1)S(1)}, u32[]{:S(2)}, u32[]{:S(2)}) collective-permute-start(bf16[320,1408]{1,0:T(8,128)(2,1)S(1)} %collective-permute-done.11.refs_1_), channel_id=1, source_target_pairs={{0,2},{2,0},{4,6},{6,4},{8,10},{10,8},{12,14},{14,12},{16,18},{18,... | collective-permute-start | bytes 2703368 | tf_op jit(solution)/shard_map/ppermute | solution.py:191
  85.7 19.3 %collective-permute-start.15 = (bf16[320,1408]{1,0:T(8,128)(2,1)S(1)}, bf16[320,1408]{1,0:T(8,128)(2,1)S(1)}, u32[]{:S(2)}, u32[]{:S(2)}) collective-permute-start(bf16[320,1408]{1,0:T(8,128)(2,1)S(1)} %collective-permute-done.11.refs_1_), channel_id=1, source_target_pairs={{0,8},{10,2},{8,16},{18,10},{16,24},{26,18},{24,28},{30,26},{28,20... | collective-permute-start | bytes 2703368 | tf_op jit(solution)/shard_map/ppermute | solution.py:191
  95.4 11.7 %collective-permute-start.22 = (bf16[320,1408]{1,0:T(8,128)(2,1)S(1)}, bf16[320,1408]{1,0:T(8,128)(2,1)S(1)}, u32[]{:S(2)}, u32[]{:S(2)}) collective-permute-start(bf16[320,1408]{1,0:T(8,128)(2,1)S(1)} %collective-permute-done.21.refs_1_), channel_id=1, source_target_pairs={{0,2},{2,0},{4,6},{6,4},{8,10},{10,8},{12,14},{14,12},{16,18},{18,... | collective-permute-start | bytes 2703368 | tf_op jit(solution)/shard_map/ppermute | solution.py:191
  95.4 19.3 %collective-permute-start.24 = (bf16[320,1408]{1,0:T(8,128)(2,1)S(1)}, bf16[320,1408]{1,0:T(8,128)(2,1)S(1)}, u32[]{:S(2)}, u32[]{:S(2)}) collective-permute-start(bf16[320,1408]{1,0:T(8,128)(2,1)S(1)} %collective-permute-done.21.refs_1_), channel_id=1, source_target_pairs={{0,8},{10,2},{8,16},{18,10},{16,24},{26,18},{24,28},{30,26},{28,20... | collective-permute-start | bytes 2703368 | tf_op jit(solution)/shard_map/ppermute | solution.py:191
  105.0 19.3 %collective-permute-start.19 = (bf16[320,1408]{1,0:T(8,128)(2,1)S(1)}, bf16[320,1408]{1,0:T(8,128)(2,1)S(1)}, u32[]{:S(2)}, u32[]{:S(2)}) collective-permute-start(bf16[320,1408]{1,0:T(8,128)(2,1)S(1)} %collective-permute-done.15.refs_1_), channel_id=1, source_target_pairs={{0,8},{10,2},{8,16},{18,10},{16,24},{26,18},{24,28},{30,26},{28,20... | collective-permute-start | bytes 2703368 | tf_op jit(solution)/shard_map/ppermute | solution.py:191
  114.7 12.2 %collective-permute-start.25 = (bf16[320,1408]{1,0:T(8,128)(2,1)S(1)}, bf16[320,1408]{1,0:T(8,128)(2,1)S(1)}, u32[]{:S(2)}, u32[]{:S(2)}) collective-permute-start(bf16[320,1408]{1,0:T(8,128)(2,1)S(1)} %collective-permute-done.24.refs_1_), channel_id=1, source_target_pairs={{0,2},{2,0},{4,6},{6,4},{8,10},{10,8},{12,14},{14,12},{16,18},{18,... | collective-permute-start | bytes 2703368 | tf_op jit(solution)/shard_map/ppermute | solution.py:191
  124.6 17.1 %collective-permute-start.29 = (bf16[320,1408]{1,0:T(8,128)(2,1)S(1)}, bf16[320,1408]{1,0:T(8,128)(2,1)}, u32[]{:S(2)}, u32[]{:S(2)}) collective-permute-start(bf16[320,1408]{1,0:T(8,128)(2,1)S(1)} %bitcast.8), channel_id=1, source_target_pairs={{8,0},{2,10},{16,8},{10,18},{24,16},{18,26},{28,24},{26,30},{20,28... | collective-permute-start | bytes 2703368 | tf_op jit(solution)/shard_map/ppermute | solution.py:191
  135.5 13.4 %collective-permute-start.33 = (bf16[320,1408]{1,0:T(8,128)(2,1)S(1)}, bf16[320,1408]{1,0:T(8,128)(2,1)}, u32[]{:S(2)}, u32[]{:S(2)}) collective-permute-start(bf16[320,1408]{1,0:T(8,128)(2,1)S(1)} %bitcast.7), channel_id=1, source_target_pairs={{8,0},{2,10},{16,8},{10,18},{24,16},{18,26},{28,24},{26,30},{20,28... | collective-permute-start | bytes 2703368 | tf_op jit(solution)/shard_map/ppermute | solution.py:191
  137.1 21.4 %collective-permute-start.31 = (bf16[320,1408]{1,0:T(8,128)(2,1)S(1)}, bf16[320,1408]{1,0:T(8,128)(2,1)}, u32[]{:S(2)}, u32[]{:S(2)}) collective-permute-start(bf16[320,1408]{1,0:T(8,128)(2,1)S(1)} %bitcast.6), channel_id=1, source_target_pairs={{8,0},{2,10},{16,8},{10,18},{24,16},{18,26},{28,24},{26,30},{20,28... | collective-permute-start | bytes 2703368 | tf_op jit(solution)/shard_map/ppermute | solution.py:191
  138.7 29.4 %collective-permute-start.27 = (bf16[320,1408]{1,0:T(8,128)(2,1)S(1)}, bf16[320,1408]{1,0:T(8,128)(2,1)S(1)}, u32[]{:S(2)}, u32[]{:S(2)}) collective-permute-start(bf16[320,1408]{1,0:T(8,128)(2,1)S(1)} %bitcast.5), channel_id=1, source_target_pairs={{8,0},{2,10},{16,8},{10,18},{24,16},{18,26},{28,24},{26,30},{20,28... | collective-permute-start | bytes 2703368 | tf_op jit(solution)/shard_map/ppermute | solution.py:191
  140.3 45.6 %collective-permute-start.26 = (bf16[640,1408]{1,0:T(8,128)(2,1)S(1)}, bf16[640,1408]{1,0:T(8,128)(2,1)}, u32[]{:S(2)}, u32[]{:S(2)}) collective-permute-start(bf16[640,1408]{1,0:T(8,128)(2,1)S(1)} %shard_map.40), channel_id=1, source_target_pairs={{0,1},{1,0},{2,3},{3,2},{4,5},{5,4},{6,7},{7,6},{8,9},{9,8},{10,11... | collective-permute-start | bytes 5406728 | tf_op jit(solution)/shard_map/ppermute | solution.py:213
  141.8 26.5 %collective-permute-start.30 = (bf16[320,1408]{1,0:T(8,128)(2,1)}, bf16[320,1408]{1,0:T(8,128)(2,1)}, u32[]{:S(2)}, u32[]{:S(2)}) collective-permute-start(bf16[320,1408]{1,0:T(8,128)(2,1)} %collective-permute-done.29.refs_1_), channel_id=1, source_target_pairs={{0,2},{2,0},{4,6},{6,4},{8,10},{10,8},{12,14},{14,12},{16,18},{18,... | collective-permute-start | bytes 2703368 | tf_op jit(solution)/shard_map/ppermute | solution.py:191
  148.9 19.4 %collective-permute-start.34 = (bf16[320,1408]{1,0:T(8,128)(2,1)}, bf16[320,1408]{1,0:T(8,128)(2,1)}, u32[]{:S(2)}, u32[]{:S(2)}) collective-permute-start(bf16[320,1408]{1,0:T(8,128)(2,1)} %collective-permute-done.33.refs_5_), channel_id=1, source_target_pairs={{0,2},{2,0},{4,6},{6,4},{8,10},{10,8},{12,14},{14,12},{16,18},{18,... | collective-permute-start | bytes 2703368 | tf_op jit(solution)/shard_map/ppermute | solution.py:191
  168.1 12.2 %collective-permute-start.28 = (bf16[320,1408]{1,0:T(8,128)(2,1)S(1)}, bf16[320,1408]{1,0:T(8,128)(2,1)}, u32[]{:S(2)}, u32[]{:S(2)}) collective-permute-start(bf16[320,1408]{1,0:T(8,128)(2,1)S(1)} %collective-permute-done.27.refs_1_), channel_id=1, source_target_pairs={{0,2},{2,0},{4,6},{6,4},{8,10},{10,8},{12,14},{14,12},{16,18},{18,... | collective-permute-start | bytes 2703368 | tf_op jit(solution)/shard_map/ppermute | solution.py:191
  (11 other events, 192.9 us)

commit v4 on v3

--- a/solution.py
+++ b/solution.py
@@ -9,11 +9,13 @@
 from jax.sharding import PartitionSpec as P
 
 CORES = 2
-PARTS = 4
+PARTS = 5
 CHAINS = 2
 LAG = 2
 SLAG = 1
 FIRST = 2
+BFREE = 1
+BLAG = 2
 COSTW = 1.0
 ROW_TILE = 16
 VMEM_LIMIT = 32 * 1024 * 1024
@@ -54,19 +56,18 @@
     )(student, teacher)
 
 
-def pack_kernel(counts, which, student, teacher, *packed):
-    at = 0
+def pack_kernel(counts, at, which, student, teacher, *packed):
     for out, count in zip(packed, counts):
         out[:count, :] = normalized(student[at : at + count, :])[1]
         out[count:, :] = normalized(teacher[at : at + count, :])[1]
         at += count
 
 
-def pack_share(student, teacher, pair_index, share, counts):
+def pack_share(student, teacher, pair_index, share, counts, at=0):
     width = student.shape[1]
     mine = pl.BlockSpec((share, width), lambda i, which: (which[0], 0))
     return pl.pallas_call(
-        functools.partial(pack_kernel, counts),
+        functools.partial(pack_kernel, counts, at),
         grid_spec=pltpu.PrefetchScalarGridSpec(
             num_scalar_prefetch=1,
             grid=(1,),
@@ -181,7 +182,11 @@
     around, reverse, swap = ring_routes(seq_count)
     hops = seq_count // CORES - 2
     share = rows // pair_count
-    pieces = list(pack_share(student, teacher, pair_index, share, split(share, CHAINS)))
+    counts = split(share, CHAINS)
+    pieces, at = [], 0
+    for n in counts:
+        pieces += pack_share(student, teacher, pair_index, share, [n], at)
+        at += n
     own_half, s_scale = normalize_own(after(student, *pieces), teacher)
 
     def add(batch, total, **options):
@@ -216,18 +221,16 @@
     if not doubled:
         return s_scale * summed
 
-    nearest, at = [], 0
+    sums, at = [], 0
     for k, n in enumerate(split(rows, PARTS)):
         piece = own_half[:, at : at + n].reshape(2 * n, width)
-        nearest.append(move(piece, reverse, own if k else held[0]))
         at += n
-    batch = []
-    for x in nearest[:-1]:
-        batch += [x, move(x, swap, own)]
-    total = add(batch, None)
-    batch = [nearest[-1], move(nearest[-1], swap)]
-    total = add(batch, total, project=(student, s_scale))
-    return s_scale * (summed + total)
+        last = k == PARTS - 1
+        x = move(piece, reverse, *([own] if k >= BFREE else [held[k % CHAINS]]))
+        ready = sums[len(sums) - 1 - BLAG :][:1] if len(sums) > BLAG else [own]
+        batch = [x, move(x, swap, *ready)]
+        sums.append(add(batch, sums[-1] if sums else None, project=(student, s_scale) if last else None))
+    return s_scale * (summed + sums[-1])
 
 
 def solution(mesh):

time: 190 us -> 190 us (level)
  waiting for transfers between devices: 77 us -> 65.5 us
  Pallas kernels: 70 us -> 75.6 us
  local copies, waits for them, and re-layouts: 4.33 us -> 9.33 us
    ppermute x34 -> x36, waiting for transfers between devices: 77 us -> 65.5 us  [move(): return lax.ppermute(after(x, *wait_for), 'seq', route)]
    unnamed x16 -> x22, local copies, waits for them, and re-layouts: 4.06 us -> 9.02 us
    pallas_call x13 -> x16, Pallas kernels: 65 us -> 68 us  [add_relation(): pl.pallas_call(functools.partial(relation_kernel, margin, weight, counts,...]
    pallas_call x1 -> x2, Pallas kernels: 3.76 us -> 6.38 us  [pack_share(): pl.pallas_call(functools.partial(pack_kernel, counts, at), grid_spec=pltp...]
    ppermute x34 -> x36, starting transfers between devices: 32.7 us -> 33.5 us  [move(): return lax.ppermute(after(x, *wait_for), 'seq', route)]
  transfers between devices with their start and end apart: 35 -> 37, of which waited for: 14 -> 15; matrix products, arithmetic and copies ran while one was open for 0% -> 0% of each run, Pallas kernels for 35% -> 38%
where the time goes in v4:
time: 190 us
  Pallas kernels  75.6 us (40%)
  waiting for transfers between devices  65.5 us (34%)
  starting transfers between devices  35 us (18%)
  local copies, waits for them, and re-layouts  9.33 us (5%)
  other arithmetic  4.08 us (2%)
    pallas_call x16, Pallas kernels, add_relation(): pl.pallas_call(functools.partial(relation_kernel, margin, weight, counts,...  68 us
    ppermute x36, waiting for transfers between devices, move(): return lax.ppermute(after(x, *wait_for), 'seq', route)  65.5 us
    ppermute x36, starting transfers between devices, move(): return lax.ppermute(after(x, *wait_for), 'seq', route)  33.5 us
    unnamed x22, local copies, waits for them, and re-layouts  9.02 us
    pallas_call x2, Pallas kernels, pack_share(): pl.pallas_call(functools.partial(pack_kernel, counts, at), grid_spec=pltp...  6.38 us
    mul x1, other arithmetic, local(): return s_scale * (summed + sums[-1])  3.91 us
  transfers between devices with their start and end apart: 37, of which 15 were waited for; matrix products, arithmetic and copies ran while one was open for 0% of the time, Pallas kernels for 38%

profile of v4, /device:TPU:0, one launch (start us, length us, event | category | flops | bytes accessed | tf_op | source)
XLA Modules:
  0.0 189.9 jit_solution(12482137822570783474)
XLA Ops:
  0.0 3.2 %shard_map.28.refs_1_ = bf16[320,1408]{1,0:T(8,128)(2,1)} custom-call(s32[1]{0:T(128)} %bitcast.which, f32[640,1408]{1,0:T(8,128)} %refs_4_.3, f32[640,1408]{1,0:T(8,128)} %teacher.5), custom_call_target="tpu_custom_call" | custom-call | flops 2703360 | bytes 5406720 | tf_op jit(solution)/shard_map/pallas_call | solution.py:69
  3.2 3.0 %collective-permute-start.4 = (bf16[320,1408]{1,0:T(8,128)(2,1)}, bf16[320,1408]{1,0:T(8,128)(2,1)}, u32[]{:S(2)}, u32[]{:S(2)}) collective-permute-start(bf16[320,1408]{1,0:T(8,128)(2,1)} %shard_map.28.refs_1_), channel_id=1, source_target_pairs={{0,8},{10,2},{8,16},{18,10},{16,24},{26,18},{24,28},{30,26},{28,20... | collective-permute-start | bytes 2703368 | tf_op jit(solution)/shard_map/ppermute | solution.py:196
  6.2 3.2 %shard_map.29.refs_2_ = bf16[320,1408]{1,0:T(8,128)(2,1)} custom-call(s32[1]{0:T(128)} %bitcast.which, f32[640,1408]{1,0:T(8,128)} %refs_4_.3, f32[640,1408]{1,0:T(8,128)} %teacher.5), custom_call_target="tpu_custom_call" | custom-call | flops 2703360 | bytes 5406720 | tf_op jit(solution)/shard_map/pallas_call | solution.py:69
  11.0 6.7 %collective-permute-done.4.refs_5_ = bf16[320,1408]{1,0:T(8,128)(2,1)} collective-permute-done((bf16[320,1408]{1,0:T(8,128)(2,1)}, bf16[320,1408]{1,0:T(8,128)(2,1)}, u32[]{:S(2)}, u32[]{:S(2)}) %collective-permute-start.4) | collective-permute-done | bytes 901152 | tf_op jit(solution)/shard_map/ppermute | solution.py:196
  20.3 7.0 %collective-permute-done.refs_7_ = bf16[320,1408]{1,0:T(8,128)(2,1)S(1)} collective-permute-done((bf16[320,1408]{1,0:T(8,128)(2,1)}, bf16[320,1408]{1,0:T(8,128)(2,1)S(1)}, u32[]{:S(2)}, u32[]{:S(2)}) %collective-permute-start) | collective-permute-done | bytes 901152 | tf_op jit(solution)/shard_map/ppermute | solution.py:196
  32.6 4.4 %collective-permute-done.9.refs_1_ = bf16[320,1408]{1,0:T(8,128)(2,1)S(1)} collective-permute-done((bf16[320,1408]{1,0:T(8,128)(2,1)}, bf16[320,1408]{1,0:T(8,128)(2,1)S(1)}, u32[]{:S(2)}, u32[]{:S(2)}) %collective-permute-start.9) | collective-permute-done | bytes 901152 | tf_op jit(solution)/shard_map/ppermute | solution.py:196
  40.1 10.1 %shard_map.31.refs_3_ = f32[640,1408]{1,0:T(8,128)S(1)} custom-call(bf16[2,640,1408]{2,1,0:T(8,128)(2,1)S(1)} %get-tuple-element.29.refs_0_, bf16[320,1408]{1,0:T(8,128)(2,1)S(1)} %copy-done.9, bf16[320,1408]{1,0:T(8,128)(2,1)S(1)} %copy-done.10, bf16[320,1408]{1,0:T(8,128)(2,1)S(1)} %collective-permute-done.2.refs_3_, ...), custom_call_target="tpu_custom_call" | custom-call | flops 6920601600 | bytes 18022400 | tf_op jit(solution)/shard_map/pallas_call | solution.py:136
  51.9 4.0 %shard_map.32.refs_3_ = f32[640,1408]{1,0:T(8,128)S(1)} custom-call(bf16[2,640,1408]{2,1,0:T(8,128)(2,1)S(1)} %get-tuple-element.29.refs_0_, bf16[320,1408]{1,0:T(8,128)(2,1)S(1)} %collective-permute-done.9.refs_1_, bf16[320,1408]{1,0:T(8,128)(2,1)S(1)} %collective-permute-done.10.refs_2_, ...), custom_call_target="tpu_custom_call", output_to_operand_aliasing={{}: (3, {})} | custom-call | flops 1730150400 | bytes 12615680 | tf_op jit(solution)/shard_map/pallas_call | solution.py:136
  58.3 4.0 %shard_map.33.refs_3_ = f32[640,1408]{1,0:T(8,128)S(1)} custom-call(bf16[2,640,1408]{2,1,0:T(8,128)(2,1)S(1)} %get-tuple-element.29.refs_0_, bf16[320,1408]{1,0:T(8,128)(2,1)S(1)} %collective-permute-done.1.refs_1_, bf16[320,1408]{1,0:T(8,128)(2,1)S(1)} %collective-permute-done.8.refs_2_, ...), custom_call_target="tpu_custom_call", output_to_operand_aliasing={{}: (3, {})} | custom-call | flops 1730150400 | bytes 12615680 | tf_op jit(solution)/shard_map/pallas_call | solution.py:136
  62.3 3.6 %collective-permute-done.7.refs_1_ = bf16[320,1408]{1,0:T(8,128)(2,1)S(1)} collective-permute-done((bf16[320,1408]{1,0:T(8,128)(2,1)S(1)}, bf16[320,1408]{1,0:T(8,128)(2,1)S(1)}, u32[]{:S(2)}, u32[]{:S(2)}) %collective-permute-start.7) | collective-permute-done | bytes 901152 | tf_op jit(solution)/shard_map/ppermute | solution.py:196
  67.9 4.0 %shard_map.34.refs_3_ = f32[640,1408]{1,0:T(8,128)S(1)} custom-call(bf16[2,640,1408]{2,1,0:T(8,128)(2,1)S(1)} %get-tuple-element.29.refs_0_, bf16[320,1408]{1,0:T(8,128)(2,1)S(1)} %collective-permute-done.13.refs_1_, bf16[320,1408]{1,0:T(8,128)(2,1)S(1)} %collective-permute-done.14.refs_2_, ...), custom_call_target="tpu_custom_call", output_to_operand_aliasing={{}: (3, {})} | custom-call | flops 1730150400 | bytes 12615680 | tf_op jit(solution)/shard_map/pallas_call | solution.py:136
  71.9 3.6 %collective-permute-done.17.refs_1_ = bf16[320,1408]{1,0:T(8,128)(2,1)S(1)} collective-permute-done((bf16[320,1408]{1,0:T(8,128)(2,1)S(1)}, bf16[320,1408]{1,0:T(8,128)(2,1)S(1)}, u32[]{:S(2)}, u32[]{:S(2)}) %collective-permute-start.17) | collective-permute-done | bytes 901152 | tf_op jit(solution)/shard_map/ppermute | solution.py:196
  77.6 4.0 %shard_map.35.refs_3_ = f32[640,1408]{1,0:T(8,128)S(1)} custom-call(bf16[2,640,1408]{2,1,0:T(8,128)(2,1)S(1)} %get-tuple-element.29.refs_0_, bf16[320,1408]{1,0:T(8,128)(2,1)S(1)} %collective-permute-done.7.refs_1_, bf16[320,1408]{1,0:T(8,128)(2,1)S(1)} %collective-permute-done.12.refs_2_, ...), custom_call_target="tpu_custom_call", output_to_operand_aliasing={{}: (3, {})} | custom-call | flops 1730150400 | bytes 12615680 | tf_op jit(solution)/shard_map/pallas_call | solution.py:136
  81.6 3.6 %collective-permute-done.11.refs_1_ = bf16[320,1408]{1,0:T(8,128)(2,1)S(1)} collective-permute-done((bf16[320,1408]{1,0:T(8,128)(2,1)S(1)}, bf16[320,1408]{1,0:T(8,128)(2,1)S(1)}, u32[]{:S(2)}, u32[]{:S(2)}) %collective-permute-start.11) | collective-permute-done | bytes 901152 | tf_op jit(solution)/shard_map/ppermute | solution.py:196
  87.2 4.0 %shard_map.36.refs_3_ = f32[640,1408]{1,0:T(8,128)S(1)} custom-call(bf16[2,640,1408]{2,1,0:T(8,128)(2,1)S(1)} %get-tuple-element.29.refs_0_, bf16[320,1408]{1,0:T(8,128)(2,1)S(1)} %collective-permute-done.17.refs_1_, bf16[320,1408]{1,0:T(8,128)(2,1)S(1)} %collective-permute-done.18.refs_2_, ...), custom_call_target="tpu_custom_call", output_to_operand_aliasing={{}: (3, {})} | custom-call | flops 1730150400 | bytes 12615680 | tf_op jit(solution)/shard_map/pallas_call | solution.py:136
  91.2 3.6 %collective-permute-done.21.refs_1_ = bf16[320,1408]{1,0:T(8,128)(2,1)S(1)} collective-permute-done((bf16[320,1408]{1,0:T(8,128)(2,1)S(1)}, bf16[320,1408]{1,0:T(8,128)(2,1)S(1)}, u32[]{:S(2)}, u32[]{:S(2)}) %collective-permute-start.21) | collective-permute-done | bytes 901152 | tf_op jit(solution)/shard_map/ppermute | solution.py:196
  96.9 4.0 %shard_map.37.refs_3_ = f32[640,1408]{1,0:T(8,128)S(1)} custom-call(bf16[2,640,1408]{2,1,0:T(8,128)(2,1)S(1)} %get-tuple-element.29.refs_0_, bf16[320,1408]{1,0:T(8,128)(2,1)S(1)} %collective-permute-done.11.refs_1_, bf16[320,1408]{1,0:T(8,128)(2,1)S(1)} %collective-permute-done.16.refs_2_, ...), custom_call_target="tpu_custom_call", output_to_operand_aliasing={{}: (3, {})} | custom-call | flops 1730150400 | bytes 12615680 | tf_op jit(solution)/shard_map/pallas_call | solution.py:136
  100.9 3.6 %collective-permute-done.15.refs_1_ = bf16[320,1408]{1,0:T(8,128)(2,1)S(1)} collective-permute-done((bf16[320,1408]{1,0:T(8,128)(2,1)S(1)}, bf16[320,1408]{1,0:T(8,128)(2,1)S(1)}, u32[]{:S(2)}, u32[]{:S(2)}) %collective-permute-start.15) | collective-permute-done | bytes 901152 | tf_op jit(solution)/shard_map/ppermute | solution.py:196
  106.5 4.0 %shard_map.38.refs_3_ = f32[640,1408]{1,0:T(8,128)S(1)} custom-call(bf16[2,640,1408]{2,1,0:T(8,128)(2,1)S(1)} %get-tuple-element.29.refs_0_, bf16[320,1408]{1,0:T(8,128)(2,1)S(1)} %collective-permute-done.21.refs_1_, bf16[320,1408]{1,0:T(8,128)(2,1)S(1)} %collective-permute-done.22.refs_2_, ...), custom_call_target="tpu_custom_call", output_to_operand_aliasing={{}: (3, {})} | custom-call | flops 1730150400 | bytes 12615680 | tf_op jit(solution)/shard_map/pallas_call | solution.py:136
  110.5 3.6 %collective-permute-done.24.refs_1_ = bf16[320,1408]{1,0:T(8,128)(2,1)S(1)} collective-permute-done((bf16[320,1408]{1,0:T(8,128)(2,1)S(1)}, bf16[320,1408]{1,0:T(8,128)(2,1)S(1)}, u32[]{:S(2)}, u32[]{:S(2)}) %collective-permute-start.24) | collective-permute-done | bytes 901152 | tf_op jit(solution)/shard_map/ppermute | solution.py:196
  114.2 4.0 %shard_map.39.refs_3_ = f32[640,1408]{1,0:T(8,128)S(1)} custom-call(bf16[2,640,1408]{2,1,0:T(8,128)(2,1)S(1)} %get-tuple-element.29.refs_0_, bf16[320,1408]{1,0:T(8,128)(2,1)S(1)} %collective-permute-done.15.refs_1_, bf16[320,1408]{1,0:T(8,128)(2,1)S(1)} %collective-permute-done.20.refs_2_, ...), custom_call_target="tpu_custom_call", output_to_operand_aliasing={{}: (3, {})} | custom-call | flops 1730150400 | bytes 12615680 | tf_op jit(solution)/shard_map/pallas_call | solution.py:136
  118.2 5.6 %collective-permute-done.19.refs_1_ = bf16[320,1408]{1,0:T(8,128)(2,1)S(1)} collective-permute-done((bf16[320,1408]{1,0:T(8,128)(2,1)S(1)}, bf16[320,1408]{1,0:T(8,128)(2,1)S(1)}, u32[]{:S(2)}, u32[]{:S(2)}) %collective-permute-start.19) | collective-permute-done | bytes 901152 | tf_op jit(solution)/shard_map/ppermute | solution.py:196
  126.4 4.0 %shard_map.40.refs_3_ = f32[640,1408]{1,0:T(8,128)S(1)} custom-call(bf16[2,640,1408]{2,1,0:T(8,128)(2,1)S(1)} %get-tuple-element.29.refs_0_, bf16[320,1408]{1,0:T(8,128)(2,1)S(1)} %collective-permute-done.24.refs_1_, bf16[320,1408]{1,0:T(8,128)(2,1)S(1)} %collective-permute-done.25.refs_2_, ...), custom_call_target="tpu_custom_call", output_to_operand_aliasing={{}: (3, {})} | custom-call | flops 1730150400 | bytes 12615680 | tf_op jit(solution)/shard_map/pallas_call | solution.py:136
  130.4 4.5 %shard_map.41 = bf16[640,1408]{1,0:T(8,128)(2,1)S(1)} custom-call(bf16[2,640,1408]{2,1,0:T(8,128)(2,1)S(1)} %get-tuple-element.29.refs_0_, bf16[320,1408]{1,0:T(8,128)(2,1)S(1)} %collective-permute-done.19.refs_1_, bf16[320,1408]{1,0:T(8,128)(2,1)S(1)} %collective-permute-done.23.refs_2_, f32[640,1408]{1,0:T(8,128)S(1)} %shard_map.40.refs_3_, ...), custom_call_target="tpu_custom_call" | custom-call | flops 1730150400 | bytes 12615680 | tf_op jit(solution)/shard_map/pallas_call | solution.py:136
  141.2 5.1 %collective-permute-done.28.refs_1_ = bf16[256,1408]{1,0:T(8,128)(2,1)S(1)} collective-permute-done((bf16[256,1408]{1,0:T(8,128)(2,1)S(1)}, bf16[256,1408]{1,0:T(8,128)(2,1)S(1)}, u32[]{:S(2)}, u32[]{:S(2)}) %collective-permute-start.28) | collective-permute-done | bytes 720928 | tf_op jit(solution)/shard_map/ppermute | solution.py:196
  146.3 7.8 %collective-permute-done.35.refs_1_ = bf16[256,1408]{1,0:T(8,128)(2,1)} collective-permute-done((bf16[256,1408]{1,0:T(8,128)(2,1)S(1)}, bf16[256,1408]{1,0:T(8,128)(2,1)}, u32[]{:S(2)}, u32[]{:S(2)}) %collective-permute-start.35) | collective-permute-done | bytes 720928 | tf_op jit(solution)/shard_map/ppermute | solution.py:196
  158.2 3.6 %collective-permute-done.33.refs_1_ = bf16[256,1408]{1,0:T(8,128)(2,1)} collective-permute-done((bf16[256,1408]{1,0:T(8,128)(2,1)S(1)}, bf16[256,1408]{1,0:T(8,128)(2,1)}, u32[]{:S(2)}, u32[]{:S(2)}) %collective-permute-start.33) | collective-permute-done | bytes 720928 | tf_op jit(solution)/shard_map/ppermute | solution.py:196
  166.4 3.0 %collective-permute-done.27.refs_1_ = bf16[256,1408]{1,0:T(8,128)(2,1)S(1)} collective-permute-done((bf16[256,1408]{1,0:T(8,128)(2,1)S(1)}, bf16[256,1408]{1,0:T(8,128)(2,1)S(1)}, u32[]{:S(2)}, u32[]{:S(2)}) %collective-permute-start.27) | collective-permute-done | bytes 720928 | tf_op jit(solution)/shard_map/ppermute | solution.py:196
  173.7 3.9 %shard_map.44.refs_3_ = f32[640,1408]{1,0:T(8,128)S(1)} custom-call(bf16[2,640,1408]{2,1,0:T(8,128)(2,1)S(1)} %copy-done.1, bf16[256,1408]{1,0:T(8,128)(2,1)} %collective-permute-done.35.refs_1_, bf16[256,1408]{1,0:T(8,128)(2,1)} %collective-permute-done.36.refs_2_, f32[640,1408]{1,0:T(8,128)S(1)} %copy-done.4), custom_call_target="tpu_custom_call", output_to_operand_aliasing={{}: (3, {})} | custom-call | flops 1384120320 | bytes 12255232 | tf_op jit(solution)/shard_map/pallas_call | solution.py:136
  177.7 4.1 %shard_map.45.refs_3_ = f32[640,1408]{1,0:T(8,128)S(1)} custom-call(bf16[2,640,1408]{2,1,0:T(8,128)(2,1)S(1)} %copy-done.1, bf16[256,1408]{1,0:T(8,128)(2,1)} %collective-permute-done.33.refs_1_, bf16[256,1408]{1,0:T(8,128)(2,1)} %collective-permute-done.34.refs_2_, f32[640,1408]{1,0:T(8,128)S(1)} %shard_map.44.refs_3_), custom_call_target="tpu_custom_call", output_to_operand_aliasing={{}: (3, {})} | custom-call | flops 1384120320 | bytes 12255232 | tf_op jit(solution)/shard_map/pallas_call | solution.py:136
  181.8 4.1 %shard_map.46 = f32[640,1408]{1,0:T(8,128)S(1)} custom-call(bf16[2,640,1408]{2,1,0:T(8,128)(2,1)S(1)} %copy-done.2, bf16[256,1408]{1,0:T(8,128)(2,1)S(1)} %collective-permute-done.27.refs_1_, bf16[256,1408]{1,0:T(8,128)(2,1)} %collective-permute-done.32.refs_2_, f32[640,1408]{1,0:T(8,128)S(1)} %shard_map.45.refs_3_, ...), custom_call_target="tpu_custom_call", output_to_operand_aliasing={{}: (3, {})} | custom-call | flops 1384120320 | bytes 12255232 | tf_op jit(solution)/shard_map/pallas_call | solution.py:136
  186.0 3.9 %add_multiply_fusion = f32[640,1408]{1,0:T(8,128)} fusion(f32[640,1408]{1,0:T(8,128)S(1)} %shard_map.46, bf16[640,1408]{1,0:T(8,128)(2,1)} %collective-permute-done.26, bf16[640,1408]{1,0:T(8,128)(2,1)S(1)} %shard_map.41, f32[640]{0:T(1024)S(1)} %reduce), kind=kLoop, calls=%fused_computation | loop fusion | flops 4505600 | bytes 10816000 | tf_op jit(solution)/shard_map/mul | solution.py:233
  (86 shorter events, 48.4 us)
Async XLA Ops:
  3.2 14.5 %collective-permute-start.4 = (bf16[320,1408]{1,0:T(8,128)(2,1)}, bf16[320,1408]{1,0:T(8,128)(2,1)}, u32[]{:S(2)}, u32[]{:S(2)}) collective-permute-start(bf16[320,1408]{1,0:T(8,128)(2,1)} %shard_map.28.refs_1_), channel_id=1, source_target_pairs={{0,8},{10,2},{8,16},{18,10},{16,24},{26,18},{24,28},{30,26},{28,20... | collective-permute-start | bytes 2703368 | tf_op jit(solution)/shard_map/ppermute | solution.py:196
  9.4 17.9 %collective-permute-start = (bf16[320,1408]{1,0:T(8,128)(2,1)}, bf16[320,1408]{1,0:T(8,128)(2,1)S(1)}, u32[]{:S(2)}, u32[]{:S(2)}) collective-permute-start(bf16[320,1408]{1,0:T(8,128)(2,1)} %shard_map.29.refs_2_), channel_id=1, source_target_pairs={{0,8},{10,2},{8,16},{18,10},{16,24},{26,18},{24,28},{30,26},{28,20... | collective-permute-start | bytes 2703368 | tf_op jit(solution)/shard_map/ppermute | solution.py:196
  11.0 16.3 %collective-permute-start.2 = (bf16[320,1408]{1,0:T(8,128)(2,1)S(1)}, bf16[320,1408]{1,0:T(8,128)(2,1)S(1)}, u32[]{:S(2)}, u32[]{:S(2)}) collective-permute-start(bf16[320,1408]{1,0:T(8,128)(2,1)S(1)} %copy-done.8), channel_id=1, source_target_pairs={{0,2},{2,0},{4,6},{6,4},{8,10},{10,8},{12,14},{14,12},{16,18},{18,... | collective-permute-start | bytes 2703368 | tf_op jit(solution)/shard_map/ppermute | solution.py:196
  17.7 19.2 %collective-permute-start.9 = (bf16[320,1408]{1,0:T(8,128)(2,1)}, bf16[320,1408]{1,0:T(8,128)(2,1)S(1)}, u32[]{:S(2)}, u32[]{:S(2)}) collective-permute-start(bf16[320,1408]{1,0:T(8,128)(2,1)} %collective-permute-done.4.refs_5_), channel_id=1, source_target_pairs={{0,8},{10,2},{8,16},{18,10},{16,24},{26,18},{24,28},{30,26},{28,20... | collective-permute-start | bytes 2703368 | tf_op jit(solution)/shard_map/ppermute | solution.py:196
  19.7 17.2 %collective-permute-start.3 = (bf16[320,1408]{1,0:T(8,128)(2,1)}, bf16[320,1408]{1,0:T(8,128)(2,1)S(1)}, u32[]{:S(2)}, u32[]{:S(2)}) collective-permute-start(bf16[320,1408]{1,0:T(8,128)(2,1)} %shard_map.29.refs_2_), channel_id=1, source_target_pairs={{0,2},{2,0},{4,6},{6,4},{8,10},{10,8},{12,14},{14,12},{16,18},{18,... | collective-permute-start | bytes 2703368 | tf_op jit(solution)/shard_map/ppermute | solution.py:196
  19.8 19.2 %collective-permute-start.5 = (bf16[320,1408]{1,0:T(8,128)(2,1)}, bf16[320,1408]{1,0:T(8,128)(2,1)S(1)}, u32[]{:S(2)}, u32[]{:S(2)}) collective-permute-start(bf16[320,1408]{1,0:T(8,128)(2,1)} %collective-permute-done.4.refs_5_), channel_id=1, source_target_pairs={{0,2},{2,0},{4,6},{6,4},{8,10},{10,8},{12,14},{14,12},{16,18},{18,... | collective-permute-start | bytes 2703368 | tf_op jit(solution)/shard_map/ppermute | solution.py:196
  27.3 11.7 %collective-permute-start.6 = (bf16[320,1408]{1,0:T(8,128)(2,1)S(1)}, bf16[320,1408]{1,0:T(8,128)(2,1)S(1)}, u32[]{:S(2)}, u32[]{:S(2)}) collective-permute-start(bf16[320,1408]{1,0:T(8,128)(2,1)S(1)} %collective-permute-done.refs_7_), channel_id=1, source_target_pairs={{0,2},{2,0},{4,6},{6,4},{8,10},{10,8},{12,14},{14,12},{16,18},{18,... | collective-permute-start | bytes 2703368 | tf_op jit(solution)/shard_map/ppermute | solution.py:196
  27.3 22.9 %collective-permute-start.1 = (bf16[320,1408]{1,0:T(8,128)(2,1)S(1)}, bf16[320,1408]{1,0:T(8,128)(2,1)S(1)}, u32[]{:S(2)}, u32[]{:S(2)}) collective-permute-start(bf16[320,1408]{1,0:T(8,128)(2,1)S(1)} %collective-permute-done.refs_7_), channel_id=1, source_target_pairs={{0,8},{10,2},{8,16},{18,10},{16,24},{26,18},{24,28},{30,26},{28,20... | collective-permute-start | bytes 2703368 | tf_op jit(solution)/shard_map/ppermute | solution.py:196
  36.9 15.0 %collective-permute-start.10 = (bf16[320,1408]{1,0:T(8,128)(2,1)S(1)}, bf16[320,1408]{1,0:T(8,128)(2,1)S(1)}, u32[]{:S(2)}, u32[]{:S(2)}) collective-permute-start(bf16[320,1408]{1,0:T(8,128)(2,1)S(1)} %collective-permute-done.9.refs_1_), channel_id=1, source_target_pairs={{0,2},{2,0},{4,6},{6,4},{8,10},{10,8},{12,14},{14,12},{16,18},{18,... | collective-permute-start | bytes 2703368 | tf_op jit(solution)/shard_map/ppermute | solution.py:196
  36.9 19.3 %collective-permute-start.13 = (bf16[320,1408]{1,0:T(8,128)(2,1)S(1)}, bf16[320,1408]{1,0:T(8,128)(2,1)S(1)}, u32[]{:S(2)}, u32[]{:S(2)}) collective-permute-start(bf16[320,1408]{1,0:T(8,128)(2,1)S(1)} %collective-permute-done.9.refs_1_), channel_id=1, source_target_pairs={{0,8},{10,2},{8,16},{18,10},{16,24},{26,18},{24,28},{30,26},{28,20... | collective-permute-start | bytes 2703368 | tf_op jit(solution)/shard_map/ppermute | solution.py:196
  50.5 15.4 %collective-permute-start.7 = (bf16[320,1408]{1,0:T(8,128)(2,1)S(1)}, bf16[320,1408]{1,0:T(8,128)(2,1)S(1)}, u32[]{:S(2)}, u32[]{:S(2)}) collective-permute-start(bf16[320,1408]{1,0:T(8,128)(2,1)S(1)} %collective-permute-done.1.refs_1_), channel_id=1, source_target_pairs={{0,8},{10,2},{8,16},{18,10},{16,24},{26,18},{24,28},{30,26},{28,20... | collective-permute-start | bytes 2703368 | tf_op jit(solution)/shard_map/ppermute | solution.py:196
  56.3 11.7 %collective-permute-start.14 = (bf16[320,1408]{1,0:T(8,128)(2,1)S(1)}, bf16[320,1408]{1,0:T(8,128)(2,1)S(1)}, u32[]{:S(2)}, u32[]{:S(2)}) collective-permute-start(bf16[320,1408]{1,0:T(8,128)(2,1)S(1)} %collective-permute-done.13.refs_1_), channel_id=1, source_target_pairs={{0,2},{2,0},{4,6},{6,4},{8,10},{10,8},{12,14},{14,12},{16,18},{18,... | collective-permute-start | bytes 2703368 | tf_op jit(solution)/shard_map/ppermute | solution.py:196
  56.3 19.3 %collective-permute-start.17 = (bf16[320,1408]{1,0:T(8,128)(2,1)S(1)}, bf16[320,1408]{1,0:T(8,128)(2,1)S(1)}, u32[]{:S(2)}, u32[]{:S(2)}) collective-permute-start(bf16[320,1408]{1,0:T(8,128)(2,1)S(1)} %collective-permute-done.13.refs_1_), channel_id=1, source_target_pairs={{0,8},{10,2},{8,16},{18,10},{16,24},{26,18},{24,28},{30,26},{28,20... | collective-permute-start | bytes 2703368 | tf_op jit(solution)/shard_map/ppermute | solution.py:196
  65.9 11.7 %collective-permute-start.12 = (bf16[320,1408]{1,0:T(8,128)(2,1)S(1)}, bf16[320,1408]{1,0:T(8,128)(2,1)S(1)}, u32[]{:S(2)}, u32[]{:S(2)}) collective-permute-start(bf16[320,1408]{1,0:T(8,128)(2,1)S(1)} %collective-permute-done.7.refs_1_), channel_id=1, source_target_pairs={{0,2},{2,0},{4,6},{6,4},{8,10},{10,8},{12,14},{14,12},{16,18},{18,... | collective-permute-start | bytes 2703368 | tf_op jit(solution)/shard_map/ppermute | solution.py:196
  65.9 19.3 %collective-permute-start.11 = (bf16[320,1408]{1,0:T(8,128)(2,1)S(1)}, bf16[320,1408]{1,0:T(8,128)(2,1)S(1)}, u32[]{:S(2)}, u32[]{:S(2)}) collective-permute-start(bf16[320,1408]{1,0:T(8,128)(2,1)S(1)} %collective-permute-done.7.refs_1_), channel_id=1, source_target_pairs={{0,8},{10,2},{8,16},{18,10},{16,24},{26,18},{24,28},{30,26},{28,20... | collective-permute-start | bytes 2703368 | tf_op jit(solution)/shard_map/ppermute | solution.py:196
  75.6 11.7 %collective-permute-start.18 = (bf16[320,1408]{1,0:T(8,128)(2,1)S(1)}, bf16[320,1408]{1,0:T(8,128)(2,1)S(1)}, u32[]{:S(2)}, u32[]{:S(2)}) collective-permute-start(bf16[320,1408]{1,0:T(8,128)(2,1)S(1)} %collective-permute-done.17.refs_1_), channel_id=1, source_target_pairs={{0,2},{2,0},{4,6},{6,4},{8,10},{10,8},{12,14},{14,12},{16,18},{18,... | collective-permute-start | bytes 2703368 | tf_op jit(solution)/shard_map/ppermute | solution.py:196
  75.6 19.3 %collective-permute-start.21 = (bf16[320,1408]{1,0:T(8,128)(2,1)S(1)}, bf16[320,1408]{1,0:T(8,128)(2,1)S(1)}, u32[]{:S(2)}, u32[]{:S(2)}) collective-permute-start(bf16[320,1408]{1,0:T(8,128)(2,1)S(1)} %collective-permute-done.17.refs_1_), channel_id=1, source_target_pairs={{0,8},{10,2},{8,16},{18,10},{16,24},{26,18},{24,28},{30,26},{28,20... | collective-permute-start | bytes 2703368 | tf_op jit(solution)/shard_map/ppermute | solution.py:196
  85.2 19.3 %collective-permute-start.15 = (bf16[320,1408]{1,0:T(8,128)(2,1)S(1)}, bf16[320,1408]{1,0:T(8,128)(2,1)S(1)}, u32[]{:S(2)}, u32[]{:S(2)}) collective-permute-start(bf16[320,1408]{1,0:T(8,128)(2,1)S(1)} %collective-permute-done.11.refs_1_), channel_id=1, source_target_pairs={{0,8},{10,2},{8,16},{18,10},{16,24},{26,18},{24,28},{30,26},{28,20... | collective-permute-start | bytes 2703368 | tf_op jit(solution)/shard_map/ppermute | solution.py:196
  94.9 11.7 %collective-permute-start.22 = (bf16[320,1408]{1,0:T(8,128)(2,1)S(1)}, bf16[320,1408]{1,0:T(8,128)(2,1)S(1)}, u32[]{:S(2)}, u32[]{:S(2)}) collective-permute-start(bf16[320,1408]{1,0:T(8,128)(2,1)S(1)} %collective-permute-done.21.refs_1_), channel_id=1, source_target_pairs={{0,2},{2,0},{4,6},{6,4},{8,10},{10,8},{12,14},{14,12},{16,18},{18,... | collective-permute-start | bytes 2703368 | tf_op jit(solution)/shard_map/ppermute | solution.py:196
  94.9 19.3 %collective-permute-start.24 = (bf16[320,1408]{1,0:T(8,128)(2,1)S(1)}, bf16[320,1408]{1,0:T(8,128)(2,1)S(1)}, u32[]{:S(2)}, u32[]{:S(2)}) collective-permute-start(bf16[320,1408]{1,0:T(8,128)(2,1)S(1)} %collective-permute-done.21.refs_1_), channel_id=1, source_target_pairs={{0,8},{10,2},{8,16},{18,10},{16,24},{26,18},{24,28},{30,26},{28,20... | collective-permute-start | bytes 2703368 | tf_op jit(solution)/shard_map/ppermute | solution.py:196
  104.5 19.3 %collective-permute-start.19 = (bf16[320,1408]{1,0:T(8,128)(2,1)S(1)}, bf16[320,1408]{1,0:T(8,128)(2,1)S(1)}, u32[]{:S(2)}, u32[]{:S(2)}) collective-permute-start(bf16[320,1408]{1,0:T(8,128)(2,1)S(1)} %collective-permute-done.15.refs_1_), channel_id=1, source_target_pairs={{0,8},{10,2},{8,16},{18,10},{16,24},{26,18},{24,28},{30,26},{28,20... | collective-permute-start | bytes 2703368 | tf_op jit(solution)/shard_map/ppermute | solution.py:196
  114.2 12.2 %collective-permute-start.25 = (bf16[320,1408]{1,0:T(8,128)(2,1)S(1)}, bf16[320,1408]{1,0:T(8,128)(2,1)S(1)}, u32[]{:S(2)}, u32[]{:S(2)}) collective-permute-start(bf16[320,1408]{1,0:T(8,128)(2,1)S(1)} %collective-permute-done.24.refs_1_), channel_id=1, source_target_pairs={{0,2},{2,0},{4,6},{6,4},{8,10},{10,8},{12,14},{14,12},{16,18},{18,... | collective-permute-start | bytes 2703368 | tf_op jit(solution)/shard_map/ppermute | solution.py:196
  124.2 14.0 %collective-permute-start.30 = (bf16[256,1408]{1,0:T(8,128)(2,1)S(1)}, bf16[256,1408]{1,0:T(8,128)(2,1)S(1)}, u32[]{:S(2)}, u32[]{:S(2)}) collective-permute-start(bf16[256,1408]{1,0:T(8,128)(2,1)S(1)} %bitcast.10), channel_id=1, source_target_pairs={{8,0},{2,10},{16,8},{10,18},{24,16},{18,26},{28,24},{26,30},{20,28... | collective-permute-start | bytes 2162696 | tf_op jit(solution)/shard_map/ppermute | solution.py:196
  136.6 17.5 %collective-permute-start.35 = (bf16[256,1408]{1,0:T(8,128)(2,1)S(1)}, bf16[256,1408]{1,0:T(8,128)(2,1)}, u32[]{:S(2)}, u32[]{:S(2)}) collective-permute-start(bf16[256,1408]{1,0:T(8,128)(2,1)S(1)} %bitcast.8), channel_id=1, source_target_pairs={{8,0},{2,10},{16,8},{10,18},{24,16},{18,26},{28,24},{26,30},{20,28... | collective-permute-start | bytes 2162696 | tf_op jit(solution)/shard_map/ppermute | solution.py:196
  138.1 17.5 %collective-permute-start.31 = (bf16[256,1408]{1,0:T(8,128)(2,1)S(1)}, bf16[256,1408]{1,0:T(8,128)(2,1)S(1)}, u32[]{:S(2)}, u32[]{:S(2)}) collective-permute-start(bf16[256,1408]{1,0:T(8,128)(2,1)S(1)} %collective-permute-done.30.refs_1_), channel_id=1, source_target_pairs={{0,2},{2,0},{4,6},{6,4},{8,10},{10,8},{12,14},{14,12},{16,18},{18,... | collective-permute-start | bytes 2162696 | tf_op jit(solution)/shard_map/ppermute | solution.py:196
  138.2 47.8 %collective-permute-start.26 = (bf16[640,1408]{1,0:T(8,128)(2,1)S(1)}, bf16[640,1408]{1,0:T(8,128)(2,1)}, u32[]{:S(2)}, u32[]{:S(2)}) collective-permute-start(bf16[640,1408]{1,0:T(8,128)(2,1)S(1)} %shard_map.41), channel_id=1, source_target_pairs={{0,1},{1,0},{2,3},{3,2},{4,5},{5,4},{6,7},{7,6},{8,9},{9,8},{10,11... | collective-permute-start | bytes 5406728 | tf_op jit(solution)/shard_map/ppermute | solution.py:218
  139.6 22.2 %collective-permute-start.33 = (bf16[256,1408]{1,0:T(8,128)(2,1)S(1)}, bf16[256,1408]{1,0:T(8,128)(2,1)}, u32[]{:S(2)}, u32[]{:S(2)}) collective-permute-start(bf16[256,1408]{1,0:T(8,128)(2,1)S(1)} %bitcast.7), channel_id=1, source_target_pairs={{8,0},{2,10},{16,8},{10,18},{24,16},{18,26},{28,24},{26,30},{20,28... | collective-permute-start | bytes 2162696 | tf_op jit(solution)/shard_map/ppermute | solution.py:196
  146.3 15.6 %collective-permute-start.29 = (bf16[256,1408]{1,0:T(8,128)(2,1)S(1)}, bf16[256,1408]{1,0:T(8,128)(2,1)S(1)}, u32[]{:S(2)}, u32[]{:S(2)}) collective-permute-start(bf16[256,1408]{1,0:T(8,128)(2,1)S(1)} %collective-permute-done.28.refs_1_), channel_id=1, source_target_pairs={{0,2},{2,0},{4,6},{6,4},{8,10},{10,8},{12,14},{14,12},{16,18},{18,... | collective-permute-start | bytes 2162696 | tf_op jit(solution)/shard_map/ppermute | solution.py:196
  154.1 15.3 %collective-permute-start.27 = (bf16[256,1408]{1,0:T(8,128)(2,1)S(1)}, bf16[256,1408]{1,0:T(8,128)(2,1)S(1)}, u32[]{:S(2)}, u32[]{:S(2)}) collective-permute-start(bf16[256,1408]{1,0:T(8,128)(2,1)S(1)} %bitcast.6), channel_id=1, source_target_pairs={{8,0},{2,10},{16,8},{10,18},{24,16},{18,26},{28,24},{26,30},{20,28... | collective-permute-start | bytes 2162696 | tf_op jit(solution)/shard_map/ppermute | solution.py:196
  155.7 13.9 %collective-permute-start.36 = (bf16[256,1408]{1,0:T(8,128)(2,1)}, bf16[256,1408]{1,0:T(8,128)(2,1)}, u32[]{:S(2)}, u32[]{:S(2)}) collective-permute-start(bf16[256,1408]{1,0:T(8,128)(2,1)} %collective-permute-done.35.refs_1_), channel_id=1, source_target_pairs={{0,2},{2,0},{4,6},{6,4},{8,10},{10,8},{12,14},{14,12},{16,18},{18,... | collective-permute-start | bytes 2162696 | tf_op jit(solution)/shard_map/ppermute | solution.py:196
  161.8 15.8 %collective-permute-start.34 = (bf16[256,1408]{1,0:T(8,128)(2,1)}, bf16[256,1408]{1,0:T(8,128)(2,1)}, u32[]{:S(2)}, u32[]{:S(2)}) collective-permute-start(bf16[256,1408]{1,0:T(8,128)(2,1)} %collective-permute-done.33.refs_1_), channel_id=1, source_target_pairs={{0,2},{2,0},{4,6},{6,4},{8,10},{10,8},{12,14},{14,12},{16,18},{18,... | collective-permute-start | bytes 2162696 | tf_op jit(solution)/shard_map/ppermute | solution.py:196
  169.5 12.3 %collective-permute-start.32 = (bf16[256,1408]{1,0:T(8,128)(2,1)S(1)}, bf16[256,1408]{1,0:T(8,128)(2,1)}, u32[]{:S(2)}, u32[]{:S(2)}) collective-permute-start(bf16[256,1408]{1,0:T(8,128)(2,1)S(1)} %collective-permute-done.27.refs_1_), channel_id=1, source_target_pairs={{0,2},{2,0},{4,6},{6,4},{8,10},{10,8},{12,14},{14,12},{16,18},{18,... | collective-permute-start | bytes 2162696 | tf_op jit(solution)/shard_map/ppermute | solution.py:196
  (16 other events, 235.5 us)

commit v5 on v4

--- a/solution.py
+++ b/solution.py
@@ -18,7 +18,7 @@
 BLAG = 2
 COSTW = 1.0
 ROW_TILE = 16
-VMEM_LIMIT = 32 * 1024 * 1024
+VMEM_LIMIT = 14 * 1024 * 1024
 FIRST_VMEM_LIMIT = 58 * 1024 * 1024
 
 

time: 190 us -> 193 us (1.016)
    unnamed x22 -> x24, local copies, waits for them, and re-layouts: 9.02 us -> 10.8 us
where the time goes in v5:
time: 193 us
  Pallas kernels  75.6 us (39%)
  waiting for transfers between devices  65.6 us (34%)
  starting transfers between devices  35 us (18%)
  local copies, waits for them, and re-layouts  11.1 us (6%)
  other arithmetic  5.17 us (3%)
    pallas_call x16, Pallas kernels, add_relation(): pl.pallas_call(functools.partial(relation_kernel, margin, weight, counts,...  68 us
    ppermute x36, waiting for transfers between devices, move(): return lax.ppermute(after(x, *wait_for), 'seq', route)  65.6 us
    ppermute x36, starting transfers between devices, move(): return lax.ppermute(after(x, *wait_for), 'seq', route)  33.5 us
    unnamed x24, local copies, waits for them, and re-layouts  10.8 us
    pallas_call x2, Pallas kernels, pack_share(): pl.pallas_call(functools.partial(pack_kernel, counts, at), grid_spec=pltp...  6.38 us
    mul x1, other arithmetic, local(): return s_scale * (summed + sums[-1])  5 us
  transfers between devices with their start and end apart: 37, of which 15 were waited for; matrix products, arithmetic and copies ran while one was open for 0% of the time, Pallas kernels for 38%

profile of v5, /device:TPU:0, one launch (start us, length us, event | category | flops | bytes accessed | tf_op | source)
XLA Modules:
  0.0 192.8 jit_solution(1395538759284847234)
XLA Ops:
  0.0 3.2 %shard_map.28.refs_1_ = bf16[320,1408]{1,0:T(8,128)(2,1)} custom-call(s32[1]{0:T(128)} %bitcast.which, f32[640,1408]{1,0:T(8,128)} %refs_4_.3, f32[640,1408]{1,0:T(8,128)} %teacher.5), custom_call_target="tpu_custom_call" | custom-call | flops 2703360 | bytes 5406720 | tf_op jit(solution)/shard_map/pallas_call | solution.py:69
  3.2 3.0 %collective-permute-start.4 = (bf16[320,1408]{1,0:T(8,128)(2,1)}, bf16[320,1408]{1,0:T(8,128)(2,1)}, u32[]{:S(2)}, u32[]{:S(2)}) collective-permute-start(bf16[320,1408]{1,0:T(8,128)(2,1)} %shard_map.28.refs_1_), channel_id=1, source_target_pairs={{0,8},{10,2},{8,16},{18,10},{16,24},{26,18},{24,28},{30,26},{28,20... | collective-permute-start | bytes 2703368 | tf_op jit(solution)/shard_map/ppermute | solution.py:196
  6.2 3.2 %shard_map.29.refs_2_ = bf16[320,1408]{1,0:T(8,128)(2,1)} custom-call(s32[1]{0:T(128)} %bitcast.which, f32[640,1408]{1,0:T(8,128)} %refs_4_.3, f32[640,1408]{1,0:T(8,128)} %teacher.5), custom_call_target="tpu_custom_call" | custom-call | flops 2703360 | bytes 5406720 | tf_op jit(solution)/shard_map/pallas_call | solution.py:69
  11.0 6.8 %collective-permute-done.4.refs_5_ = bf16[320,1408]{1,0:T(8,128)(2,1)} collective-permute-done((bf16[320,1408]{1,0:T(8,128)(2,1)}, bf16[320,1408]{1,0:T(8,128)(2,1)}, u32[]{:S(2)}, u32[]{:S(2)}) %collective-permute-start.4) | collective-permute-done | bytes 901152 | tf_op jit(solution)/shard_map/ppermute | solution.py:196
  20.3 7.0 %collective-permute-done.refs_7_ = bf16[320,1408]{1,0:T(8,128)(2,1)S(1)} collective-permute-done((bf16[320,1408]{1,0:T(8,128)(2,1)}, bf16[320,1408]{1,0:T(8,128)(2,1)S(1)}, u32[]{:S(2)}, u32[]{:S(2)}) %collective-permute-start) | collective-permute-done | bytes 901152 | tf_op jit(solution)/shard_map/ppermute | solution.py:196
  32.6 4.4 %collective-permute-done.9.refs_1_ = bf16[320,1408]{1,0:T(8,128)(2,1)S(1)} collective-permute-done((bf16[320,1408]{1,0:T(8,128)(2,1)}, bf16[320,1408]{1,0:T(8,128)(2,1)S(1)}, u32[]{:S(2)}, u32[]{:S(2)}) %collective-permute-start.9) | collective-permute-done | bytes 901152 | tf_op jit(solution)/shard_map/ppermute | solution.py:196
  40.2 10.1 %shard_map.31.refs_3_ = f32[640,1408]{1,0:T(8,128)S(1)} custom-call(bf16[2,640,1408]{2,1,0:T(8,128)(2,1)S(1)} %get-tuple-element.29.refs_0_, bf16[320,1408]{1,0:T(8,128)(2,1)S(1)} %copy-done.10, bf16[320,1408]{1,0:T(8,128)(2,1)S(1)} %copy-done.11, bf16[320,1408]{1,0:T(8,128)(2,1)S(1)} %collective-permute-done.2.refs_3_, ...), custom_call_target="tpu_custom_call" | custom-call | flops 6920601600 | bytes 18022400 | tf_op jit(solution)/shard_map/pallas_call | solution.py:136
  51.9 4.0 %shard_map.32.refs_3_ = f32[640,1408]{1,0:T(8,128)S(1)} custom-call(bf16[2,640,1408]{2,1,0:T(8,128)(2,1)S(1)} %get-tuple-element.29.refs_0_, bf16[320,1408]{1,0:T(8,128)(2,1)S(1)} %collective-permute-done.9.refs_1_, bf16[320,1408]{1,0:T(8,128)(2,1)S(1)} %collective-permute-done.10.refs_2_, ...), custom_call_target="tpu_custom_call", output_to_operand_aliasing={{}: (3, {})} | custom-call | flops 1730150400 | bytes 12615680 | tf_op jit(solution)/shard_map/pallas_call | solution.py:136
  58.3 4.0 %shard_map.33.refs_3_ = f32[640,1408]{1,0:T(8,128)S(1)} custom-call(bf16[2,640,1408]{2,1,0:T(8,128)(2,1)S(1)} %get-tuple-element.29.refs_0_, bf16[320,1408]{1,0:T(8,128)(2,1)S(1)} %collective-permute-done.1.refs_1_, bf16[320,1408]{1,0:T(8,128)(2,1)S(1)} %collective-permute-done.8.refs_2_, ...), custom_call_target="tpu_custom_call", output_to_operand_aliasing={{}: (3, {})} | custom-call | flops 1730150400 | bytes 12615680 | tf_op jit(solution)/shard_map/pallas_call | solution.py:136
  62.3 3.6 %collective-permute-done.7.refs_1_ = bf16[320,1408]{1,0:T(8,128)(2,1)S(1)} collective-permute-done((bf16[320,1408]{1,0:T(8,128)(2,1)S(1)}, bf16[320,1408]{1,0:T(8,128)(2,1)S(1)}, u32[]{:S(2)}, u32[]{:S(2)}) %collective-permute-start.7) | collective-permute-done | bytes 901152 | tf_op jit(solution)/shard_map/ppermute | solution.py:196
  67.9 4.0 %shard_map.34.refs_3_ = f32[640,1408]{1,0:T(8,128)S(1)} custom-call(bf16[2,640,1408]{2,1,0:T(8,128)(2,1)S(1)} %get-tuple-element.29.refs_0_, bf16[320,1408]{1,0:T(8,128)(2,1)S(1)} %collective-permute-done.13.refs_1_, bf16[320,1408]{1,0:T(8,128)(2,1)S(1)} %collective-permute-done.14.refs_2_, ...), custom_call_target="tpu_custom_call", output_to_operand_aliasing={{}: (3, {})} | custom-call | flops 1730150400 | bytes 12615680 | tf_op jit(solution)/shard_map/pallas_call | solution.py:136
  71.9 3.6 %collective-permute-done.17.refs_1_ = bf16[320,1408]{1,0:T(8,128)(2,1)S(1)} collective-permute-done((bf16[320,1408]{1,0:T(8,128)(2,1)S(1)}, bf16[320,1408]{1,0:T(8,128)(2,1)S(1)}, u32[]{:S(2)}, u32[]{:S(2)}) %collective-permute-start.17) | collective-permute-done | bytes 901152 | tf_op jit(solution)/shard_map/ppermute | solution.py:196
  77.6 4.0 %shard_map.35.refs_3_ = f32[640,1408]{1,0:T(8,128)S(1)} custom-call(bf16[2,640,1408]{2,1,0:T(8,128)(2,1)S(1)} %get-tuple-element.29.refs_0_, bf16[320,1408]{1,0:T(8,128)(2,1)S(1)} %collective-permute-done.7.refs_1_, bf16[320,1408]{1,0:T(8,128)(2,1)S(1)} %collective-permute-done.12.refs_2_, ...), custom_call_target="tpu_custom_call", output_to_operand_aliasing={{}: (3, {})} | custom-call | flops 1730150400 | bytes 12615680 | tf_op jit(solution)/shard_map/pallas_call | solution.py:136
  81.6 3.6 %collective-permute-done.11.refs_1_ = bf16[320,1408]{1,0:T(8,128)(2,1)S(1)} collective-permute-done((bf16[320,1408]{1,0:T(8,128)(2,1)S(1)}, bf16[320,1408]{1,0:T(8,128)(2,1)S(1)}, u32[]{:S(2)}, u32[]{:S(2)}) %collective-permute-start.11) | collective-permute-done | bytes 901152 | tf_op jit(solution)/shard_map/ppermute | solution.py:196
  87.2 4.0 %shard_map.36.refs_3_ = f32[640,1408]{1,0:T(8,128)S(1)} custom-call(bf16[2,640,1408]{2,1,0:T(8,128)(2,1)S(1)} %get-tuple-element.29.refs_0_, bf16[320,1408]{1,0:T(8,128)(2,1)S(1)} %collective-permute-done.17.refs_1_, bf16[320,1408]{1,0:T(8,128)(2,1)S(1)} %collective-permute-done.18.refs_2_, ...), custom_call_target="tpu_custom_call", output_to_operand_aliasing={{}: (3, {})} | custom-call | flops 1730150400 | bytes 12615680 | tf_op jit(solution)/shard_map/pallas_call | solution.py:136
  91.2 3.6 %collective-permute-done.21.refs_1_ = bf16[320,1408]{1,0:T(8,128)(2,1)S(1)} collective-permute-done((bf16[320,1408]{1,0:T(8,128)(2,1)S(1)}, bf16[320,1408]{1,0:T(8,128)(2,1)S(1)}, u32[]{:S(2)}, u32[]{:S(2)}) %collective-permute-start.21) | collective-permute-done | bytes 901152 | tf_op jit(solution)/shard_map/ppermute | solution.py:196
  96.9 4.0 %shard_map.37.refs_3_ = f32[640,1408]{1,0:T(8,128)S(1)} custom-call(bf16[2,640,1408]{2,1,0:T(8,128)(2,1)S(1)} %get-tuple-element.29.refs_0_, bf16[320,1408]{1,0:T(8,128)(2,1)S(1)} %collective-permute-done.11.refs_1_, bf16[320,1408]{1,0:T(8,128)(2,1)S(1)} %collective-permute-done.16.refs_2_, ...), custom_call_target="tpu_custom_call", output_to_operand_aliasing={{}: (3, {})} | custom-call | flops 1730150400 | bytes 12615680 | tf_op jit(solution)/shard_map/pallas_call | solution.py:136
  100.9 3.6 %collective-permute-done.15.refs_1_ = bf16[320,1408]{1,0:T(8,128)(2,1)S(1)} collective-permute-done((bf16[320,1408]{1,0:T(8,128)(2,1)S(1)}, bf16[320,1408]{1,0:T(8,128)(2,1)S(1)}, u32[]{:S(2)}, u32[]{:S(2)}) %collective-permute-start.15) | collective-permute-done | bytes 901152 | tf_op jit(solution)/shard_map/ppermute | solution.py:196
  106.6 4.0 %shard_map.38.refs_3_ = f32[640,1408]{1,0:T(8,128)S(1)} custom-call(bf16[2,640,1408]{2,1,0:T(8,128)(2,1)S(1)} %get-tuple-element.29.refs_0_, bf16[320,1408]{1,0:T(8,128)(2,1)S(1)} %collective-permute-done.21.refs_1_, bf16[320,1408]{1,0:T(8,128)(2,1)S(1)} %collective-permute-done.22.refs_2_, ...), custom_call_target="tpu_custom_call", output_to_operand_aliasing={{}: (3, {})} | custom-call | flops 1730150400 | bytes 12615680 | tf_op jit(solution)/shard_map/pallas_call | solution.py:136
  110.6 3.6 %collective-permute-done.24.refs_1_ = bf16[320,1408]{1,0:T(8,128)(2,1)S(1)} collective-permute-done((bf16[320,1408]{1,0:T(8,128)(2,1)S(1)}, bf16[320,1408]{1,0:T(8,128)(2,1)S(1)}, u32[]{:S(2)}, u32[]{:S(2)}) %collective-permute-start.24) | collective-permute-done | bytes 901152 | tf_op jit(solution)/shard_map/ppermute | solution.py:196
  114.2 4.0 %shard_map.39.refs_3_ = f32[640,1408]{1,0:T(8,128)S(1)} custom-call(bf16[2,640,1408]{2,1,0:T(8,128)(2,1)S(1)} %get-tuple-element.29.refs_0_, bf16[320,1408]{1,0:T(8,128)(2,1)S(1)} %collective-permute-done.15.refs_1_, bf16[320,1408]{1,0:T(8,128)(2,1)S(1)} %collective-permute-done.20.refs_2_, ...), custom_call_target="tpu_custom_call", output_to_operand_aliasing={{}: (3, {})} | custom-call | flops 1730150400 | bytes 12615680 | tf_op jit(solution)/shard_map/pallas_call | solution.py:136
  118.2 5.6 %collective-permute-done.19.refs_1_ = bf16[320,1408]{1,0:T(8,128)(2,1)S(1)} collective-permute-done((bf16[320,1408]{1,0:T(8,128)(2,1)S(1)}, bf16[320,1408]{1,0:T(8,128)(2,1)S(1)}, u32[]{:S(2)}, u32[]{:S(2)}) %collective-permute-start.19) | collective-permute-done | bytes 901152 | tf_op jit(solution)/shard_map/ppermute | solution.py:196
  126.4 4.0 %shard_map.40.refs_3_ = f32[640,1408]{1,0:T(8,128)S(1)} custom-call(bf16[2,640,1408]{2,1,0:T(8,128)(2,1)S(1)} %get-tuple-element.29.refs_0_, bf16[320,1408]{1,0:T(8,128)(2,1)S(1)} %collective-permute-done.24.refs_1_, bf16[320,1408]{1,0:T(8,128)(2,1)S(1)} %collective-permute-done.25.refs_2_, ...), custom_call_target="tpu_custom_call", output_to_operand_aliasing={{}: (3, {})} | custom-call | flops 1730150400 | bytes 12615680 | tf_op jit(solution)/shard_map/pallas_call | solution.py:136
  130.4 4.5 %shard_map.41 = bf16[640,1408]{1,0:T(8,128)(2,1)S(1)} custom-call(bf16[2,640,1408]{2,1,0:T(8,128)(2,1)S(1)} %get-tuple-element.29.refs_0_, bf16[320,1408]{1,0:T(8,128)(2,1)S(1)} %collective-permute-done.19.refs_1_, bf16[320,1408]{1,0:T(8,128)(2,1)S(1)} %collective-permute-done.23.refs_2_, f32[640,1408]{1,0:T(8,128)S(1)} %shard_map.40.refs_3_, ...), custom_call_target="tpu_custom_call" | custom-call | flops 1730150400 | bytes 12615680 | tf_op jit(solution)/shard_map/pallas_call | solution.py:136
  141.2 5.1 %collective-permute-done.28.refs_1_ = bf16[256,1408]{1,0:T(8,128)(2,1)S(1)} collective-permute-done((bf16[256,1408]{1,0:T(8,128)(2,1)S(1)}, bf16[256,1408]{1,0:T(8,128)(2,1)S(1)}, u32[]{:S(2)}, u32[]{:S(2)}) %collective-permute-start.28) | collective-permute-done | bytes 720928 | tf_op jit(solution)/shard_map/ppermute | solution.py:196
  146.3 7.8 %collective-permute-done.35.refs_1_ = bf16[256,1408]{1,0:T(8,128)(2,1)} collective-permute-done((bf16[256,1408]{1,0:T(8,128)(2,1)S(1)}, bf16[256,1408]{1,0:T(8,128)(2,1)}, u32[]{:S(2)}, u32[]{:S(2)}) %collective-permute-start.35) | collective-permute-done | bytes 720928 | tf_op jit(solution)/shard_map/ppermute | solution.py:196
  158.2 3.6 %collective-permute-done.33.refs_1_ = bf16[256,1408]{1,0:T(8,128)(2,1)} collective-permute-done((bf16[256,1408]{1,0:T(8,128)(2,1)S(1)}, bf16[256,1408]{1,0:T(8,128)(2,1)}, u32[]{:S(2)}, u32[]{:S(2)}) %collective-permute-start.33) | collective-permute-done | bytes 720928 | tf_op jit(solution)/shard_map/ppermute | solution.py:196
  166.4 3.0 %collective-permute-done.27.refs_1_ = bf16[256,1408]{1,0:T(8,128)(2,1)S(1)} collective-permute-done((bf16[256,1408]{1,0:T(8,128)(2,1)S(1)}, bf16[256,1408]{1,0:T(8,128)(2,1)S(1)}, u32[]{:S(2)}, u32[]{:S(2)}) %collective-permute-start.27) | collective-permute-done | bytes 720928 | tf_op jit(solution)/shard_map/ppermute | solution.py:196
  173.7 3.9 %shard_map.44.refs_3_ = f32[640,1408]{1,0:T(8,128)S(1)} custom-call(bf16[2,640,1408]{2,1,0:T(8,128)(2,1)S(1)} %copy-done.1, bf16[256,1408]{1,0:T(8,128)(2,1)} %collective-permute-done.35.refs_1_, bf16[256,1408]{1,0:T(8,128)(2,1)} %collective-permute-done.36.refs_2_, f32[640,1408]{1,0:T(8,128)S(1)} %copy-done.4), custom_call_target="tpu_custom_call", output_to_operand_aliasing={{}: (3, {})} | custom-call | flops 1384120320 | bytes 12255232 | tf_op jit(solution)/shard_map/pallas_call | solution.py:136
  177.7 4.1 %shard_map.45.refs_3_ = f32[640,1408]{1,0:T(8,128)S(1)} custom-call(bf16[2,640,1408]{2,1,0:T(8,128)(2,1)S(1)} %copy-done.1, bf16[256,1408]{1,0:T(8,128)(2,1)} %collective-permute-done.33.refs_1_, bf16[256,1408]{1,0:T(8,128)(2,1)} %collective-permute-done.34.refs_2_, f32[640,1408]{1,0:T(8,128)S(1)} %shard_map.44.refs_3_), custom_call_target="tpu_custom_call", output_to_operand_aliasing={{}: (3, {})} | custom-call | flops 1384120320 | bytes 12255232 | tf_op jit(solution)/shard_map/pallas_call | solution.py:136
  181.9 4.1 %shard_map.46 = f32[640,1408]{1,0:T(8,128)S(1)} custom-call(bf16[2,640,1408]{2,1,0:T(8,128)(2,1)S(1)} %copy-done.2, bf16[256,1408]{1,0:T(8,128)(2,1)S(1)} %collective-permute-done.27.refs_1_, bf16[256,1408]{1,0:T(8,128)(2,1)} %collective-permute-done.32.refs_2_, f32[640,1408]{1,0:T(8,128)S(1)} %shard_map.45.refs_3_, ...), custom_call_target="tpu_custom_call", output_to_operand_aliasing={{}: (3, {})} | custom-call | flops 1384120320 | bytes 12255232 | tf_op jit(solution)/shard_map/pallas_call | solution.py:136
  187.8 5.0 %add_multiply_fusion = f32[640,1408]{1,0:T(8,128)} fusion(f32[640,1408]{1,0:T(8,128)} %copy-done.5, bf16[640,1408]{1,0:T(8,128)(2,1)} %collective-permute-done.26, bf16[640,1408]{1,0:T(8,128)(2,1)S(1)} %shard_map.41, f32[640]{0:T(1024)S(1)} %reduce), kind=kLoop, calls=%fused_computation | loop fusion | flops 4505600 | bytes 10816000 | tf_op jit(solution)/shard_map/mul | solution.py:233
  (88 shorter events, 50.2 us)
Async XLA Ops:
  3.2 14.5 %collective-permute-start.4 = (bf16[320,1408]{1,0:T(8,128)(2,1)}, bf16[320,1408]{1,0:T(8,128)(2,1)}, u32[]{:S(2)}, u32[]{:S(2)}) collective-permute-start(bf16[320,1408]{1,0:T(8,128)(2,1)} %shard_map.28.refs_1_), channel_id=1, source_target_pairs={{0,8},{10,2},{8,16},{18,10},{16,24},{26,18},{24,28},{30,26},{28,20... | collective-permute-start | bytes 2703368 | tf_op jit(solution)/shard_map/ppermute | solution.py:196
  9.4 17.9 %collective-permute-start = (bf16[320,1408]{1,0:T(8,128)(2,1)}, bf16[320,1408]{1,0:T(8,128)(2,1)S(1)}, u32[]{:S(2)}, u32[]{:S(2)}) collective-permute-start(bf16[320,1408]{1,0:T(8,128)(2,1)} %shard_map.29.refs_2_), channel_id=1, source_target_pairs={{0,8},{10,2},{8,16},{18,10},{16,24},{26,18},{24,28},{30,26},{28,20... | collective-permute-start | bytes 2703368 | tf_op jit(solution)/shard_map/ppermute | solution.py:196
  11.0 16.3 %collective-permute-start.2 = (bf16[320,1408]{1,0:T(8,128)(2,1)S(1)}, bf16[320,1408]{1,0:T(8,128)(2,1)S(1)}, u32[]{:S(2)}, u32[]{:S(2)}) collective-permute-start(bf16[320,1408]{1,0:T(8,128)(2,1)S(1)} %copy-done.9), channel_id=1, source_target_pairs={{0,2},{2,0},{4,6},{6,4},{8,10},{10,8},{12,14},{14,12},{16,18},{18,... | collective-permute-start | bytes 2703368 | tf_op jit(solution)/shard_map/ppermute | solution.py:196
  17.7 19.2 %collective-permute-start.9 = (bf16[320,1408]{1,0:T(8,128)(2,1)}, bf16[320,1408]{1,0:T(8,128)(2,1)S(1)}, u32[]{:S(2)}, u32[]{:S(2)}) collective-permute-start(bf16[320,1408]{1,0:T(8,128)(2,1)} %collective-permute-done.4.refs_5_), channel_id=1, source_target_pairs={{0,8},{10,2},{8,16},{18,10},{16,24},{26,18},{24,28},{30,26},{28,20... | collective-permute-start | bytes 2703368 | tf_op jit(solution)/shard_map/ppermute | solution.py:196
  19.8 17.2 %collective-permute-start.3 = (bf16[320,1408]{1,0:T(8,128)(2,1)}, bf16[320,1408]{1,0:T(8,128)(2,1)S(1)}, u32[]{:S(2)}, u32[]{:S(2)}) collective-permute-start(bf16[320,1408]{1,0:T(8,128)(2,1)} %shard_map.29.refs_2_), channel_id=1, source_target_pairs={{0,2},{2,0},{4,6},{6,4},{8,10},{10,8},{12,14},{14,12},{16,18},{18,... | collective-permute-start | bytes 2703368 | tf_op jit(solution)/shard_map/ppermute | solution.py:196
  19.8 19.2 %collective-permute-start.5 = (bf16[320,1408]{1,0:T(8,128)(2,1)}, bf16[320,1408]{1,0:T(8,128)(2,1)S(1)}, u32[]{:S(2)}, u32[]{:S(2)}) collective-permute-start(bf16[320,1408]{1,0:T(8,128)(2,1)} %collective-permute-done.4.refs_5_), channel_id=1, source_target_pairs={{0,2},{2,0},{4,6},{6,4},{8,10},{10,8},{12,14},{14,12},{16,18},{18,... | collective-permute-start | bytes 2703368 | tf_op jit(solution)/shard_map/ppermute | solution.py:196
  27.3 11.7 %collective-permute-start.6 = (bf16[320,1408]{1,0:T(8,128)(2,1)S(1)}, bf16[320,1408]{1,0:T(8,128)(2,1)S(1)}, u32[]{:S(2)}, u32[]{:S(2)}) collective-permute-start(bf16[320,1408]{1,0:T(8,128)(2,1)S(1)} %collective-permute-done.refs_7_), channel_id=1, source_target_pairs={{0,2},{2,0},{4,6},{6,4},{8,10},{10,8},{12,14},{14,12},{16,18},{18,... | collective-permute-start | bytes 2703368 | tf_op jit(solution)/shard_map/ppermute | solution.py:196
  27.3 22.9 %collective-permute-start.1 = (bf16[320,1408]{1,0:T(8,128)(2,1)S(1)}, bf16[320,1408]{1,0:T(8,128)(2,1)S(1)}, u32[]{:S(2)}, u32[]{:S(2)}) collective-permute-start(bf16[320,1408]{1,0:T(8,128)(2,1)S(1)} %collective-permute-done.refs_7_), channel_id=1, source_target_pairs={{0,8},{10,2},{8,16},{18,10},{16,24},{26,18},{24,28},{30,26},{28,20... | collective-permute-start | bytes 2703368 | tf_op jit(solution)/shard_map/ppermute | solution.py:196
  37.0 15.0 %collective-permute-start.10 = (bf16[320,1408]{1,0:T(8,128)(2,1)S(1)}, bf16[320,1408]{1,0:T(8,128)(2,1)S(1)}, u32[]{:S(2)}, u32[]{:S(2)}) collective-permute-start(bf16[320,1408]{1,0:T(8,128)(2,1)S(1)} %collective-permute-done.9.refs_1_), channel_id=1, source_target_pairs={{0,2},{2,0},{4,6},{6,4},{8,10},{10,8},{12,14},{14,12},{16,18},{18,... | collective-permute-start | bytes 2703368 | tf_op jit(solution)/shard_map/ppermute | solution.py:196
  37.0 19.3 %collective-permute-start.13 = (bf16[320,1408]{1,0:T(8,128)(2,1)S(1)}, bf16[320,1408]{1,0:T(8,128)(2,1)S(1)}, u32[]{:S(2)}, u32[]{:S(2)}) collective-permute-start(bf16[320,1408]{1,0:T(8,128)(2,1)S(1)} %collective-permute-done.9.refs_1_), channel_id=1, source_target_pairs={{0,8},{10,2},{8,16},{18,10},{16,24},{26,18},{24,28},{30,26},{28,20... | collective-permute-start | bytes 2703368 | tf_op jit(solution)/shard_map/ppermute | solution.py:196
  50.5 15.4 %collective-permute-start.7 = (bf16[320,1408]{1,0:T(8,128)(2,1)S(1)}, bf16[320,1408]{1,0:T(8,128)(2,1)S(1)}, u32[]{:S(2)}, u32[]{:S(2)}) collective-permute-start(bf16[320,1408]{1,0:T(8,128)(2,1)S(1)} %collective-permute-done.1.refs_1_), channel_id=1, source_target_pairs={{0,8},{10,2},{8,16},{18,10},{16,24},{26,18},{24,28},{30,26},{28,20... | collective-permute-start | bytes 2703368 | tf_op jit(solution)/shard_map/ppermute | solution.py:196
  56.3 11.7 %collective-permute-start.14 = (bf16[320,1408]{1,0:T(8,128)(2,1)S(1)}, bf16[320,1408]{1,0:T(8,128)(2,1)S(1)}, u32[]{:S(2)}, u32[]{:S(2)}) collective-permute-start(bf16[320,1408]{1,0:T(8,128)(2,1)S(1)} %collective-permute-done.13.refs_1_), channel_id=1, source_target_pairs={{0,2},{2,0},{4,6},{6,4},{8,10},{10,8},{12,14},{14,12},{16,18},{18,... | collective-permute-start | bytes 2703368 | tf_op jit(solution)/shard_map/ppermute | solution.py:196
  56.3 19.3 %collective-permute-start.17 = (bf16[320,1408]{1,0:T(8,128)(2,1)S(1)}, bf16[320,1408]{1,0:T(8,128)(2,1)S(1)}, u32[]{:S(2)}, u32[]{:S(2)}) collective-permute-start(bf16[320,1408]{1,0:T(8,128)(2,1)S(1)} %collective-permute-done.13.refs_1_), channel_id=1, source_target_pairs={{0,8},{10,2},{8,16},{18,10},{16,24},{26,18},{24,28},{30,26},{28,20... | collective-permute-start | bytes 2703368 | tf_op jit(solution)/shard_map/ppermute | solution.py:196
  65.9 11.7 %collective-permute-start.12 = (bf16[320,1408]{1,0:T(8,128)(2,1)S(1)}, bf16[320,1408]{1,0:T(8,128)(2,1)S(1)}, u32[]{:S(2)}, u32[]{:S(2)}) collective-permute-start(bf16[320,1408]{1,0:T(8,128)(2,1)S(1)} %collective-permute-done.7.refs_1_), channel_id=1, source_target_pairs={{0,2},{2,0},{4,6},{6,4},{8,10},{10,8},{12,14},{14,12},{16,18},{18,... | collective-permute-start | bytes 2703368 | tf_op jit(solution)/shard_map/ppermute | solution.py:196
  65.9 19.3 %collective-permute-start.11 = (bf16[320,1408]{1,0:T(8,128)(2,1)S(1)}, bf16[320,1408]{1,0:T(8,128)(2,1)S(1)}, u32[]{:S(2)}, u32[]{:S(2)}) collective-permute-start(bf16[320,1408]{1,0:T(8,128)(2,1)S(1)} %collective-permute-done.7.refs_1_), channel_id=1, source_target_pairs={{0,8},{10,2},{8,16},{18,10},{16,24},{26,18},{24,28},{30,26},{28,20... | collective-permute-start | bytes 2703368 | tf_op jit(solution)/shard_map/ppermute | solution.py:196
  75.6 11.7 %collective-permute-start.18 = (bf16[320,1408]{1,0:T(8,128)(2,1)S(1)}, bf16[320,1408]{1,0:T(8,128)(2,1)S(1)}, u32[]{:S(2)}, u32[]{:S(2)}) collective-permute-start(bf16[320,1408]{1,0:T(8,128)(2,1)S(1)} %collective-permute-done.17.refs_1_), channel_id=1, source_target_pairs={{0,2},{2,0},{4,6},{6,4},{8,10},{10,8},{12,14},{14,12},{16,18},{18,... | collective-permute-start | bytes 2703368 | tf_op jit(solution)/shard_map/ppermute | solution.py:196
  75.6 19.3 %collective-permute-start.21 = (bf16[320,1408]{1,0:T(8,128)(2,1)S(1)}, bf16[320,1408]{1,0:T(8,128)(2,1)S(1)}, u32[]{:S(2)}, u32[]{:S(2)}) collective-permute-start(bf16[320,1408]{1,0:T(8,128)(2,1)S(1)} %collective-permute-done.17.refs_1_), channel_id=1, source_target_pairs={{0,8},{10,2},{8,16},{18,10},{16,24},{26,18},{24,28},{30,26},{28,20... | collective-permute-start | bytes 2703368 | tf_op jit(solution)/shard_map/ppermute | solution.py:196
  85.2 11.7 %collective-permute-start.16 = (bf16[320,1408]{1,0:T(8,128)(2,1)S(1)}, bf16[320,1408]{1,0:T(8,128)(2,1)S(1)}, u32[]{:S(2)}, u32[]{:S(2)}) collective-permute-start(bf16[320,1408]{1,0:T(8,128)(2,1)S(1)} %collective-permute-done.11.refs_1_), channel_id=1, source_target_pairs={{0,2},{2,0},{4,6},{6,4},{8,10},{10,8},{12,14},{14,12},{16,18},{18,... | collective-permute-start | bytes 2703368 | tf_op jit(solution)/shard_map/ppermute | solution.py:196
  85.2 19.3 %collective-permute-start.15 = (bf16[320,1408]{1,0:T(8,128)(2,1)S(1)}, bf16[320,1408]{1,0:T(8,128)(2,1)S(1)}, u32[]{:S(2)}, u32[]{:S(2)}) collective-permute-start(bf16[320,1408]{1,0:T(8,128)(2,1)S(1)} %collective-permute-done.11.refs_1_), channel_id=1, source_target_pairs={{0,8},{10,2},{8,16},{18,10},{16,24},{26,18},{24,28},{30,26},{28,20... | collective-permute-start | bytes 2703368 | tf_op jit(solution)/shard_map/ppermute | solution.py:196
  94.9 19.3 %collective-permute-start.24 = (bf16[320,1408]{1,0:T(8,128)(2,1)S(1)}, bf16[320,1408]{1,0:T(8,128)(2,1)S(1)}, u32[]{:S(2)}, u32[]{:S(2)}) collective-permute-start(bf16[320,1408]{1,0:T(8,128)(2,1)S(1)} %collective-permute-done.21.refs_1_), channel_id=1, source_target_pairs={{0,8},{10,2},{8,16},{18,10},{16,24},{26,18},{24,28},{30,26},{28,20... | collective-permute-start | bytes 2703368 | tf_op jit(solution)/shard_map/ppermute | solution.py:196
  104.5 19.3 %collective-permute-start.19 = (bf16[320,1408]{1,0:T(8,128)(2,1)S(1)}, bf16[320,1408]{1,0:T(8,128)(2,1)S(1)}, u32[]{:S(2)}, u32[]{:S(2)}) collective-permute-start(bf16[320,1408]{1,0:T(8,128)(2,1)S(1)} %collective-permute-done.15.refs_1_), channel_id=1, source_target_pairs={{0,8},{10,2},{8,16},{18,10},{16,24},{26,18},{24,28},{30,26},{28,20... | collective-permute-start | bytes 2703368 | tf_op jit(solution)/shard_map/ppermute | solution.py:196
  114.2 12.2 %collective-permute-start.25 = (bf16[320,1408]{1,0:T(8,128)(2,1)S(1)}, bf16[320,1408]{1,0:T(8,128)(2,1)S(1)}, u32[]{:S(2)}, u32[]{:S(2)}) collective-permute-start(bf16[320,1408]{1,0:T(8,128)(2,1)S(1)} %collective-permute-done.24.refs_1_), channel_id=1, source_target_pairs={{0,2},{2,0},{4,6},{6,4},{8,10},{10,8},{12,14},{14,12},{16,18},{18,... | collective-permute-start | bytes 2703368 | tf_op jit(solution)/shard_map/ppermute | solution.py:196
  124.2 14.0 %collective-permute-start.30 = (bf16[256,1408]{1,0:T(8,128)(2,1)S(1)}, bf16[256,1408]{1,0:T(8,128)(2,1)S(1)}, u32[]{:S(2)}, u32[]{:S(2)}) collective-permute-start(bf16[256,1408]{1,0:T(8,128)(2,1)S(1)} %bitcast.10), channel_id=1, source_target_pairs={{8,0},{2,10},{16,8},{10,18},{24,16},{18,26},{28,24},{26,30},{20,28... | collective-permute-start | bytes 2162696 | tf_op jit(solution)/shard_map/ppermute | solution.py:196
  136.6 17.5 %collective-permute-start.35 = (bf16[256,1408]{1,0:T(8,128)(2,1)S(1)}, bf16[256,1408]{1,0:T(8,128)(2,1)}, u32[]{:S(2)}, u32[]{:S(2)}) collective-permute-start(bf16[256,1408]{1,0:T(8,128)(2,1)S(1)} %bitcast.8), channel_id=1, source_target_pairs={{8,0},{2,10},{16,8},{10,18},{24,16},{18,26},{28,24},{26,30},{20,28... | collective-permute-start | bytes 2162696 | tf_op jit(solution)/shard_map/ppermute | solution.py:196
  138.2 17.5 %collective-permute-start.31 = (bf16[256,1408]{1,0:T(8,128)(2,1)S(1)}, bf16[256,1408]{1,0:T(8,128)(2,1)S(1)}, u32[]{:S(2)}, u32[]{:S(2)}) collective-permute-start(bf16[256,1408]{1,0:T(8,128)(2,1)S(1)} %collective-permute-done.30.refs_1_), channel_id=1, source_target_pairs={{0,2},{2,0},{4,6},{6,4},{8,10},{10,8},{12,14},{14,12},{16,18},{18,... | collective-permute-start | bytes 2162696 | tf_op jit(solution)/shard_map/ppermute | solution.py:196
  138.2 49.6 %collective-permute-start.26 = (bf16[640,1408]{1,0:T(8,128)(2,1)S(1)}, bf16[640,1408]{1,0:T(8,128)(2,1)}, u32[]{:S(2)}, u32[]{:S(2)}) collective-permute-start(bf16[640,1408]{1,0:T(8,128)(2,1)S(1)} %shard_map.41), channel_id=1, source_target_pairs={{0,1},{1,0},{2,3},{3,2},{4,5},{5,4},{6,7},{7,6},{8,9},{9,8},{10,11... | collective-permute-start | bytes 5406728 | tf_op jit(solution)/shard_map/ppermute | solution.py:218
  139.7 22.2 %collective-permute-start.33 = (bf16[256,1408]{1,0:T(8,128)(2,1)S(1)}, bf16[256,1408]{1,0:T(8,128)(2,1)}, u32[]{:S(2)}, u32[]{:S(2)}) collective-permute-start(bf16[256,1408]{1,0:T(8,128)(2,1)S(1)} %bitcast.7), channel_id=1, source_target_pairs={{8,0},{2,10},{16,8},{10,18},{24,16},{18,26},{28,24},{26,30},{20,28... | collective-permute-start | bytes 2162696 | tf_op jit(solution)/shard_map/ppermute | solution.py:196
  146.3 15.6 %collective-permute-start.29 = (bf16[256,1408]{1,0:T(8,128)(2,1)S(1)}, bf16[256,1408]{1,0:T(8,128)(2,1)S(1)}, u32[]{:S(2)}, u32[]{:S(2)}) collective-permute-start(bf16[256,1408]{1,0:T(8,128)(2,1)S(1)} %collective-permute-done.28.refs_1_), channel_id=1, source_target_pairs={{0,2},{2,0},{4,6},{6,4},{8,10},{10,8},{12,14},{14,12},{16,18},{18,... | collective-permute-start | bytes 2162696 | tf_op jit(solution)/shard_map/ppermute | solution.py:196
  154.1 15.3 %collective-permute-start.27 = (bf16[256,1408]{1,0:T(8,128)(2,1)S(1)}, bf16[256,1408]{1,0:T(8,128)(2,1)S(1)}, u32[]{:S(2)}, u32[]{:S(2)}) collective-permute-start(bf16[256,1408]{1,0:T(8,128)(2,1)S(1)} %bitcast.6), channel_id=1, source_target_pairs={{8,0},{2,10},{16,8},{10,18},{24,16},{18,26},{28,24},{26,30},{20,28... | collective-permute-start | bytes 2162696 | tf_op jit(solution)/shard_map/ppermute | solution.py:196
  155.7 13.9 %collective-permute-start.36 = (bf16[256,1408]{1,0:T(8,128)(2,1)}, bf16[256,1408]{1,0:T(8,128)(2,1)}, u32[]{:S(2)}, u32[]{:S(2)}) collective-permute-start(bf16[256,1408]{1,0:T(8,128)(2,1)} %collective-permute-done.35.refs_1_), channel_id=1, source_target_pairs={{0,2},{2,0},{4,6},{6,4},{8,10},{10,8},{12,14},{14,12},{16,18},{18,... | collective-permute-start | bytes 2162696 | tf_op jit(solution)/shard_map/ppermute | solution.py:196
  161.9 15.8 %collective-permute-start.34 = (bf16[256,1408]{1,0:T(8,128)(2,1)}, bf16[256,1408]{1,0:T(8,128)(2,1)}, u32[]{:S(2)}, u32[]{:S(2)}) collective-permute-start(bf16[256,1408]{1,0:T(8,128)(2,1)} %collective-permute-done.33.refs_1_), channel_id=1, source_target_pairs={{0,2},{2,0},{4,6},{6,4},{8,10},{10,8},{12,14},{14,12},{16,18},{18,... | collective-permute-start | bytes 2162696 | tf_op jit(solution)/shard_map/ppermute | solution.py:196
  169.5 12.3 %collective-permute-start.32 = (bf16[256,1408]{1,0:T(8,128)(2,1)S(1)}, bf16[256,1408]{1,0:T(8,128)(2,1)}, u32[]{:S(2)}, u32[]{:S(2)}) collective-permute-start(bf16[256,1408]{1,0:T(8,128)(2,1)S(1)} %collective-permute-done.27.refs_1_), channel_id=1, source_target_pairs={{0,2},{2,0},{4,6},{6,4},{8,10},{10,8},{12,14},{14,12},{16,18},{18,... | collective-permute-start | bytes 2162696 | tf_op jit(solution)/shard_map/ppermute | solution.py:196
  (17 other events, 237.3 us)

commit v6 on v3

--- a/solution.py
+++ b/solution.py
@@ -212,9 +212,8 @@
         route = [(i, i ^ distance) for i in range(pair_count)]
         summands = (value, lax.ppermute(value, "pair", route))
         distance *= 2
-    summed = sum(x.astype(jnp.float32) for x in summands)
     if not doubled:
-        return s_scale * summed
+        return s_scale * sum(x.astype(jnp.float32) for x in summands)
 
     nearest, at = [], 0
     for k, n in enumerate(split(rows, PARTS)):
@@ -226,8 +225,7 @@
         batch += [x, move(x, swap, own)]
     total = add(batch, None)
     batch = [nearest[-1], move(nearest[-1], swap)]
-    total = add(batch, total, project=(student, s_scale))
-    return s_scale * (summed + total)
+    return add(batch, total, project=(student, s_scale), summands=summands)
 
 
 def solution(mesh):

time: 190 us -> 189 us (level)
  waiting for transfers between devices: 77 us -> 81.2 us
  other arithmetic: 4.08 us -> 0 us
  local copies, waits for them, and re-layouts: 4.33 us -> 2.3 us
    ppermute x1, waiting for transfers between devices: 0.01 us -> 4.22 us  [local(): summands = (value, lax.ppermute(value, 'pair', route))]
    mul x1 -> x0, other arithmetic: 3.91 us -> none  [local(): return s_scale * (summed + total)]
    unnamed x16 -> x8, local copies, waits for them, and re-layouts: 4.06 us -> 2.03 us
  transfers between devices with their start and end apart: 35 -> 35, of which waited for: 14 -> 15; matrix products, arithmetic and copies ran while one was open for 0% -> 0% of each run, Pallas kernels for 35% -> 31%
where the time goes in v6:
time: 189 us; the launch traced here: 188 us
  waiting for transfers between devices  81.2 us (43%)
  Pallas kernels  70.6 us (37%)
  starting transfers between devices  34.2 us (18%)
  local copies, waits for them, and re-layouts  2.3 us (1%)
    ppermute x34, waiting for transfers between devices, move(): return lax.ppermute(after(x, *wait_for), 'seq', route)  77 us
    pallas_call x13, Pallas kernels, add_relation(): pl.pallas_call(functools.partial(relation_kernel, margin, weight, counts,...  65.6 us
    ppermute x34, starting transfers between devices, move(): return lax.ppermute(after(x, *wait_for), 'seq', route)  32.7 us
    ppermute x1, waiting for transfers between devices, local(): summands = (value, lax.ppermute(value, 'pair', route))  4.22 us
  transfers between devices with their start and end apart: 35, of which 15 were waited for; matrix products, arithmetic and copies ran while one was open for 0% of the time, Pallas kernels for 31%

profile of v6, /device:TPU:0, one launch (start us, length us, event | category | flops | bytes accessed | tf_op | source)
XLA Modules:
  0.0 188.4 jit_solution(6706900539807763640)
XLA Ops:
  0.0 3.7 %shard_map.28 = (bf16[320,1408]{1,0:T(8,128)(2,1)}, bf16[320,1408]{1,0:T(8,128)(2,1)}) custom-call(s32[1]{0:T(128)} %bitcast.which, f32[640,1408]{1,0:T(8,128)} %refs_4_.3, f32[640,1408]{1,0:T(8,128)} %teacher.3), custom_call_target="tpu_custom_call" | custom-call | flops 2703360 | bytes 5406720 | tf_op jit(solution)/shard_map/pallas_call | solution.py:68
  3.7 3.0 %collective-permute-start.4 = (bf16[320,1408]{1,0:T(8,128)(2,1)}, bf16[320,1408]{1,0:T(8,128)(2,1)S(1)}, u32[]{:S(2)}, u32[]{:S(2)}) collective-permute-start(bf16[320,1408]{1,0:T(8,128)(2,1)} %get-tuple-element.26.refs_1_), channel_id=1, source_target_pairs={{0,8},{10,2},{8,16},{18,10},{16,24},{26,18},{24,28},{30,26},{28,20... | collective-permute-start | bytes 2703368 | tf_op jit(solution)/shard_map/ppermute | solution.py:191
  8.4 9.8 %collective-permute-done.4.refs_5_ = bf16[320,1408]{1,0:T(8,128)(2,1)S(1)} collective-permute-done((bf16[320,1408]{1,0:T(8,128)(2,1)}, bf16[320,1408]{1,0:T(8,128)(2,1)S(1)}, u32[]{:S(2)}, u32[]{:S(2)}) %collective-permute-start.4) | collective-permute-done | bytes 901152 | tf_op jit(solution)/shard_map/ppermute | solution.py:191
  20.7 7.1 %collective-permute-done.refs_7_ = bf16[320,1408]{1,0:T(8,128)(2,1)S(1)} collective-permute-done((bf16[320,1408]{1,0:T(8,128)(2,1)}, bf16[320,1408]{1,0:T(8,128)(2,1)S(1)}, u32[]{:S(2)}, u32[]{:S(2)}) %collective-permute-start) | collective-permute-done | bytes 901152 | tf_op jit(solution)/shard_map/ppermute | solution.py:191
  27.8 2.1 %collective-permute-start.1 = (bf16[320,1408]{1,0:T(8,128)(2,1)S(1)}, bf16[320,1408]{1,0:T(8,128)(2,1)S(1)}, u32[]{:S(2)}, u32[]{:S(2)}) collective-permute-start(bf16[320,1408]{1,0:T(8,128)(2,1)S(1)} %collective-permute-done.refs_7_), channel_id=1, source_target_pairs={{0,8},{10,2},{8,16},{18,10},{16,24},{26,18},{24,28},{30,26},{28,20... | collective-permute-start | bytes 2703368 | tf_op jit(solution)/shard_map/ppermute | solution.py:191
  33.1 4.3 %collective-permute-done.9.refs_1_ = bf16[320,1408]{1,0:T(8,128)(2,1)S(1)} collective-permute-done((bf16[320,1408]{1,0:T(8,128)(2,1)S(1)}, bf16[320,1408]{1,0:T(8,128)(2,1)S(1)}, u32[]{:S(2)}, u32[]{:S(2)}) %collective-permute-start.9) | collective-permute-done | bytes 901152 | tf_op jit(solution)/shard_map/ppermute | solution.py:191
  39.5 9.0 %shard_map.30.refs_3_ = f32[640,1408]{1,0:T(8,128)S(1)} custom-call(bf16[2,640,1408]{2,1,0:T(8,128)(2,1)S(1)} %get-tuple-element.29.refs_0_, bf16[320,1408]{1,0:T(8,128)(2,1)S(1)} %copy-done.2, bf16[320,1408]{1,0:T(8,128)(2,1)S(1)} %copy-done.3, bf16[320,1408]{1,0:T(8,128)(2,1)S(1)} %collective-permute-done.2.refs_3_, ...), custom_call_target="tpu_custom_call" | custom-call | flops 6920601600 | bytes 18022400 | tf_op jit(solution)/shard_map/pallas_call | solution.py:135
  50.3 4.0 %shard_map.31.refs_3_ = f32[640,1408]{1,0:T(8,128)S(1)} custom-call(bf16[2,640,1408]{2,1,0:T(8,128)(2,1)S(1)} %get-tuple-element.29.refs_0_, bf16[320,1408]{1,0:T(8,128)(2,1)S(1)} %collective-permute-done.9.refs_1_, bf16[320,1408]{1,0:T(8,128)(2,1)S(1)} %collective-permute-done.10.refs_2_, ...), custom_call_target="tpu_custom_call", output_to_operand_aliasing={{}: (3, {})} | custom-call | flops 1730150400 | bytes 12615680 | tf_op jit(solution)/shard_map/pallas_call | solution.py:135
  54.3 2.4 %collective-permute-done.13.refs_1_ = bf16[320,1408]{1,0:T(8,128)(2,1)S(1)} collective-permute-done((bf16[320,1408]{1,0:T(8,128)(2,1)S(1)}, bf16[320,1408]{1,0:T(8,128)(2,1)S(1)}, u32[]{:S(2)}, u32[]{:S(2)}) %collective-permute-start.13) | collective-permute-done | bytes 901152 | tf_op jit(solution)/shard_map/ppermute | solution.py:191
  58.8 4.0 %shard_map.32.refs_3_ = f32[640,1408]{1,0:T(8,128)S(1)} custom-call(bf16[2,640,1408]{2,1,0:T(8,128)(2,1)S(1)} %get-tuple-element.29.refs_0_, bf16[320,1408]{1,0:T(8,128)(2,1)S(1)} %collective-permute-done.1.refs_1_, bf16[320,1408]{1,0:T(8,128)(2,1)S(1)} %collective-permute-done.8.refs_2_, ...), custom_call_target="tpu_custom_call", output_to_operand_aliasing={{}: (3, {})} | custom-call | flops 1730150400 | bytes 12615680 | tf_op jit(solution)/shard_map/pallas_call | solution.py:135
  62.8 3.6 %collective-permute-done.7.refs_1_ = bf16[320,1408]{1,0:T(8,128)(2,1)S(1)} collective-permute-done((bf16[320,1408]{1,0:T(8,128)(2,1)S(1)}, bf16[320,1408]{1,0:T(8,128)(2,1)S(1)}, u32[]{:S(2)}, u32[]{:S(2)}) %collective-permute-start.7) | collective-permute-done | bytes 901152 | tf_op jit(solution)/shard_map/ppermute | solution.py:191
  68.5 4.0 %shard_map.33.refs_3_ = f32[640,1408]{1,0:T(8,128)S(1)} custom-call(bf16[2,640,1408]{2,1,0:T(8,128)(2,1)S(1)} %get-tuple-element.29.refs_0_, bf16[320,1408]{1,0:T(8,128)(2,1)S(1)} %collective-permute-done.13.refs_1_, bf16[320,1408]{1,0:T(8,128)(2,1)S(1)} %collective-permute-done.14.refs_2_, ...), custom_call_target="tpu_custom_call", output_to_operand_aliasing={{}: (3, {})} | custom-call | flops 1730150400 | bytes 12615680 | tf_op jit(solution)/shard_map/pallas_call | solution.py:135
  72.5 3.6 %collective-permute-done.17.refs_1_ = bf16[320,1408]{1,0:T(8,128)(2,1)S(1)} collective-permute-done((bf16[320,1408]{1,0:T(8,128)(2,1)S(1)}, bf16[320,1408]{1,0:T(8,128)(2,1)S(1)}, u32[]{:S(2)}, u32[]{:S(2)}) %collective-permute-start.17) | collective-permute-done | bytes 901152 | tf_op jit(solution)/shard_map/ppermute | solution.py:191
  78.1 4.0 %shard_map.34.refs_3_ = f32[640,1408]{1,0:T(8,128)S(1)} custom-call(bf16[2,640,1408]{2,1,0:T(8,128)(2,1)S(1)} %get-tuple-element.29.refs_0_, bf16[320,1408]{1,0:T(8,128)(2,1)S(1)} %collective-permute-done.7.refs_1_, bf16[320,1408]{1,0:T(8,128)(2,1)S(1)} %collective-permute-done.12.refs_2_, ...), custom_call_target="tpu_custom_call", output_to_operand_aliasing={{}: (3, {})} | custom-call | flops 1730150400 | bytes 12615680 | tf_op jit(solution)/shard_map/pallas_call | solution.py:135
  82.1 3.6 %collective-permute-done.11.refs_1_ = bf16[320,1408]{1,0:T(8,128)(2,1)S(1)} collective-permute-done((bf16[320,1408]{1,0:T(8,128)(2,1)S(1)}, bf16[320,1408]{1,0:T(8,128)(2,1)S(1)}, u32[]{:S(2)}, u32[]{:S(2)}) %collective-permute-start.11) | collective-permute-done | bytes 901152 | tf_op jit(solution)/shard_map/ppermute | solution.py:191
  87.8 4.0 %shard_map.35.refs_3_ = f32[640,1408]{1,0:T(8,128)S(1)} custom-call(bf16[2,640,1408]{2,1,0:T(8,128)(2,1)S(1)} %get-tuple-element.29.refs_0_, bf16[320,1408]{1,0:T(8,128)(2,1)S(1)} %collective-permute-done.17.refs_1_, bf16[320,1408]{1,0:T(8,128)(2,1)S(1)} %collective-permute-done.18.refs_2_, ...), custom_call_target="tpu_custom_call", output_to_operand_aliasing={{}: (3, {})} | custom-call | flops 1730150400 | bytes 12615680 | tf_op jit(solution)/shard_map/pallas_call | solution.py:135
  91.8 3.6 %collective-permute-done.21.refs_1_ = bf16[320,1408]{1,0:T(8,128)(2,1)S(1)} collective-permute-done((bf16[320,1408]{1,0:T(8,128)(2,1)S(1)}, bf16[320,1408]{1,0:T(8,128)(2,1)S(1)}, u32[]{:S(2)}, u32[]{:S(2)}) %collective-permute-start.21) | collective-permute-done | bytes 901152 | tf_op jit(solution)/shard_map/ppermute | solution.py:191
  97.5 4.0 %shard_map.36.refs_3_ = f32[640,1408]{1,0:T(8,128)S(1)} custom-call(bf16[2,640,1408]{2,1,0:T(8,128)(2,1)S(1)} %get-tuple-element.29.refs_0_, bf16[320,1408]{1,0:T(8,128)(2,1)S(1)} %collective-permute-done.11.refs_1_, bf16[320,1408]{1,0:T(8,128)(2,1)S(1)} %collective-permute-done.16.refs_2_, ...), custom_call_target="tpu_custom_call", output_to_operand_aliasing={{}: (3, {})} | custom-call | flops 1730150400 | bytes 12615680 | tf_op jit(solution)/shard_map/pallas_call | solution.py:135
  101.5 3.6 %collective-permute-done.15.refs_1_ = bf16[320,1408]{1,0:T(8,128)(2,1)S(1)} collective-permute-done((bf16[320,1408]{1,0:T(8,128)(2,1)S(1)}, bf16[320,1408]{1,0:T(8,128)(2,1)S(1)}, u32[]{:S(2)}, u32[]{:S(2)}) %collective-permute-start.15) | collective-permute-done | bytes 901152 | tf_op jit(solution)/shard_map/ppermute | solution.py:191
  107.1 4.0 %shard_map.37.refs_3_ = f32[640,1408]{1,0:T(8,128)S(1)} custom-call(bf16[2,640,1408]{2,1,0:T(8,128)(2,1)S(1)} %get-tuple-element.29.refs_0_, bf16[320,1408]{1,0:T(8,128)(2,1)S(1)} %collective-permute-done.21.refs_1_, bf16[320,1408]{1,0:T(8,128)(2,1)S(1)} %collective-permute-done.22.refs_2_, ...), custom_call_target="tpu_custom_call", output_to_operand_aliasing={{}: (3, {})} | custom-call | flops 1730150400 | bytes 12615680 | tf_op jit(solution)/shard_map/pallas_call | solution.py:135
  111.1 3.6 %collective-permute-done.24.refs_1_ = bf16[320,1408]{1,0:T(8,128)(2,1)S(1)} collective-permute-done((bf16[320,1408]{1,0:T(8,128)(2,1)S(1)}, bf16[320,1408]{1,0:T(8,128)(2,1)S(1)}, u32[]{:S(2)}, u32[]{:S(2)}) %collective-permute-start.24) | collective-permute-done | bytes 901152 | tf_op jit(solution)/shard_map/ppermute | solution.py:191
  114.7 4.0 %shard_map.38.refs_3_ = f32[640,1408]{1,0:T(8,128)S(1)} custom-call(bf16[2,640,1408]{2,1,0:T(8,128)(2,1)S(1)} %get-tuple-element.29.refs_0_, bf16[320,1408]{1,0:T(8,128)(2,1)S(1)} %collective-permute-done.15.refs_1_, bf16[320,1408]{1,0:T(8,128)(2,1)S(1)} %collective-permute-done.20.refs_2_, ...), custom_call_target="tpu_custom_call", output_to_operand_aliasing={{}: (3, {})} | custom-call | flops 1730150400 | bytes 12615680 | tf_op jit(solution)/shard_map/pallas_call | solution.py:135
  118.7 5.7 %collective-permute-done.19.refs_1_ = bf16[320,1408]{1,0:T(8,128)(2,1)S(1)} collective-permute-done((bf16[320,1408]{1,0:T(8,128)(2,1)S(1)}, bf16[320,1408]{1,0:T(8,128)(2,1)S(1)}, u32[]{:S(2)}, u32[]{:S(2)}) %collective-permute-start.19) | collective-permute-done | bytes 901152 | tf_op jit(solution)/shard_map/ppermute | solution.py:191
  124.6 2.3 %collective-permute-start.28 = (bf16[320,1408]{1,0:T(8,128)(2,1)S(1)}, bf16[320,1408]{1,0:T(8,128)(2,1)S(1)}, u32[]{:S(2)}, u32[]{:S(2)}) collective-permute-start(bf16[320,1408]{1,0:T(8,128)(2,1)S(1)} %bitcast.8), channel_id=1, source_target_pairs={{8,0},{2,10},{16,8},{10,18},{24,16},{18,26},{28,24},{26,30},{20,28... | collective-permute-start | bytes 2703368 | tf_op jit(solution)/shard_map/ppermute | solution.py:191
  126.9 4.0 %shard_map.39.refs_3_ = f32[640,1408]{1,0:T(8,128)S(1)} custom-call(bf16[2,640,1408]{2,1,0:T(8,128)(2,1)S(1)} %get-tuple-element.29.refs_0_, bf16[320,1408]{1,0:T(8,128)(2,1)S(1)} %collective-permute-done.24.refs_1_, bf16[320,1408]{1,0:T(8,128)(2,1)S(1)} %collective-permute-done.25.refs_2_, ...), custom_call_target="tpu_custom_call", output_to_operand_aliasing={{}: (3, {})} | custom-call | flops 1730150400 | bytes 12615680 | tf_op jit(solution)/shard_map/pallas_call | solution.py:135
  130.9 4.5 %shard_map.40.refs_6_ = bf16[640,1408]{1,0:T(8,128)(2,1)S(1)} custom-call(bf16[2,640,1408]{2,1,0:T(8,128)(2,1)S(1)} %get-tuple-element.29.refs_0_, bf16[320,1408]{1,0:T(8,128)(2,1)S(1)} %collective-permute-done.19.refs_1_, bf16[320,1408]{1,0:T(8,128)(2,1)S(1)} %collective-permute-done.23.refs_2_, f32[640,1408]{1,0:T(8,128)S(1)} %shard_map.39.refs_3_, ...), custom_call_target="tpu_custom_call" | custom-call | flops 1730150400 | bytes 12615680 | tf_op jit(solution)/shard_map/pallas_call | solution.py:135
  141.8 7.0 %collective-permute-done.32.refs_5_ = bf16[320,1408]{1,0:T(8,128)(2,1)S(1)} collective-permute-done((bf16[320,1408]{1,0:T(8,128)(2,1)S(1)}, bf16[320,1408]{1,0:T(8,128)(2,1)S(1)}, u32[]{:S(2)}, u32[]{:S(2)}) %collective-permute-start.32) | collective-permute-done | bytes 901152 | tf_op jit(solution)/shard_map/ppermute | solution.py:191
  148.7 9.7 %collective-permute-done.30.refs_3_ = bf16[320,1408]{1,0:T(8,128)(2,1)S(1)} collective-permute-done((bf16[320,1408]{1,0:T(8,128)(2,1)S(1)}, bf16[320,1408]{1,0:T(8,128)(2,1)S(1)}, u32[]{:S(2)}, u32[]{:S(2)}) %collective-permute-start.30) | collective-permute-done | bytes 901152 | tf_op jit(solution)/shard_map/ppermute | solution.py:191
  158.4 9.7 %collective-permute-done.26.refs_1_ = bf16[320,1408]{1,0:T(8,128)(2,1)S(1)} collective-permute-done((bf16[320,1408]{1,0:T(8,128)(2,1)S(1)}, bf16[320,1408]{1,0:T(8,128)(2,1)S(1)}, u32[]{:S(2)}, u32[]{:S(2)}) %collective-permute-start.26) | collective-permute-done | bytes 901152 | tf_op jit(solution)/shard_map/ppermute | solution.py:191
  168.1 8.6 %shard_map.41.refs_3_ = f32[640,1408]{1,0:T(8,128)} custom-call(bf16[2,640,1408]{2,1,0:T(8,128)(2,1)S(1)} %get-tuple-element.29.refs_0_, bf16[320,1408]{1,0:T(8,128)(2,1)S(1)} %collective-permute-done.28.refs_1_, bf16[320,1408]{1,0:T(8,128)(2,1)S(1)} %collective-permute-done.29.refs_2_, bf16[320,1408]{1,0:T(8,128)(2,1)S(1)} %collective-permute-done.30.refs_3_, ...), custom_call_target="tpu_custom_call" | custom-call | flops 5190451200 | bytes 16220160 | tf_op jit(solution)/shard_map/pallas_call | solution.py:135
  176.6 4.2 %collective-permute-done.34.refs_7_ = bf16[640,1408]{1,0:T(8,128)(2,1)S(1)} collective-permute-done((bf16[640,1408]{1,0:T(8,128)(2,1)S(1)}, bf16[640,1408]{1,0:T(8,128)(2,1)S(1)}, u32[]{:S(2)}, u32[]{:S(2)}) %collective-permute-start.34) | collective-permute-done | bytes 1802272 | tf_op jit(solution)/shard_map/ppermute | solution.py:213
  180.9 7.6 %shard_map.42 = f32[640,1408]{1,0:T(8,128)} custom-call(bf16[2,640,1408]{2,1,0:T(8,128)(2,1)S(1)} %get-tuple-element.29.refs_0_, bf16[320,1408]{1,0:T(8,128)(2,1)S(1)} %collective-permute-done.26.refs_1_, bf16[320,1408]{1,0:T(8,128)(2,1)S(1)} %collective-permute-done.27.refs_2_, f32[640,1408]{1,0:T(8,128)} %shard_map.41.refs_3_, ...), custom_call_target="tpu_custom_call", output_to_operand_aliasing={{}: (3, {})} | custom-call | flops 1730150400 | bytes 12615680 | tf_op jit(solution)/shard_map/pallas_call | solution.py:135
  (62 shorter events, 30.3 us)
Async XLA Ops:
  3.7 14.4 %collective-permute-start.4 = (bf16[320,1408]{1,0:T(8,128)(2,1)}, bf16[320,1408]{1,0:T(8,128)(2,1)S(1)}, u32[]{:S(2)}, u32[]{:S(2)}) collective-permute-start(bf16[320,1408]{1,0:T(8,128)(2,1)} %get-tuple-element.26.refs_1_), channel_id=1, source_target_pairs={{0,8},{10,2},{8,16},{18,10},{16,24},{26,18},{24,28},{30,26},{28,20... | collective-permute-start | bytes 2703368 | tf_op jit(solution)/shard_map/ppermute | solution.py:191
  6.8 21.0 %collective-permute-start = (bf16[320,1408]{1,0:T(8,128)(2,1)}, bf16[320,1408]{1,0:T(8,128)(2,1)S(1)}, u32[]{:S(2)}, u32[]{:S(2)}) collective-permute-start(bf16[320,1408]{1,0:T(8,128)(2,1)} %get-tuple-element.27.refs_2_), channel_id=1, source_target_pairs={{0,8},{10,2},{8,16},{18,10},{16,24},{26,18},{24,28},{30,26},{28,20... | collective-permute-start | bytes 2703368 | tf_op jit(solution)/shard_map/ppermute | solution.py:191
  8.3 19.4 %collective-permute-start.2 = (bf16[320,1408]{1,0:T(8,128)(2,1)}, bf16[320,1408]{1,0:T(8,128)(2,1)S(1)}, u32[]{:S(2)}, u32[]{:S(2)}) collective-permute-start(bf16[320,1408]{1,0:T(8,128)(2,1)} %get-tuple-element.26.refs_1_), channel_id=1, source_target_pairs={{0,2},{2,0},{4,6},{6,4},{8,10},{10,8},{12,14},{14,12},{16,18},{18,... | collective-permute-start | bytes 2703368 | tf_op jit(solution)/shard_map/ppermute | solution.py:191
  18.1 19.3 %collective-permute-start.9 = (bf16[320,1408]{1,0:T(8,128)(2,1)S(1)}, bf16[320,1408]{1,0:T(8,128)(2,1)S(1)}, u32[]{:S(2)}, u32[]{:S(2)}) collective-permute-start(bf16[320,1408]{1,0:T(8,128)(2,1)S(1)} %collective-permute-done.4.refs_5_), channel_id=1, source_target_pairs={{0,8},{10,2},{8,16},{18,10},{16,24},{26,18},{24,28},{30,26},{28,20... | collective-permute-start | bytes 2703368 | tf_op jit(solution)/shard_map/ppermute | solution.py:191
  20.2 17.2 %collective-permute-start.3 = (bf16[320,1408]{1,0:T(8,128)(2,1)}, bf16[320,1408]{1,0:T(8,128)(2,1)S(1)}, u32[]{:S(2)}, u32[]{:S(2)}) collective-permute-start(bf16[320,1408]{1,0:T(8,128)(2,1)} %get-tuple-element.27.refs_2_), channel_id=1, source_target_pairs={{0,2},{2,0},{4,6},{6,4},{8,10},{10,8},{12,14},{14,12},{16,18},{18,... | collective-permute-start | bytes 2703368 | tf_op jit(solution)/shard_map/ppermute | solution.py:191
  20.2 19.3 %collective-permute-start.5 = (bf16[320,1408]{1,0:T(8,128)(2,1)S(1)}, bf16[320,1408]{1,0:T(8,128)(2,1)S(1)}, u32[]{:S(2)}, u32[]{:S(2)}) collective-permute-start(bf16[320,1408]{1,0:T(8,128)(2,1)S(1)} %collective-permute-done.4.refs_5_), channel_id=1, source_target_pairs={{0,2},{2,0},{4,6},{6,4},{8,10},{10,8},{12,14},{14,12},{16,18},{18,... | collective-permute-start | bytes 2703368 | tf_op jit(solution)/shard_map/ppermute | solution.py:191
  27.8 11.7 %collective-permute-start.6 = (bf16[320,1408]{1,0:T(8,128)(2,1)S(1)}, bf16[320,1408]{1,0:T(8,128)(2,1)S(1)}, u32[]{:S(2)}, u32[]{:S(2)}) collective-permute-start(bf16[320,1408]{1,0:T(8,128)(2,1)S(1)} %collective-permute-done.refs_7_), channel_id=1, source_target_pairs={{0,2},{2,0},{4,6},{6,4},{8,10},{10,8},{12,14},{14,12},{16,18},{18,... | collective-permute-start | bytes 2703368 | tf_op jit(solution)/shard_map/ppermute | solution.py:191
  27.8 20.8 %collective-permute-start.1 = (bf16[320,1408]{1,0:T(8,128)(2,1)S(1)}, bf16[320,1408]{1,0:T(8,128)(2,1)S(1)}, u32[]{:S(2)}, u32[]{:S(2)}) collective-permute-start(bf16[320,1408]{1,0:T(8,128)(2,1)S(1)} %collective-permute-done.refs_7_), channel_id=1, source_target_pairs={{0,8},{10,2},{8,16},{18,10},{16,24},{26,18},{24,28},{30,26},{28,20... | collective-permute-start | bytes 2703368 | tf_op jit(solution)/shard_map/ppermute | solution.py:191
  37.4 12.9 %collective-permute-start.10 = (bf16[320,1408]{1,0:T(8,128)(2,1)S(1)}, bf16[320,1408]{1,0:T(8,128)(2,1)S(1)}, u32[]{:S(2)}, u32[]{:S(2)}) collective-permute-start(bf16[320,1408]{1,0:T(8,128)(2,1)S(1)} %collective-permute-done.9.refs_1_), channel_id=1, source_target_pairs={{0,2},{2,0},{4,6},{6,4},{8,10},{10,8},{12,14},{14,12},{16,18},{18,... | collective-permute-start | bytes 2703368 | tf_op jit(solution)/shard_map/ppermute | solution.py:191
  37.4 19.3 %collective-permute-start.13 = (bf16[320,1408]{1,0:T(8,128)(2,1)S(1)}, bf16[320,1408]{1,0:T(8,128)(2,1)S(1)}, u32[]{:S(2)}, u32[]{:S(2)}) collective-permute-start(bf16[320,1408]{1,0:T(8,128)(2,1)S(1)} %collective-permute-done.9.refs_1_), channel_id=1, source_target_pairs={{0,8},{10,2},{8,16},{18,10},{16,24},{26,18},{24,28},{30,26},{28,20... | collective-permute-start | bytes 2703368 | tf_op jit(solution)/shard_map/ppermute | solution.py:191
  48.6 10.2 %collective-permute-start.8 = (bf16[320,1408]{1,0:T(8,128)(2,1)S(1)}, bf16[320,1408]{1,0:T(8,128)(2,1)S(1)}, u32[]{:S(2)}, u32[]{:S(2)}) collective-permute-start(bf16[320,1408]{1,0:T(8,128)(2,1)S(1)} %collective-permute-done.1.refs_1_), channel_id=1, source_target_pairs={{0,2},{2,0},{4,6},{6,4},{8,10},{10,8},{12,14},{14,12},{16,18},{18,... | collective-permute-start | bytes 2703368 | tf_op jit(solution)/shard_map/ppermute | solution.py:191
  48.8 17.6 %collective-permute-start.7 = (bf16[320,1408]{1,0:T(8,128)(2,1)S(1)}, bf16[320,1408]{1,0:T(8,128)(2,1)S(1)}, u32[]{:S(2)}, u32[]{:S(2)}) collective-permute-start(bf16[320,1408]{1,0:T(8,128)(2,1)S(1)} %collective-permute-done.1.refs_1_), channel_id=1, source_target_pairs={{0,8},{10,2},{8,16},{18,10},{16,24},{26,18},{24,28},{30,26},{28,20... | collective-permute-start | bytes 2703368 | tf_op jit(solution)/shard_map/ppermute | solution.py:191
  56.7 11.7 %collective-permute-start.14 = (bf16[320,1408]{1,0:T(8,128)(2,1)S(1)}, bf16[320,1408]{1,0:T(8,128)(2,1)S(1)}, u32[]{:S(2)}, u32[]{:S(2)}) collective-permute-start(bf16[320,1408]{1,0:T(8,128)(2,1)S(1)} %collective-permute-done.13.refs_1_), channel_id=1, source_target_pairs={{0,2},{2,0},{4,6},{6,4},{8,10},{10,8},{12,14},{14,12},{16,18},{18,... | collective-permute-start | bytes 2703368 | tf_op jit(solution)/shard_map/ppermute | solution.py:191
  56.7 19.3 %collective-permute-start.17 = (bf16[320,1408]{1,0:T(8,128)(2,1)S(1)}, bf16[320,1408]{1,0:T(8,128)(2,1)S(1)}, u32[]{:S(2)}, u32[]{:S(2)}) collective-permute-start(bf16[320,1408]{1,0:T(8,128)(2,1)S(1)} %collective-permute-done.13.refs_1_), channel_id=1, source_target_pairs={{0,8},{10,2},{8,16},{18,10},{16,24},{26,18},{24,28},{30,26},{28,20... | collective-permute-start | bytes 2703368 | tf_op jit(solution)/shard_map/ppermute | solution.py:191
  66.4 11.7 %collective-permute-start.12 = (bf16[320,1408]{1,0:T(8,128)(2,1)S(1)}, bf16[320,1408]{1,0:T(8,128)(2,1)S(1)}, u32[]{:S(2)}, u32[]{:S(2)}) collective-permute-start(bf16[320,1408]{1,0:T(8,128)(2,1)S(1)} %collective-permute-done.7.refs_1_), channel_id=1, source_target_pairs={{0,2},{2,0},{4,6},{6,4},{8,10},{10,8},{12,14},{14,12},{16,18},{18,... | collective-permute-start | bytes 2703368 | tf_op jit(solution)/shard_map/ppermute | solution.py:191
  66.4 19.3 %collective-permute-start.11 = (bf16[320,1408]{1,0:T(8,128)(2,1)S(1)}, bf16[320,1408]{1,0:T(8,128)(2,1)S(1)}, u32[]{:S(2)}, u32[]{:S(2)}) collective-permute-start(bf16[320,1408]{1,0:T(8,128)(2,1)S(1)} %collective-permute-done.7.refs_1_), channel_id=1, source_target_pairs={{0,8},{10,2},{8,16},{18,10},{16,24},{26,18},{24,28},{30,26},{28,20... | collective-permute-start | bytes 2703368 | tf_op jit(solution)/shard_map/ppermute | solution.py:191
  76.1 11.7 %collective-permute-start.18 = (bf16[320,1408]{1,0:T(8,128)(2,1)S(1)}, bf16[320,1408]{1,0:T(8,128)(2,1)S(1)}, u32[]{:S(2)}, u32[]{:S(2)}) collective-permute-start(bf16[320,1408]{1,0:T(8,128)(2,1)S(1)} %collective-permute-done.17.refs_1_), channel_id=1, source_target_pairs={{0,2},{2,0},{4,6},{6,4},{8,10},{10,8},{12,14},{14,12},{16,18},{18,... | collective-permute-start | bytes 2703368 | tf_op jit(solution)/shard_map/ppermute | solution.py:191
  76.1 19.3 %collective-permute-start.21 = (bf16[320,1408]{1,0:T(8,128)(2,1)S(1)}, bf16[320,1408]{1,0:T(8,128)(2,1)S(1)}, u32[]{:S(2)}, u32[]{:S(2)}) collective-permute-start(bf16[320,1408]{1,0:T(8,128)(2,1)S(1)} %collective-permute-done.17.refs_1_), channel_id=1, source_target_pairs={{0,8},{10,2},{8,16},{18,10},{16,24},{26,18},{24,28},{30,26},{28,20... | collective-permute-start | bytes 2703368 | tf_op jit(solution)/shard_map/ppermute | solution.py:191
  85.7 11.7 %collective-permute-start.16 = (bf16[320,1408]{1,0:T(8,128)(2,1)S(1)}, bf16[320,1408]{1,0:T(8,128)(2,1)S(1)}, u32[]{:S(2)}, u32[]{:S(2)}) collective-permute-start(bf16[320,1408]{1,0:T(8,128)(2,1)S(1)} %collective-permute-done.11.refs_1_), channel_id=1, source_target_pairs={{0,2},{2,0},{4,6},{6,4},{8,10},{10,8},{12,14},{14,12},{16,18},{18,... | collective-permute-start | bytes 2703368 | tf_op jit(solution)/shard_map/ppermute | solution.py:191
  85.7 19.3 %collective-permute-start.15 = (bf16[320,1408]{1,0:T(8,128)(2,1)S(1)}, bf16[320,1408]{1,0:T(8,128)(2,1)S(1)}, u32[]{:S(2)}, u32[]{:S(2)}) collective-permute-start(bf16[320,1408]{1,0:T(8,128)(2,1)S(1)} %collective-permute-done.11.refs_1_), channel_id=1, source_target_pairs={{0,8},{10,2},{8,16},{18,10},{16,24},{26,18},{24,28},{30,26},{28,20... | collective-permute-start | bytes 2703368 | tf_op jit(solution)/shard_map/ppermute | solution.py:191
  95.4 11.7 %collective-permute-start.22 = (bf16[320,1408]{1,0:T(8,128)(2,1)S(1)}, bf16[320,1408]{1,0:T(8,128)(2,1)S(1)}, u32[]{:S(2)}, u32[]{:S(2)}) collective-permute-start(bf16[320,1408]{1,0:T(8,128)(2,1)S(1)} %collective-permute-done.21.refs_1_), channel_id=1, source_target_pairs={{0,2},{2,0},{4,6},{6,4},{8,10},{10,8},{12,14},{14,12},{16,18},{18,... | collective-permute-start | bytes 2703368 | tf_op jit(solution)/shard_map/ppermute | solution.py:191
  95.4 19.3 %collective-permute-start.24 = (bf16[320,1408]{1,0:T(8,128)(2,1)S(1)}, bf16[320,1408]{1,0:T(8,128)(2,1)S(1)}, u32[]{:S(2)}, u32[]{:S(2)}) collective-permute-start(bf16[320,1408]{1,0:T(8,128)(2,1)S(1)} %collective-permute-done.21.refs_1_), channel_id=1, source_target_pairs={{0,8},{10,2},{8,16},{18,10},{16,24},{26,18},{24,28},{30,26},{28,20... | collective-permute-start | bytes 2703368 | tf_op jit(solution)/shard_map/ppermute | solution.py:191
  105.0 19.3 %collective-permute-start.19 = (bf16[320,1408]{1,0:T(8,128)(2,1)S(1)}, bf16[320,1408]{1,0:T(8,128)(2,1)S(1)}, u32[]{:S(2)}, u32[]{:S(2)}) collective-permute-start(bf16[320,1408]{1,0:T(8,128)(2,1)S(1)} %collective-permute-done.15.refs_1_), channel_id=1, source_target_pairs={{0,8},{10,2},{8,16},{18,10},{16,24},{26,18},{24,28},{30,26},{28,20... | collective-permute-start | bytes 2703368 | tf_op jit(solution)/shard_map/ppermute | solution.py:191
  114.7 12.2 %collective-permute-start.25 = (bf16[320,1408]{1,0:T(8,128)(2,1)S(1)}, bf16[320,1408]{1,0:T(8,128)(2,1)S(1)}, u32[]{:S(2)}, u32[]{:S(2)}) collective-permute-start(bf16[320,1408]{1,0:T(8,128)(2,1)S(1)} %collective-permute-done.24.refs_1_), channel_id=1, source_target_pairs={{0,2},{2,0},{4,6},{6,4},{8,10},{10,8},{12,14},{14,12},{16,18},{18,... | collective-permute-start | bytes 2703368 | tf_op jit(solution)/shard_map/ppermute | solution.py:191
  124.6 17.1 %collective-permute-start.28 = (bf16[320,1408]{1,0:T(8,128)(2,1)S(1)}, bf16[320,1408]{1,0:T(8,128)(2,1)S(1)}, u32[]{:S(2)}, u32[]{:S(2)}) collective-permute-start(bf16[320,1408]{1,0:T(8,128)(2,1)S(1)} %bitcast.8), channel_id=1, source_target_pairs={{8,0},{2,10},{16,8},{10,18},{24,16},{18,26},{28,24},{26,30},{20,28... | collective-permute-start | bytes 2703368 | tf_op jit(solution)/shard_map/ppermute | solution.py:191
  135.5 13.3 %collective-permute-start.32 = (bf16[320,1408]{1,0:T(8,128)(2,1)S(1)}, bf16[320,1408]{1,0:T(8,128)(2,1)S(1)}, u32[]{:S(2)}, u32[]{:S(2)}) collective-permute-start(bf16[320,1408]{1,0:T(8,128)(2,1)S(1)} %bitcast.7), channel_id=1, source_target_pairs={{8,0},{2,10},{16,8},{10,18},{24,16},{18,26},{28,24},{26,30},{20,28... | collective-permute-start | bytes 2703368 | tf_op jit(solution)/shard_map/ppermute | solution.py:191
  137.1 21.3 %collective-permute-start.30 = (bf16[320,1408]{1,0:T(8,128)(2,1)S(1)}, bf16[320,1408]{1,0:T(8,128)(2,1)S(1)}, u32[]{:S(2)}, u32[]{:S(2)}) collective-permute-start(bf16[320,1408]{1,0:T(8,128)(2,1)S(1)} %bitcast.6), channel_id=1, source_target_pairs={{8,0},{2,10},{16,8},{10,18},{24,16},{18,26},{28,24},{26,30},{20,28... | collective-permute-start | bytes 2703368 | tf_op jit(solution)/shard_map/ppermute | solution.py:191
  138.7 29.4 %collective-permute-start.26 = (bf16[320,1408]{1,0:T(8,128)(2,1)S(1)}, bf16[320,1408]{1,0:T(8,128)(2,1)S(1)}, u32[]{:S(2)}, u32[]{:S(2)}) collective-permute-start(bf16[320,1408]{1,0:T(8,128)(2,1)S(1)} %bitcast.5), channel_id=1, source_target_pairs={{8,0},{2,10},{16,8},{10,18},{24,16},{18,26},{28,24},{26,30},{20,28... | collective-permute-start | bytes 2703368 | tf_op jit(solution)/shard_map/ppermute | solution.py:191
  140.2 40.6 %collective-permute-start.34 = (bf16[640,1408]{1,0:T(8,128)(2,1)S(1)}, bf16[640,1408]{1,0:T(8,128)(2,1)S(1)}, u32[]{:S(2)}, u32[]{:S(2)}) collective-permute-start(bf16[640,1408]{1,0:T(8,128)(2,1)S(1)} %shard_map.40.refs_6_), channel_id=1, source_target_pairs={{0,1},{1,0},{2,3},{3,2},{4,5},{5,4},{6,7},{7,6},{8,9},{9,8},{10,11... | collective-permute-start | bytes 5406728 | tf_op jit(solution)/shard_map/ppermute | solution.py:213
  141.7 26.3 %collective-permute-start.29 = (bf16[320,1408]{1,0:T(8,128)(2,1)S(1)}, bf16[320,1408]{1,0:T(8,128)(2,1)S(1)}, u32[]{:S(2)}, u32[]{:S(2)}) collective-permute-start(bf16[320,1408]{1,0:T(8,128)(2,1)S(1)} %collective-permute-done.28.refs_1_), channel_id=1, source_target_pairs={{0,2},{2,0},{4,6},{6,4},{8,10},{10,8},{12,14},{14,12},{16,18},{18,... | collective-permute-start | bytes 2703368 | tf_op jit(solution)/shard_map/ppermute | solution.py:191
  148.7 19.3 %collective-permute-start.33 = (bf16[320,1408]{1,0:T(8,128)(2,1)S(1)}, bf16[320,1408]{1,0:T(8,128)(2,1)S(1)}, u32[]{:S(2)}, u32[]{:S(2)}) collective-permute-start(bf16[320,1408]{1,0:T(8,128)(2,1)S(1)} %collective-permute-done.32.refs_5_), channel_id=1, source_target_pairs={{0,2},{2,0},{4,6},{6,4},{8,10},{10,8},{12,14},{14,12},{16,18},{18,... | collective-permute-start | bytes 2703368 | tf_op jit(solution)/shard_map/ppermute | solution.py:191
  158.4 9.7 %collective-permute-start.31 = (bf16[320,1408]{1,0:T(8,128)(2,1)S(1)}, bf16[320,1408]{1,0:T(8,128)(2,1)S(1)}, u32[]{:S(2)}, u32[]{:S(2)}) collective-permute-start(bf16[320,1408]{1,0:T(8,128)(2,1)S(1)} %collective-permute-done.30.refs_3_), channel_id=1, source_target_pairs={{0,2},{2,0},{4,6},{6,4},{8,10},{10,8},{12,14},{14,12},{16,18},{18,... | collective-permute-start | bytes 2703368 | tf_op jit(solution)/shard_map/ppermute | solution.py:191
  (7 other events, 72.0 us)

commit v7 on v6

--- a/solution.py
+++ b/solution.py
@@ -220,12 +220,9 @@
         piece = own_half[:, at : at + n].reshape(2 * n, width)
         nearest.append(move(piece, reverse, own if k else held[0]))
         at += n
-    batch = []
-    for x in nearest[:-1]:
-        batch += [x, move(x, swap, own)]
-    total = add(batch, None)
-    batch = [nearest[-1], move(nearest[-1], swap)]
-    return add(batch, total, project=(student, s_scale), summands=summands)
+    batch = nearest + [move(x, swap, own) for x in nearest]
+    total = add(batch, None, project=(student, s_scale))
+    return s_scale * (sum(x.astype(jnp.float32) for x in summands) + total)
 
 
 def solution(mesh):

time: 189 us -> 191 us (1.011)
  other arithmetic: 0 us -> 4.08 us
  local copies, waits for them, and re-layouts: 2.3 us -> 6.35 us
  Pallas kernels: 70.6 us -> 66.7 us
    ppermute x1, waiting for transfers between devices: 4.22 us -> 0.01 us  [local(): summands = (value, lax.ppermute(value, 'pair', route))]
    unnamed x8 -> x14, local copies, waits for them, and re-layouts: 2.03 us -> 6.08 us
    pallas_call x13 -> x12, Pallas kernels: 65.6 us -> 61.7 us  [add_relation(): pl.pallas_call(functools.partial(relation_kernel, margin, weight, counts,...]
    mul x0 -> x1, other arithmetic: none -> 3.91 us  [local(): return s_scale * (sum((x.astype(jnp.float32) for x in summands)) + total)]
    ppermute x34, waiting for transfers between devices: 77 us -> 79.7 us  [move(): return lax.ppermute(after(x, *wait_for), 'seq', route)]
  transfers between devices with their start and end apart: 35 -> 35, of which waited for: 15 -> 15; matrix products, arithmetic and copies ran while one was open for 0% -> 0% of each run, Pallas kernels for 31% -> 33%
where the time goes in v7:
time: 191 us
  waiting for transfers between devices  79.7 us (42%)
  Pallas kernels  66.7 us (35%)
  starting transfers between devices  34.1 us (18%)
  local copies, waits for them, and re-layouts  6.35 us (3%)
  other arithmetic  4.08 us (2%)
    ppermute x34, waiting for transfers between devices, move(): return lax.ppermute(after(x, *wait_for), 'seq', route)  79.7 us
    pallas_call x12, Pallas kernels, add_relation(): pl.pallas_call(functools.partial(relation_kernel, margin, weight, counts,...  61.7 us
    ppermute x34, starting transfers between devices, move(): return lax.ppermute(after(x, *wait_for), 'seq', route)  32.7 us
    unnamed x14, local copies, waits for them, and re-layouts  6.08 us
    mul x1, other arithmetic, local(): return s_scale * (sum((x.astype(jnp.float32) for x in summands)) + total)  3.91 us
  transfers between devices with their start and end apart: 35, of which 15 were waited for; matrix products, arithmetic and copies ran while one was open for 0% of the time, Pallas kernels for 33%

profile of v7, /device:TPU:0, one launch (start us, length us, event | category | flops | bytes accessed | tf_op | source)
XLA Modules:
  0.0 191.2 jit_solution(17878600751747804775)
XLA Ops:
  0.0 3.8 %shard_map.28 = (bf16[320,1408]{1,0:T(8,128)(2,1)}, bf16[320,1408]{1,0:T(8,128)(2,1)}) custom-call(s32[1]{0:T(128)} %bitcast.which, f32[640,1408]{1,0:T(8,128)} %refs_9_.1, f32[640,1408]{1,0:T(8,128)} %teacher.3), custom_call_target="tpu_custom_call" | custom-call | flops 2703360 | bytes 5406720 | tf_op jit(solution)/shard_map/pallas_call | solution.py:68
  3.8 3.0 %collective-permute-start.4 = (bf16[320,1408]{1,0:T(8,128)(2,1)}, bf16[320,1408]{1,0:T(8,128)(2,1)S(1)}, u32[]{:S(2)}, u32[]{:S(2)}) collective-permute-start(bf16[320,1408]{1,0:T(8,128)(2,1)} %get-tuple-element.27.refs_1_), channel_id=1, source_target_pairs={{0,8},{10,2},{8,16},{18,10},{16,24},{26,18},{24,28},{30,26},{28,20... | collective-permute-start | bytes 2703368 | tf_op jit(solution)/shard_map/ppermute | solution.py:191
  8.4 9.8 %collective-permute-done.4.refs_5_ = bf16[320,1408]{1,0:T(8,128)(2,1)S(1)} collective-permute-done((bf16[320,1408]{1,0:T(8,128)(2,1)}, bf16[320,1408]{1,0:T(8,128)(2,1)S(1)}, u32[]{:S(2)}, u32[]{:S(2)}) %collective-permute-start.4) | collective-permute-done | bytes 901152 | tf_op jit(solution)/shard_map/ppermute | solution.py:191
  20.7 7.1 %collective-permute-done.refs_7_ = bf16[320,1408]{1,0:T(8,128)(2,1)S(1)} collective-permute-done((bf16[320,1408]{1,0:T(8,128)(2,1)}, bf16[320,1408]{1,0:T(8,128)(2,1)S(1)}, u32[]{:S(2)}, u32[]{:S(2)}) %collective-permute-start) | collective-permute-done | bytes 901152 | tf_op jit(solution)/shard_map/ppermute | solution.py:191
  27.8 2.1 %collective-permute-start.1 = (bf16[320,1408]{1,0:T(8,128)(2,1)S(1)}, bf16[320,1408]{1,0:T(8,128)(2,1)S(1)}, u32[]{:S(2)}, u32[]{:S(2)}) collective-permute-start(bf16[320,1408]{1,0:T(8,128)(2,1)S(1)} %collective-permute-done.refs_7_), channel_id=1, source_target_pairs={{0,8},{10,2},{8,16},{18,10},{16,24},{26,18},{24,28},{30,26},{28,20... | collective-permute-start | bytes 2703368 | tf_op jit(solution)/shard_map/ppermute | solution.py:191
  33.2 4.3 %collective-permute-done.9.refs_1_ = bf16[320,1408]{1,0:T(8,128)(2,1)S(1)} collective-permute-done((bf16[320,1408]{1,0:T(8,128)(2,1)S(1)}, bf16[320,1408]{1,0:T(8,128)(2,1)S(1)}, u32[]{:S(2)}, u32[]{:S(2)}) %collective-permute-start.9) | collective-permute-done | bytes 901152 | tf_op jit(solution)/shard_map/ppermute | solution.py:191
  39.6 9.0 %shard_map.30.refs_3_ = f32[640,1408]{1,0:T(8,128)S(1)} custom-call(bf16[2,640,1408]{2,1,0:T(8,128)(2,1)S(1)} %get-tuple-element.31.refs_0_, bf16[320,1408]{1,0:T(8,128)(2,1)S(1)} %copy-done.5, bf16[320,1408]{1,0:T(8,128)(2,1)S(1)} %copy-done.6, bf16[320,1408]{1,0:T(8,128)(2,1)S(1)} %collective-permute-done.2.refs_3_, ...), custom_call_target="tpu_custom_call" | custom-call | flops 6920601600 | bytes 18022400 | tf_op jit(solution)/shard_map/pallas_call | solution.py:135
  50.3 4.0 %shard_map.31.refs_3_ = f32[640,1408]{1,0:T(8,128)S(1)} custom-call(bf16[2,640,1408]{2,1,0:T(8,128)(2,1)S(1)} %get-tuple-element.31.refs_0_, bf16[320,1408]{1,0:T(8,128)(2,1)S(1)} %collective-permute-done.9.refs_1_, bf16[320,1408]{1,0:T(8,128)(2,1)S(1)} %collective-permute-done.10.refs_2_, ...), custom_call_target="tpu_custom_call", output_to_operand_aliasing={{}: (3, {})} | custom-call | flops 1730150400 | bytes 12615680 | tf_op jit(solution)/shard_map/pallas_call | solution.py:135
  54.3 2.4 %collective-permute-done.13.refs_1_ = bf16[320,1408]{1,0:T(8,128)(2,1)S(1)} collective-permute-done((bf16[320,1408]{1,0:T(8,128)(2,1)S(1)}, bf16[320,1408]{1,0:T(8,128)(2,1)S(1)}, u32[]{:S(2)}, u32[]{:S(2)}) %collective-permute-start.13) | collective-permute-done | bytes 901152 | tf_op jit(solution)/shard_map/ppermute | solution.py:191
  58.9 4.0 %shard_map.32.refs_3_ = f32[640,1408]{1,0:T(8,128)S(1)} custom-call(bf16[2,640,1408]{2,1,0:T(8,128)(2,1)S(1)} %get-tuple-element.31.refs_0_, bf16[320,1408]{1,0:T(8,128)(2,1)S(1)} %collective-permute-done.1.refs_1_, bf16[320,1408]{1,0:T(8,128)(2,1)S(1)} %collective-permute-done.8.refs_2_, ...), custom_call_target="tpu_custom_call", output_to_operand_aliasing={{}: (3, {})} | custom-call | flops 1730150400 | bytes 12615680 | tf_op jit(solution)/shard_map/pallas_call | solution.py:135
  62.8 3.6 %collective-permute-done.7.refs_1_ = bf16[320,1408]{1,0:T(8,128)(2,1)S(1)} collective-permute-done((bf16[320,1408]{1,0:T(8,128)(2,1)S(1)}, bf16[320,1408]{1,0:T(8,128)(2,1)S(1)}, u32[]{:S(2)}, u32[]{:S(2)}) %collective-permute-start.7) | collective-permute-done | bytes 901152 | tf_op jit(solution)/shard_map/ppermute | solution.py:191
  68.5 4.0 %shard_map.33.refs_3_ = f32[640,1408]{1,0:T(8,128)S(1)} custom-call(bf16[2,640,1408]{2,1,0:T(8,128)(2,1)S(1)} %get-tuple-element.31.refs_0_, bf16[320,1408]{1,0:T(8,128)(2,1)S(1)} %collective-permute-done.13.refs_1_, bf16[320,1408]{1,0:T(8,128)(2,1)S(1)} %collective-permute-done.14.refs_2_, ...), custom_call_target="tpu_custom_call", output_to_operand_aliasing={{}: (3, {})} | custom-call | flops 1730150400 | bytes 12615680 | tf_op jit(solution)/shard_map/pallas_call | solution.py:135
  72.5 3.6 %collective-permute-done.17.refs_1_ = bf16[320,1408]{1,0:T(8,128)(2,1)S(1)} collective-permute-done((bf16[320,1408]{1,0:T(8,128)(2,1)S(1)}, bf16[320,1408]{1,0:T(8,128)(2,1)S(1)}, u32[]{:S(2)}, u32[]{:S(2)}) %collective-permute-start.17) | collective-permute-done | bytes 901152 | tf_op jit(solution)/shard_map/ppermute | solution.py:191
  78.2 4.0 %shard_map.34.refs_3_ = f32[640,1408]{1,0:T(8,128)S(1)} custom-call(bf16[2,640,1408]{2,1,0:T(8,128)(2,1)S(1)} %get-tuple-element.31.refs_0_, bf16[320,1408]{1,0:T(8,128)(2,1)S(1)} %collective-permute-done.7.refs_1_, bf16[320,1408]{1,0:T(8,128)(2,1)S(1)} %collective-permute-done.12.refs_2_, ...), custom_call_target="tpu_custom_call", output_to_operand_aliasing={{}: (3, {})} | custom-call | flops 1730150400 | bytes 12615680 | tf_op jit(solution)/shard_map/pallas_call | solution.py:135
  82.2 3.6 %collective-permute-done.11.refs_1_ = bf16[320,1408]{1,0:T(8,128)(2,1)S(1)} collective-permute-done((bf16[320,1408]{1,0:T(8,128)(2,1)S(1)}, bf16[320,1408]{1,0:T(8,128)(2,1)S(1)}, u32[]{:S(2)}, u32[]{:S(2)}) %collective-permute-start.11) | collective-permute-done | bytes 901152 | tf_op jit(solution)/shard_map/ppermute | solution.py:191
  87.8 4.0 %shard_map.35.refs_3_ = f32[640,1408]{1,0:T(8,128)S(1)} custom-call(bf16[2,640,1408]{2,1,0:T(8,128)(2,1)S(1)} %get-tuple-element.31.refs_0_, bf16[320,1408]{1,0:T(8,128)(2,1)S(1)} %collective-permute-done.17.refs_1_, bf16[320,1408]{1,0:T(8,128)(2,1)S(1)} %collective-permute-done.18.refs_2_, ...), custom_call_target="tpu_custom_call", output_to_operand_aliasing={{}: (3, {})} | custom-call | flops 1730150400 | bytes 12615680 | tf_op jit(solution)/shard_map/pallas_call | solution.py:135
  91.8 3.6 %collective-permute-done.21.refs_1_ = bf16[320,1408]{1,0:T(8,128)(2,1)S(1)} collective-permute-done((bf16[320,1408]{1,0:T(8,128)(2,1)S(1)}, bf16[320,1408]{1,0:T(8,128)(2,1)S(1)}, u32[]{:S(2)}, u32[]{:S(2)}) %collective-permute-start.21) | collective-permute-done | bytes 901152 | tf_op jit(solution)/shard_map/ppermute | solution.py:191
  97.5 4.0 %shard_map.36.refs_3_ = f32[640,1408]{1,0:T(8,128)S(1)} custom-call(bf16[2,640,1408]{2,1,0:T(8,128)(2,1)S(1)} %get-tuple-element.31.refs_0_, bf16[320,1408]{1,0:T(8,128)(2,1)S(1)} %collective-permute-done.11.refs_1_, bf16[320,1408]{1,0:T(8,128)(2,1)S(1)} %collective-permute-done.16.refs_2_, ...), custom_call_target="tpu_custom_call", output_to_operand_aliasing={{}: (3, {})} | custom-call | flops 1730150400 | bytes 12615680 | tf_op jit(solution)/shard_map/pallas_call | solution.py:135
  101.5 3.6 %collective-permute-done.15.refs_1_ = bf16[320,1408]{1,0:T(8,128)(2,1)S(1)} collective-permute-done((bf16[320,1408]{1,0:T(8,128)(2,1)S(1)}, bf16[320,1408]{1,0:T(8,128)(2,1)S(1)}, u32[]{:S(2)}, u32[]{:S(2)}) %collective-permute-start.15) | collective-permute-done | bytes 901152 | tf_op jit(solution)/shard_map/ppermute | solution.py:191
  107.1 4.0 %shard_map.37.refs_3_ = f32[640,1408]{1,0:T(8,128)S(1)} custom-call(bf16[2,640,1408]{2,1,0:T(8,128)(2,1)S(1)} %get-tuple-element.31.refs_0_, bf16[320,1408]{1,0:T(8,128)(2,1)S(1)} %collective-permute-done.21.refs_1_, bf16[320,1408]{1,0:T(8,128)(2,1)S(1)} %collective-permute-done.22.refs_2_, ...), custom_call_target="tpu_custom_call", output_to_operand_aliasing={{}: (3, {})} | custom-call | flops 1730150400 | bytes 12615680 | tf_op jit(solution)/shard_map/pallas_call | solution.py:135
  111.1 3.6 %collective-permute-done.24.refs_1_ = bf16[320,1408]{1,0:T(8,128)(2,1)S(1)} collective-permute-done((bf16[320,1408]{1,0:T(8,128)(2,1)S(1)}, bf16[320,1408]{1,0:T(8,128)(2,1)S(1)}, u32[]{:S(2)}, u32[]{:S(2)}) %collective-permute-start.24) | collective-permute-done | bytes 901152 | tf_op jit(solution)/shard_map/ppermute | solution.py:191
  114.7 4.0 %shard_map.38.refs_3_ = f32[640,1408]{1,0:T(8,128)S(1)} custom-call(bf16[2,640,1408]{2,1,0:T(8,128)(2,1)S(1)} %get-tuple-element.31.refs_0_, bf16[320,1408]{1,0:T(8,128)(2,1)S(1)} %collective-permute-done.15.refs_1_, bf16[320,1408]{1,0:T(8,128)(2,1)S(1)} %collective-permute-done.20.refs_2_, ...), custom_call_target="tpu_custom_call", output_to_operand_aliasing={{}: (3, {})} | custom-call | flops 1730150400 | bytes 12615680 | tf_op jit(solution)/shard_map/pallas_call | solution.py:135
  118.7 5.6 %collective-permute-done.19.refs_1_ = bf16[320,1408]{1,0:T(8,128)(2,1)S(1)} collective-permute-done((bf16[320,1408]{1,0:T(8,128)(2,1)S(1)}, bf16[320,1408]{1,0:T(8,128)(2,1)S(1)}, u32[]{:S(2)}, u32[]{:S(2)}) %collective-permute-start.19) | collective-permute-done | bytes 901152 | tf_op jit(solution)/shard_map/ppermute | solution.py:191
  124.6 2.3 %collective-permute-start.27 = (bf16[320,1408]{1,0:T(8,128)(2,1)S(1)}, bf16[320,1408]{1,0:T(8,128)(2,1)}, u32[]{:S(2)}, u32[]{:S(2)}) collective-permute-start(bf16[320,1408]{1,0:T(8,128)(2,1)S(1)} %bitcast.8), channel_id=1, source_target_pairs={{8,0},{2,10},{16,8},{10,18},{24,16},{18,26},{28,24},{26,30},{20,28... | collective-permute-start | bytes 2703368 | tf_op jit(solution)/shard_map/ppermute | solution.py:191
  126.9 4.0 %shard_map.39.refs_3_ = f32[640,1408]{1,0:T(8,128)S(1)} custom-call(bf16[2,640,1408]{2,1,0:T(8,128)(2,1)S(1)} %get-tuple-element.31.refs_0_, bf16[320,1408]{1,0:T(8,128)(2,1)S(1)} %collective-permute-done.24.refs_1_, bf16[320,1408]{1,0:T(8,128)(2,1)S(1)} %collective-permute-done.25.refs_2_, ...), custom_call_target="tpu_custom_call", output_to_operand_aliasing={{}: (3, {})} | custom-call | flops 1730150400 | bytes 12615680 | tf_op jit(solution)/shard_map/pallas_call | solution.py:135
  131.0 4.5 %shard_map.40 = bf16[640,1408]{1,0:T(8,128)(2,1)S(1)} custom-call(bf16[2,640,1408]{2,1,0:T(8,128)(2,1)S(1)} %get-tuple-element.31.refs_0_, bf16[320,1408]{1,0:T(8,128)(2,1)S(1)} %collective-permute-done.19.refs_1_, bf16[320,1408]{1,0:T(8,128)(2,1)S(1)} %collective-permute-done.23.refs_2_, f32[640,1408]{1,0:T(8,128)S(1)} %shard_map.39.refs_3_, ...), custom_call_target="tpu_custom_call" | custom-call | flops 1730150400 | bytes 12615680 | tf_op jit(solution)/shard_map/pallas_call | solution.py:135
  141.8 7.0 %collective-permute-done.30.refs_4_ = bf16[320,1408]{1,0:T(8,128)(2,1)S(1)} collective-permute-done((bf16[320,1408]{1,0:T(8,128)(2,1)S(1)}, bf16[320,1408]{1,0:T(8,128)(2,1)S(1)}, u32[]{:S(2)}, u32[]{:S(2)}) %collective-permute-start.30) | collective-permute-done | bytes 901152 | tf_op jit(solution)/shard_map/ppermute | solution.py:191
  148.8 9.8 %collective-permute-done.29.refs_3_ = bf16[320,1408]{1,0:T(8,128)(2,1)} collective-permute-done((bf16[320,1408]{1,0:T(8,128)(2,1)S(1)}, bf16[320,1408]{1,0:T(8,128)(2,1)}, u32[]{:S(2)}, u32[]{:S(2)}) %collective-permute-start.29) | collective-permute-done | bytes 901152 | tf_op jit(solution)/shard_map/ppermute | solution.py:191
  158.5 9.7 %collective-permute-done.28.refs_2_ = bf16[320,1408]{1,0:T(8,128)(2,1)} collective-permute-done((bf16[320,1408]{1,0:T(8,128)(2,1)S(1)}, bf16[320,1408]{1,0:T(8,128)(2,1)}, u32[]{:S(2)}, u32[]{:S(2)}) %collective-permute-start.28) | collective-permute-done | bytes 901152 | tf_op jit(solution)/shard_map/ppermute | solution.py:191
  168.4 2.6 %collective-permute-done.32.refs_6_ = bf16[320,1408]{1,0:T(8,128)(2,1)} collective-permute-done((bf16[320,1408]{1,0:T(8,128)(2,1)}, bf16[320,1408]{1,0:T(8,128)(2,1)}, u32[]{:S(2)}, u32[]{:S(2)}) %collective-permute-start.32) | collective-permute-done | bytes 901152 | tf_op jit(solution)/shard_map/ppermute | solution.py:191
  175.0 12.2 %shard_map.41 = f32[640,1408]{1,0:T(8,128)S(1)} custom-call(bf16[2,640,1408]{2,1,0:T(8,128)(2,1)S(1)} %copy-done.1, bf16[320,1408]{1,0:T(8,128)(2,1)} %collective-permute-done.27.refs_1_, bf16[320,1408]{1,0:T(8,128)(2,1)} %collective-permute-done.28.refs_2_, bf16[320,1408]{1,0:T(8,128)(2,1)} %collective-permute-done.29.refs_3_, ...), custom_call_target="tpu_custom_call" | custom-call | flops 6920601600 | bytes 18022400 | tf_op jit(solution)/shard_map/pallas_call | solution.py:135
  187.2 3.9 %add_multiply_fusion = f32[640,1408]{1,0:T(8,128)} fusion(f32[640,1408]{1,0:T(8,128)S(1)} %shard_map.41, bf16[640,1408]{1,0:T(8,128)(2,1)} %collective-permute-done.26, bf16[640,1408]{1,0:T(8,128)(2,1)S(1)} %shard_map.40, f32[640]{0:T(1024)S(1)} %reduce), kind=kLoop, calls=%fused_computation | loop fusion | flops 4505600 | bytes 10816000 | tf_op jit(solution)/shard_map/mul | solution.py:225
  (69 shorter events, 34.5 us)
Async XLA Ops:
  3.8 14.4 %collective-permute-start.4 = (bf16[320,1408]{1,0:T(8,128)(2,1)}, bf16[320,1408]{1,0:T(8,128)(2,1)S(1)}, u32[]{:S(2)}, u32[]{:S(2)}) collective-permute-start(bf16[320,1408]{1,0:T(8,128)(2,1)} %get-tuple-element.27.refs_1_), channel_id=1, source_target_pairs={{0,8},{10,2},{8,16},{18,10},{16,24},{26,18},{24,28},{30,26},{28,20... | collective-permute-start | bytes 2703368 | tf_op jit(solution)/shard_map/ppermute | solution.py:191
  6.8 21.0 %collective-permute-start = (bf16[320,1408]{1,0:T(8,128)(2,1)}, bf16[320,1408]{1,0:T(8,128)(2,1)S(1)}, u32[]{:S(2)}, u32[]{:S(2)}) collective-permute-start(bf16[320,1408]{1,0:T(8,128)(2,1)} %get-tuple-element.28.refs_2_), channel_id=1, source_target_pairs={{0,8},{10,2},{8,16},{18,10},{16,24},{26,18},{24,28},{30,26},{28,20... | collective-permute-start | bytes 2703368 | tf_op jit(solution)/shard_map/ppermute | solution.py:191
  8.4 19.4 %collective-permute-start.2 = (bf16[320,1408]{1,0:T(8,128)(2,1)}, bf16[320,1408]{1,0:T(8,128)(2,1)S(1)}, u32[]{:S(2)}, u32[]{:S(2)}) collective-permute-start(bf16[320,1408]{1,0:T(8,128)(2,1)} %get-tuple-element.27.refs_1_), channel_id=1, source_target_pairs={{0,2},{2,0},{4,6},{6,4},{8,10},{10,8},{12,14},{14,12},{16,18},{18,... | collective-permute-start | bytes 2703368 | tf_op jit(solution)/shard_map/ppermute | solution.py:191
  18.1 19.3 %collective-permute-start.9 = (bf16[320,1408]{1,0:T(8,128)(2,1)S(1)}, bf16[320,1408]{1,0:T(8,128)(2,1)S(1)}, u32[]{:S(2)}, u32[]{:S(2)}) collective-permute-start(bf16[320,1408]{1,0:T(8,128)(2,1)S(1)} %collective-permute-done.4.refs_5_), channel_id=1, source_target_pairs={{0,8},{10,2},{8,16},{18,10},{16,24},{26,18},{24,28},{30,26},{28,20... | collective-permute-start | bytes 2703368 | tf_op jit(solution)/shard_map/ppermute | solution.py:191
  20.2 17.2 %collective-permute-start.3 = (bf16[320,1408]{1,0:T(8,128)(2,1)}, bf16[320,1408]{1,0:T(8,128)(2,1)S(1)}, u32[]{:S(2)}, u32[]{:S(2)}) collective-permute-start(bf16[320,1408]{1,0:T(8,128)(2,1)} %get-tuple-element.28.refs_2_), channel_id=1, source_target_pairs={{0,2},{2,0},{4,6},{6,4},{8,10},{10,8},{12,14},{14,12},{16,18},{18,... | collective-permute-start | bytes 2703368 | tf_op jit(solution)/shard_map/ppermute | solution.py:191
  20.2 19.3 %collective-permute-start.5 = (bf16[320,1408]{1,0:T(8,128)(2,1)S(1)}, bf16[320,1408]{1,0:T(8,128)(2,1)S(1)}, u32[]{:S(2)}, u32[]{:S(2)}) collective-permute-start(bf16[320,1408]{1,0:T(8,128)(2,1)S(1)} %collective-permute-done.4.refs_5_), channel_id=1, source_target_pairs={{0,2},{2,0},{4,6},{6,4},{8,10},{10,8},{12,14},{14,12},{16,18},{18,... | collective-permute-start | bytes 2703368 | tf_op jit(solution)/shard_map/ppermute | solution.py:191
  27.8 11.7 %collective-permute-start.6 = (bf16[320,1408]{1,0:T(8,128)(2,1)S(1)}, bf16[320,1408]{1,0:T(8,128)(2,1)S(1)}, u32[]{:S(2)}, u32[]{:S(2)}) collective-permute-start(bf16[320,1408]{1,0:T(8,128)(2,1)S(1)} %collective-permute-done.refs_7_), channel_id=1, source_target_pairs={{0,2},{2,0},{4,6},{6,4},{8,10},{10,8},{12,14},{14,12},{16,18},{18,... | collective-permute-start | bytes 2703368 | tf_op jit(solution)/shard_map/ppermute | solution.py:191
  27.8 20.8 %collective-permute-start.1 = (bf16[320,1408]{1,0:T(8,128)(2,1)S(1)}, bf16[320,1408]{1,0:T(8,128)(2,1)S(1)}, u32[]{:S(2)}, u32[]{:S(2)}) collective-permute-start(bf16[320,1408]{1,0:T(8,128)(2,1)S(1)} %collective-permute-done.refs_7_), channel_id=1, source_target_pairs={{0,8},{10,2},{8,16},{18,10},{16,24},{26,18},{24,28},{30,26},{28,20... | collective-permute-start | bytes 2703368 | tf_op jit(solution)/shard_map/ppermute | solution.py:191
  37.5 12.9 %collective-permute-start.10 = (bf16[320,1408]{1,0:T(8,128)(2,1)S(1)}, bf16[320,1408]{1,0:T(8,128)(2,1)S(1)}, u32[]{:S(2)}, u32[]{:S(2)}) collective-permute-start(bf16[320,1408]{1,0:T(8,128)(2,1)S(1)} %collective-permute-done.9.refs_1_), channel_id=1, source_target_pairs={{0,2},{2,0},{4,6},{6,4},{8,10},{10,8},{12,14},{14,12},{16,18},{18,... | collective-permute-start | bytes 2703368 | tf_op jit(solution)/shard_map/ppermute | solution.py:191
  37.5 19.3 %collective-permute-start.13 = (bf16[320,1408]{1,0:T(8,128)(2,1)S(1)}, bf16[320,1408]{1,0:T(8,128)(2,1)S(1)}, u32[]{:S(2)}, u32[]{:S(2)}) collective-permute-start(bf16[320,1408]{1,0:T(8,128)(2,1)S(1)} %collective-permute-done.9.refs_1_), channel_id=1, source_target_pairs={{0,8},{10,2},{8,16},{18,10},{16,24},{26,18},{24,28},{30,26},{28,20... | collective-permute-start | bytes 2703368 | tf_op jit(solution)/shard_map/ppermute | solution.py:191
  48.6 10.2 %collective-permute-start.8 = (bf16[320,1408]{1,0:T(8,128)(2,1)S(1)}, bf16[320,1408]{1,0:T(8,128)(2,1)S(1)}, u32[]{:S(2)}, u32[]{:S(2)}) collective-permute-start(bf16[320,1408]{1,0:T(8,128)(2,1)S(1)} %collective-permute-done.1.refs_1_), channel_id=1, source_target_pairs={{0,2},{2,0},{4,6},{6,4},{8,10},{10,8},{12,14},{14,12},{16,18},{18,... | collective-permute-start | bytes 2703368 | tf_op jit(solution)/shard_map/ppermute | solution.py:191
  48.9 17.6 %collective-permute-start.7 = (bf16[320,1408]{1,0:T(8,128)(2,1)S(1)}, bf16[320,1408]{1,0:T(8,128)(2,1)S(1)}, u32[]{:S(2)}, u32[]{:S(2)}) collective-permute-start(bf16[320,1408]{1,0:T(8,128)(2,1)S(1)} %collective-permute-done.1.refs_1_), channel_id=1, source_target_pairs={{0,8},{10,2},{8,16},{18,10},{16,24},{26,18},{24,28},{30,26},{28,20... | collective-permute-start | bytes 2703368 | tf_op jit(solution)/shard_map/ppermute | solution.py:191
  56.8 11.7 %collective-permute-start.14 = (bf16[320,1408]{1,0:T(8,128)(2,1)S(1)}, bf16[320,1408]{1,0:T(8,128)(2,1)S(1)}, u32[]{:S(2)}, u32[]{:S(2)}) collective-permute-start(bf16[320,1408]{1,0:T(8,128)(2,1)S(1)} %collective-permute-done.13.refs_1_), channel_id=1, source_target_pairs={{0,2},{2,0},{4,6},{6,4},{8,10},{10,8},{12,14},{14,12},{16,18},{18,... | collective-permute-start | bytes 2703368 | tf_op jit(solution)/shard_map/ppermute | solution.py:191
  56.8 19.3 %collective-permute-start.17 = (bf16[320,1408]{1,0:T(8,128)(2,1)S(1)}, bf16[320,1408]{1,0:T(8,128)(2,1)S(1)}, u32[]{:S(2)}, u32[]{:S(2)}) collective-permute-start(bf16[320,1408]{1,0:T(8,128)(2,1)S(1)} %collective-permute-done.13.refs_1_), channel_id=1, source_target_pairs={{0,8},{10,2},{8,16},{18,10},{16,24},{26,18},{24,28},{30,26},{28,20... | collective-permute-start | bytes 2703368 | tf_op jit(solution)/shard_map/ppermute | solution.py:191
  66.4 11.7 %collective-permute-start.12 = (bf16[320,1408]{1,0:T(8,128)(2,1)S(1)}, bf16[320,1408]{1,0:T(8,128)(2,1)S(1)}, u32[]{:S(2)}, u32[]{:S(2)}) collective-permute-start(bf16[320,1408]{1,0:T(8,128)(2,1)S(1)} %collective-permute-done.7.refs_1_), channel_id=1, source_target_pairs={{0,2},{2,0},{4,6},{6,4},{8,10},{10,8},{12,14},{14,12},{16,18},{18,... | collective-permute-start | bytes 2703368 | tf_op jit(solution)/shard_map/ppermute | solution.py:191
  66.4 19.3 %collective-permute-start.11 = (bf16[320,1408]{1,0:T(8,128)(2,1)S(1)}, bf16[320,1408]{1,0:T(8,128)(2,1)S(1)}, u32[]{:S(2)}, u32[]{:S(2)}) collective-permute-start(bf16[320,1408]{1,0:T(8,128)(2,1)S(1)} %collective-permute-done.7.refs_1_), channel_id=1, source_target_pairs={{0,8},{10,2},{8,16},{18,10},{16,24},{26,18},{24,28},{30,26},{28,20... | collective-permute-start | bytes 2703368 | tf_op jit(solution)/shard_map/ppermute | solution.py:191
  76.1 11.7 %collective-permute-start.18 = (bf16[320,1408]{1,0:T(8,128)(2,1)S(1)}, bf16[320,1408]{1,0:T(8,128)(2,1)S(1)}, u32[]{:S(2)}, u32[]{:S(2)}) collective-permute-start(bf16[320,1408]{1,0:T(8,128)(2,1)S(1)} %collective-permute-done.17.refs_1_), channel_id=1, source_target_pairs={{0,2},{2,0},{4,6},{6,4},{8,10},{10,8},{12,14},{14,12},{16,18},{18,... | collective-permute-start | bytes 2703368 | tf_op jit(solution)/shard_map/ppermute | solution.py:191
  76.1 19.3 %collective-permute-start.21 = (bf16[320,1408]{1,0:T(8,128)(2,1)S(1)}, bf16[320,1408]{1,0:T(8,128)(2,1)S(1)}, u32[]{:S(2)}, u32[]{:S(2)}) collective-permute-start(bf16[320,1408]{1,0:T(8,128)(2,1)S(1)} %collective-permute-done.17.refs_1_), channel_id=1, source_target_pairs={{0,8},{10,2},{8,16},{18,10},{16,24},{26,18},{24,28},{30,26},{28,20... | collective-permute-start | bytes 2703368 | tf_op jit(solution)/shard_map/ppermute | solution.py:191
  85.7 11.7 %collective-permute-start.16 = (bf16[320,1408]{1,0:T(8,128)(2,1)S(1)}, bf16[320,1408]{1,0:T(8,128)(2,1)S(1)}, u32[]{:S(2)}, u32[]{:S(2)}) collective-permute-start(bf16[320,1408]{1,0:T(8,128)(2,1)S(1)} %collective-permute-done.11.refs_1_), channel_id=1, source_target_pairs={{0,2},{2,0},{4,6},{6,4},{8,10},{10,8},{12,14},{14,12},{16,18},{18,... | collective-permute-start | bytes 2703368 | tf_op jit(solution)/shard_map/ppermute | solution.py:191
  85.7 19.3 %collective-permute-start.15 = (bf16[320,1408]{1,0:T(8,128)(2,1)S(1)}, bf16[320,1408]{1,0:T(8,128)(2,1)S(1)}, u32[]{:S(2)}, u32[]{:S(2)}) collective-permute-start(bf16[320,1408]{1,0:T(8,128)(2,1)S(1)} %collective-permute-done.11.refs_1_), channel_id=1, source_target_pairs={{0,8},{10,2},{8,16},{18,10},{16,24},{26,18},{24,28},{30,26},{28,20... | collective-permute-start | bytes 2703368 | tf_op jit(solution)/shard_map/ppermute | solution.py:191
  95.4 11.7 %collective-permute-start.22 = (bf16[320,1408]{1,0:T(8,128)(2,1)S(1)}, bf16[320,1408]{1,0:T(8,128)(2,1)S(1)}, u32[]{:S(2)}, u32[]{:S(2)}) collective-permute-start(bf16[320,1408]{1,0:T(8,128)(2,1)S(1)} %collective-permute-done.21.refs_1_), channel_id=1, source_target_pairs={{0,2},{2,0},{4,6},{6,4},{8,10},{10,8},{12,14},{14,12},{16,18},{18,... | collective-permute-start | bytes 2703368 | tf_op jit(solution)/shard_map/ppermute | solution.py:191
  95.4 19.3 %collective-permute-start.24 = (bf16[320,1408]{1,0:T(8,128)(2,1)S(1)}, bf16[320,1408]{1,0:T(8,128)(2,1)S(1)}, u32[]{:S(2)}, u32[]{:S(2)}) collective-permute-start(bf16[320,1408]{1,0:T(8,128)(2,1)S(1)} %collective-permute-done.21.refs_1_), channel_id=1, source_target_pairs={{0,8},{10,2},{8,16},{18,10},{16,24},{26,18},{24,28},{30,26},{28,20... | collective-permute-start | bytes 2703368 | tf_op jit(solution)/shard_map/ppermute | solution.py:191
  105.0 19.3 %collective-permute-start.19 = (bf16[320,1408]{1,0:T(8,128)(2,1)S(1)}, bf16[320,1408]{1,0:T(8,128)(2,1)S(1)}, u32[]{:S(2)}, u32[]{:S(2)}) collective-permute-start(bf16[320,1408]{1,0:T(8,128)(2,1)S(1)} %collective-permute-done.15.refs_1_), channel_id=1, source_target_pairs={{0,8},{10,2},{8,16},{18,10},{16,24},{26,18},{24,28},{30,26},{28,20... | collective-permute-start | bytes 2703368 | tf_op jit(solution)/shard_map/ppermute | solution.py:191
  114.7 12.2 %collective-permute-start.25 = (bf16[320,1408]{1,0:T(8,128)(2,1)S(1)}, bf16[320,1408]{1,0:T(8,128)(2,1)S(1)}, u32[]{:S(2)}, u32[]{:S(2)}) collective-permute-start(bf16[320,1408]{1,0:T(8,128)(2,1)S(1)} %collective-permute-done.24.refs_1_), channel_id=1, source_target_pairs={{0,2},{2,0},{4,6},{6,4},{8,10},{10,8},{12,14},{14,12},{16,18},{18,... | collective-permute-start | bytes 2703368 | tf_op jit(solution)/shard_map/ppermute | solution.py:191
  124.6 17.1 %collective-permute-start.27 = (bf16[320,1408]{1,0:T(8,128)(2,1)S(1)}, bf16[320,1408]{1,0:T(8,128)(2,1)}, u32[]{:S(2)}, u32[]{:S(2)}) collective-permute-start(bf16[320,1408]{1,0:T(8,128)(2,1)S(1)} %bitcast.8), channel_id=1, source_target_pairs={{8,0},{2,10},{16,8},{10,18},{24,16},{18,26},{28,24},{26,30},{20,28... | collective-permute-start | bytes 2703368 | tf_op jit(solution)/shard_map/ppermute | solution.py:191
  135.5 13.3 %collective-permute-start.30 = (bf16[320,1408]{1,0:T(8,128)(2,1)S(1)}, bf16[320,1408]{1,0:T(8,128)(2,1)S(1)}, u32[]{:S(2)}, u32[]{:S(2)}) collective-permute-start(bf16[320,1408]{1,0:T(8,128)(2,1)S(1)} %bitcast.7), channel_id=1, source_target_pairs={{8,0},{2,10},{16,8},{10,18},{24,16},{18,26},{28,24},{26,30},{20,28... | collective-permute-start | bytes 2703368 | tf_op jit(solution)/shard_map/ppermute | solution.py:191
  137.1 21.4 %collective-permute-start.29 = (bf16[320,1408]{1,0:T(8,128)(2,1)S(1)}, bf16[320,1408]{1,0:T(8,128)(2,1)}, u32[]{:S(2)}, u32[]{:S(2)}) collective-permute-start(bf16[320,1408]{1,0:T(8,128)(2,1)S(1)} %bitcast.6), channel_id=1, source_target_pairs={{8,0},{2,10},{16,8},{10,18},{24,16},{18,26},{28,24},{26,30},{20,28... | collective-permute-start | bytes 2703368 | tf_op jit(solution)/shard_map/ppermute | solution.py:191
  138.7 29.5 %collective-permute-start.28 = (bf16[320,1408]{1,0:T(8,128)(2,1)S(1)}, bf16[320,1408]{1,0:T(8,128)(2,1)}, u32[]{:S(2)}, u32[]{:S(2)}) collective-permute-start(bf16[320,1408]{1,0:T(8,128)(2,1)S(1)} %bitcast.5), channel_id=1, source_target_pairs={{8,0},{2,10},{16,8},{10,18},{24,16},{18,26},{28,24},{26,30},{20,28... | collective-permute-start | bytes 2703368 | tf_op jit(solution)/shard_map/ppermute | solution.py:191
  140.3 47.0 %collective-permute-start.26 = (bf16[640,1408]{1,0:T(8,128)(2,1)S(1)}, bf16[640,1408]{1,0:T(8,128)(2,1)}, u32[]{:S(2)}, u32[]{:S(2)}) collective-permute-start(bf16[640,1408]{1,0:T(8,128)(2,1)S(1)} %shard_map.40), channel_id=1, source_target_pairs={{0,1},{1,0},{2,3},{3,2},{4,5},{5,4},{6,7},{7,6},{8,9},{9,8},{10,11... | collective-permute-start | bytes 5406728 | tf_op jit(solution)/shard_map/ppermute | solution.py:213
  141.8 26.6 %collective-permute-start.31 = (bf16[320,1408]{1,0:T(8,128)(2,1)}, bf16[320,1408]{1,0:T(8,128)(2,1)}, u32[]{:S(2)}, u32[]{:S(2)}) collective-permute-start(bf16[320,1408]{1,0:T(8,128)(2,1)} %collective-permute-done.27.refs_1_), channel_id=1, source_target_pairs={{0,2},{2,0},{4,6},{6,4},{8,10},{10,8},{12,14},{14,12},{16,18},{18,... | collective-permute-start | bytes 2703368 | tf_op jit(solution)/shard_map/ppermute | solution.py:191
  148.8 19.6 %collective-permute-start.34 = (bf16[320,1408]{1,0:T(8,128)(2,1)S(1)}, bf16[320,1408]{1,0:T(8,128)(2,1)}, u32[]{:S(2)}, u32[]{:S(2)}) collective-permute-start(bf16[320,1408]{1,0:T(8,128)(2,1)S(1)} %collective-permute-done.30.refs_4_), channel_id=1, source_target_pairs={{0,2},{2,0},{4,6},{6,4},{8,10},{10,8},{12,14},{14,12},{16,18},{18,... | collective-permute-start | bytes 2703368 | tf_op jit(solution)/shard_map/ppermute | solution.py:191
  158.5 9.9 %collective-permute-start.33 = (bf16[320,1408]{1,0:T(8,128)(2,1)}, bf16[320,1408]{1,0:T(8,128)(2,1)}, u32[]{:S(2)}, u32[]{:S(2)}) collective-permute-start(bf16[320,1408]{1,0:T(8,128)(2,1)} %collective-permute-done.29.refs_3_), channel_id=1, source_target_pairs={{0,2},{2,0},{4,6},{6,4},{8,10},{10,8},{12,14},{14,12},{16,18},{18,... | collective-permute-start | bytes 2703368 | tf_op jit(solution)/shard_map/ppermute | solution.py:191
  (10 other events, 168.1 us)

commit v8 on v6

--- a/solution.py
+++ b/solution.py
@@ -118,7 +118,7 @@
 
 def add_relation(half, partners, terms, margin, weight, project=None, summands=(), dtype=jnp.float32):
     _, rows, width = half.shape
-    block = rows // 2
+    block = rows // (2 if project is None else 4)
     counts = tuple(x.shape[0] // 2 for x in partners)
     tokens = sum(counts)
     by_row = pl.BlockSpec((block, width), lambda i: (i, 0))

time: 189 us -> 191 us (1.011)
  Pallas kernels: 70.6 us -> 72.6 us
    pallas_call x13, Pallas kernels: 65.6 us -> 67.6 us  [add_relation(): pl.pallas_call(functools.partial(relation_kernel, margin, weight, counts,...]
  transfers between devices with their start and end apart: 35 -> 35, of which waited for: 15 -> 15; matrix products, arithmetic and copies ran while one was open for 0% -> 0% of each run, Pallas kernels for 31% -> 32%
where the time goes in v8:
time: 191 us; the launch traced here: 190 us
  waiting for transfers between devices  81.2 us (43%)
  Pallas kernels  72.6 us (38%)
  starting transfers between devices  34.2 us (18%)
  local copies, waits for them, and re-layouts  2.3 us (1%)
    ppermute x34, waiting for transfers between devices, move(): return lax.ppermute(after(x, *wait_for), 'seq', route)  77 us
    pallas_call x13, Pallas kernels, add_relation(): pl.pallas_call(functools.partial(relation_kernel, margin, weight, counts,...  67.6 us
    ppermute x34, starting transfers between devices, move(): return lax.ppermute(after(x, *wait_for), 'seq', route)  32.7 us
    ppermute x1, waiting for transfers between devices, local(): summands = (value, lax.ppermute(value, 'pair', route))  4.19 us
  transfers between devices with their start and end apart: 35, of which 15 were waited for; matrix products, arithmetic and copies ran while one was open for 0% of the time, Pallas kernels for 32%

profile of v8, /device:TPU:0, one launch (start us, length us, event | category | flops | bytes accessed | tf_op | source)
XLA Modules:
  0.0 190.4 jit_solution(15771211056840811519)
XLA Ops:
  0.0 3.7 %shard_map.28 = (bf16[320,1408]{1,0:T(8,128)(2,1)}, bf16[320,1408]{1,0:T(8,128)(2,1)}) custom-call(s32[1]{0:T(128)} %bitcast.which, f32[640,1408]{1,0:T(8,128)} %refs_4_.3, f32[640,1408]{1,0:T(8,128)} %teacher.3), custom_call_target="tpu_custom_call" | custom-call | flops 2703360 | bytes 5406720 | tf_op jit(solution)/shard_map/pallas_call | solution.py:68
  3.7 3.0 %collective-permute-start.4 = (bf16[320,1408]{1,0:T(8,128)(2,1)}, bf16[320,1408]{1,0:T(8,128)(2,1)S(1)}, u32[]{:S(2)}, u32[]{:S(2)}) collective-permute-start(bf16[320,1408]{1,0:T(8,128)(2,1)} %get-tuple-element.26.refs_1_), channel_id=1, source_target_pairs={{0,8},{10,2},{8,16},{18,10},{16,24},{26,18},{24,28},{30,26},{28,20... | collective-permute-start | bytes 2703368 | tf_op jit(solution)/shard_map/ppermute | solution.py:191
  8.4 9.8 %collective-permute-done.4.refs_5_ = bf16[320,1408]{1,0:T(8,128)(2,1)S(1)} collective-permute-done((bf16[320,1408]{1,0:T(8,128)(2,1)}, bf16[320,1408]{1,0:T(8,128)(2,1)S(1)}, u32[]{:S(2)}, u32[]{:S(2)}) %collective-permute-start.4) | collective-permute-done | bytes 901152 | tf_op jit(solution)/shard_map/ppermute | solution.py:191
  20.7 7.1 %collective-permute-done.refs_7_ = bf16[320,1408]{1,0:T(8,128)(2,1)S(1)} collective-permute-done((bf16[320,1408]{1,0:T(8,128)(2,1)}, bf16[320,1408]{1,0:T(8,128)(2,1)S(1)}, u32[]{:S(2)}, u32[]{:S(2)}) %collective-permute-start) | collective-permute-done | bytes 901152 | tf_op jit(solution)/shard_map/ppermute | solution.py:191
  33.1 4.3 %collective-permute-done.9.refs_1_ = bf16[320,1408]{1,0:T(8,128)(2,1)S(1)} collective-permute-done((bf16[320,1408]{1,0:T(8,128)(2,1)S(1)}, bf16[320,1408]{1,0:T(8,128)(2,1)S(1)}, u32[]{:S(2)}, u32[]{:S(2)}) %collective-permute-start.9) | collective-permute-done | bytes 901152 | tf_op jit(solution)/shard_map/ppermute | solution.py:191
  37.4 2.1 %collective-permute-start.13 = (bf16[320,1408]{1,0:T(8,128)(2,1)S(1)}, bf16[320,1408]{1,0:T(8,128)(2,1)S(1)}, u32[]{:S(2)}, u32[]{:S(2)}) collective-permute-start(bf16[320,1408]{1,0:T(8,128)(2,1)S(1)} %collective-permute-done.9.refs_1_), channel_id=1, source_target_pairs={{0,8},{10,2},{8,16},{18,10},{16,24},{26,18},{24,28},{30,26},{28,20... | collective-permute-start | bytes 2703368 | tf_op jit(solution)/shard_map/ppermute | solution.py:191
  39.5 9.0 %shard_map.30.refs_3_ = f32[640,1408]{1,0:T(8,128)S(1)} custom-call(bf16[2,640,1408]{2,1,0:T(8,128)(2,1)S(1)} %get-tuple-element.29.refs_0_, bf16[320,1408]{1,0:T(8,128)(2,1)S(1)} %copy-done.2, bf16[320,1408]{1,0:T(8,128)(2,1)S(1)} %copy-done.3, bf16[320,1408]{1,0:T(8,128)(2,1)S(1)} %collective-permute-done.2.refs_3_, ...), custom_call_target="tpu_custom_call" | custom-call | flops 6920601600 | bytes 18022400 | tf_op jit(solution)/shard_map/pallas_call | solution.py:135
  50.3 4.0 %shard_map.31.refs_3_ = f32[640,1408]{1,0:T(8,128)S(1)} custom-call(bf16[2,640,1408]{2,1,0:T(8,128)(2,1)S(1)} %get-tuple-element.29.refs_0_, bf16[320,1408]{1,0:T(8,128)(2,1)S(1)} %collective-permute-done.9.refs_1_, bf16[320,1408]{1,0:T(8,128)(2,1)S(1)} %collective-permute-done.10.refs_2_, ...), custom_call_target="tpu_custom_call", output_to_operand_aliasing={{}: (3, {})} | custom-call | flops 1730150400 | bytes 12615680 | tf_op jit(solution)/shard_map/pallas_call | solution.py:135
  54.3 2.4 %collective-permute-done.13.refs_1_ = bf16[320,1408]{1,0:T(8,128)(2,1)S(1)} collective-permute-done((bf16[320,1408]{1,0:T(8,128)(2,1)S(1)}, bf16[320,1408]{1,0:T(8,128)(2,1)S(1)}, u32[]{:S(2)}, u32[]{:S(2)}) %collective-permute-start.13) | collective-permute-done | bytes 901152 | tf_op jit(solution)/shard_map/ppermute | solution.py:191
  58.8 4.0 %shard_map.32.refs_3_ = f32[640,1408]{1,0:T(8,128)S(1)} custom-call(bf16[2,640,1408]{2,1,0:T(8,128)(2,1)S(1)} %get-tuple-element.29.refs_0_, bf16[320,1408]{1,0:T(8,128)(2,1)S(1)} %collective-permute-done.1.refs_1_, bf16[320,1408]{1,0:T(8,128)(2,1)S(1)} %collective-permute-done.8.refs_2_, ...), custom_call_target="tpu_custom_call", output_to_operand_aliasing={{}: (3, {})} | custom-call | flops 1730150400 | bytes 12615680 | tf_op jit(solution)/shard_map/pallas_call | solution.py:135
  62.8 3.6 %collective-permute-done.7.refs_1_ = bf16[320,1408]{1,0:T(8,128)(2,1)S(1)} collective-permute-done((bf16[320,1408]{1,0:T(8,128)(2,1)S(1)}, bf16[320,1408]{1,0:T(8,128)(2,1)S(1)}, u32[]{:S(2)}, u32[]{:S(2)}) %collective-permute-start.7) | collective-permute-done | bytes 901152 | tf_op jit(solution)/shard_map/ppermute | solution.py:191
  68.5 4.0 %shard_map.33.refs_3_ = f32[640,1408]{1,0:T(8,128)S(1)} custom-call(bf16[2,640,1408]{2,1,0:T(8,128)(2,1)S(1)} %get-tuple-element.29.refs_0_, bf16[320,1408]{1,0:T(8,128)(2,1)S(1)} %collective-permute-done.13.refs_1_, bf16[320,1408]{1,0:T(8,128)(2,1)S(1)} %collective-permute-done.14.refs_2_, ...), custom_call_target="tpu_custom_call", output_to_operand_aliasing={{}: (3, {})} | custom-call | flops 1730150400 | bytes 12615680 | tf_op jit(solution)/shard_map/pallas_call | solution.py:135
  72.5 3.6 %collective-permute-done.17.refs_1_ = bf16[320,1408]{1,0:T(8,128)(2,1)S(1)} collective-permute-done((bf16[320,1408]{1,0:T(8,128)(2,1)S(1)}, bf16[320,1408]{1,0:T(8,128)(2,1)S(1)}, u32[]{:S(2)}, u32[]{:S(2)}) %collective-permute-start.17) | collective-permute-done | bytes 901152 | tf_op jit(solution)/shard_map/ppermute | solution.py:191
  78.1 4.0 %shard_map.34.refs_3_ = f32[640,1408]{1,0:T(8,128)S(1)} custom-call(bf16[2,640,1408]{2,1,0:T(8,128)(2,1)S(1)} %get-tuple-element.29.refs_0_, bf16[320,1408]{1,0:T(8,128)(2,1)S(1)} %collective-permute-done.7.refs_1_, bf16[320,1408]{1,0:T(8,128)(2,1)S(1)} %collective-permute-done.12.refs_2_, ...), custom_call_target="tpu_custom_call", output_to_operand_aliasing={{}: (3, {})} | custom-call | flops 1730150400 | bytes 12615680 | tf_op jit(solution)/shard_map/pallas_call | solution.py:135
  82.1 3.6 %collective-permute-done.11.refs_1_ = bf16[320,1408]{1,0:T(8,128)(2,1)S(1)} collective-permute-done((bf16[320,1408]{1,0:T(8,128)(2,1)S(1)}, bf16[320,1408]{1,0:T(8,128)(2,1)S(1)}, u32[]{:S(2)}, u32[]{:S(2)}) %collective-permute-start.11) | collective-permute-done | bytes 901152 | tf_op jit(solution)/shard_map/ppermute | solution.py:191
  87.8 4.0 %shard_map.35.refs_3_ = f32[640,1408]{1,0:T(8,128)S(1)} custom-call(bf16[2,640,1408]{2,1,0:T(8,128)(2,1)S(1)} %get-tuple-element.29.refs_0_, bf16[320,1408]{1,0:T(8,128)(2,1)S(1)} %collective-permute-done.17.refs_1_, bf16[320,1408]{1,0:T(8,128)(2,1)S(1)} %collective-permute-done.18.refs_2_, ...), custom_call_target="tpu_custom_call", output_to_operand_aliasing={{}: (3, {})} | custom-call | flops 1730150400 | bytes 12615680 | tf_op jit(solution)/shard_map/pallas_call | solution.py:135
  91.8 3.6 %collective-permute-done.21.refs_1_ = bf16[320,1408]{1,0:T(8,128)(2,1)S(1)} collective-permute-done((bf16[320,1408]{1,0:T(8,128)(2,1)S(1)}, bf16[320,1408]{1,0:T(8,128)(2,1)S(1)}, u32[]{:S(2)}, u32[]{:S(2)}) %collective-permute-start.21) | collective-permute-done | bytes 901152 | tf_op jit(solution)/shard_map/ppermute | solution.py:191
  97.5 4.0 %shard_map.36.refs_3_ = f32[640,1408]{1,0:T(8,128)S(1)} custom-call(bf16[2,640,1408]{2,1,0:T(8,128)(2,1)S(1)} %get-tuple-element.29.refs_0_, bf16[320,1408]{1,0:T(8,128)(2,1)S(1)} %collective-permute-done.11.refs_1_, bf16[320,1408]{1,0:T(8,128)(2,1)S(1)} %collective-permute-done.16.refs_2_, ...), custom_call_target="tpu_custom_call", output_to_operand_aliasing={{}: (3, {})} | custom-call | flops 1730150400 | bytes 12615680 | tf_op jit(solution)/shard_map/pallas_call | solution.py:135
  101.5 3.6 %collective-permute-done.15.refs_1_ = bf16[320,1408]{1,0:T(8,128)(2,1)S(1)} collective-permute-done((bf16[320,1408]{1,0:T(8,128)(2,1)S(1)}, bf16[320,1408]{1,0:T(8,128)(2,1)S(1)}, u32[]{:S(2)}, u32[]{:S(2)}) %collective-permute-start.15) | collective-permute-done | bytes 901152 | tf_op jit(solution)/shard_map/ppermute | solution.py:191
  107.1 4.0 %shard_map.37.refs_3_ = f32[640,1408]{1,0:T(8,128)S(1)} custom-call(bf16[2,640,1408]{2,1,0:T(8,128)(2,1)S(1)} %get-tuple-element.29.refs_0_, bf16[320,1408]{1,0:T(8,128)(2,1)S(1)} %collective-permute-done.21.refs_1_, bf16[320,1408]{1,0:T(8,128)(2,1)S(1)} %collective-permute-done.22.refs_2_, ...), custom_call_target="tpu_custom_call", output_to_operand_aliasing={{}: (3, {})} | custom-call | flops 1730150400 | bytes 12615680 | tf_op jit(solution)/shard_map/pallas_call | solution.py:135
  111.1 3.6 %collective-permute-done.24.refs_1_ = bf16[320,1408]{1,0:T(8,128)(2,1)S(1)} collective-permute-done((bf16[320,1408]{1,0:T(8,128)(2,1)S(1)}, bf16[320,1408]{1,0:T(8,128)(2,1)S(1)}, u32[]{:S(2)}, u32[]{:S(2)}) %collective-permute-start.24) | collective-permute-done | bytes 901152 | tf_op jit(solution)/shard_map/ppermute | solution.py:191
  114.7 4.0 %shard_map.38.refs_3_ = f32[640,1408]{1,0:T(8,128)S(1)} custom-call(bf16[2,640,1408]{2,1,0:T(8,128)(2,1)S(1)} %get-tuple-element.29.refs_0_, bf16[320,1408]{1,0:T(8,128)(2,1)S(1)} %collective-permute-done.15.refs_1_, bf16[320,1408]{1,0:T(8,128)(2,1)S(1)} %collective-permute-done.20.refs_2_, ...), custom_call_target="tpu_custom_call", output_to_operand_aliasing={{}: (3, {})} | custom-call | flops 1730150400 | bytes 12615680 | tf_op jit(solution)/shard_map/pallas_call | solution.py:135
  118.7 5.7 %collective-permute-done.19.refs_1_ = bf16[320,1408]{1,0:T(8,128)(2,1)S(1)} collective-permute-done((bf16[320,1408]{1,0:T(8,128)(2,1)S(1)}, bf16[320,1408]{1,0:T(8,128)(2,1)S(1)}, u32[]{:S(2)}, u32[]{:S(2)}) %collective-permute-start.19) | collective-permute-done | bytes 901152 | tf_op jit(solution)/shard_map/ppermute | solution.py:191
  124.6 2.3 %collective-permute-start.28 = (bf16[320,1408]{1,0:T(8,128)(2,1)S(1)}, bf16[320,1408]{1,0:T(8,128)(2,1)S(1)}, u32[]{:S(2)}, u32[]{:S(2)}) collective-permute-start(bf16[320,1408]{1,0:T(8,128)(2,1)S(1)} %bitcast.8), channel_id=1, source_target_pairs={{8,0},{2,10},{16,8},{10,18},{24,16},{18,26},{28,24},{26,30},{20,28... | collective-permute-start | bytes 2703368 | tf_op jit(solution)/shard_map/ppermute | solution.py:191
  126.9 4.0 %shard_map.39.refs_3_ = f32[640,1408]{1,0:T(8,128)S(1)} custom-call(bf16[2,640,1408]{2,1,0:T(8,128)(2,1)S(1)} %get-tuple-element.29.refs_0_, bf16[320,1408]{1,0:T(8,128)(2,1)S(1)} %collective-permute-done.24.refs_1_, bf16[320,1408]{1,0:T(8,128)(2,1)S(1)} %collective-permute-done.25.refs_2_, ...), custom_call_target="tpu_custom_call", output_to_operand_aliasing={{}: (3, {})} | custom-call | flops 1730150400 | bytes 12615680 | tf_op jit(solution)/shard_map/pallas_call | solution.py:135
  130.9 5.8 %shard_map.40.refs_6_ = bf16[640,1408]{1,0:T(8,128)(2,1)S(1)} custom-call(bf16[2,640,1408]{2,1,0:T(8,128)(2,1)S(1)} %get-tuple-element.29.refs_0_, bf16[320,1408]{1,0:T(8,128)(2,1)S(1)} %collective-permute-done.19.refs_1_, bf16[320,1408]{1,0:T(8,128)(2,1)S(1)} %collective-permute-done.23.refs_2_, f32[640,1408]{1,0:T(8,128)S(1)} %shard_map.39.refs_3_, ...), custom_call_target="tpu_custom_call" | custom-call | flops 1730150400 | bytes 12615680 | tf_op jit(solution)/shard_map/pallas_call | solution.py:135
  143.0 7.0 %collective-permute-done.32.refs_5_ = bf16[320,1408]{1,0:T(8,128)(2,1)S(1)} collective-permute-done((bf16[320,1408]{1,0:T(8,128)(2,1)S(1)}, bf16[320,1408]{1,0:T(8,128)(2,1)S(1)}, u32[]{:S(2)}, u32[]{:S(2)}) %collective-permute-start.32) | collective-permute-done | bytes 901152 | tf_op jit(solution)/shard_map/ppermute | solution.py:191
  150.0 9.7 %collective-permute-done.30.refs_3_ = bf16[320,1408]{1,0:T(8,128)(2,1)S(1)} collective-permute-done((bf16[320,1408]{1,0:T(8,128)(2,1)S(1)}, bf16[320,1408]{1,0:T(8,128)(2,1)S(1)}, u32[]{:S(2)}, u32[]{:S(2)}) %collective-permute-start.30) | collective-permute-done | bytes 901152 | tf_op jit(solution)/shard_map/ppermute | solution.py:191
  159.7 9.7 %collective-permute-done.26.refs_1_ = bf16[320,1408]{1,0:T(8,128)(2,1)S(1)} collective-permute-done((bf16[320,1408]{1,0:T(8,128)(2,1)S(1)}, bf16[320,1408]{1,0:T(8,128)(2,1)S(1)}, u32[]{:S(2)}, u32[]{:S(2)}) %collective-permute-start.26) | collective-permute-done | bytes 901152 | tf_op jit(solution)/shard_map/ppermute | solution.py:191
  169.4 8.6 %shard_map.41.refs_3_ = f32[640,1408]{1,0:T(8,128)} custom-call(bf16[2,640,1408]{2,1,0:T(8,128)(2,1)S(1)} %get-tuple-element.29.refs_0_, bf16[320,1408]{1,0:T(8,128)(2,1)S(1)} %collective-permute-done.28.refs_1_, bf16[320,1408]{1,0:T(8,128)(2,1)S(1)} %collective-permute-done.29.refs_2_, bf16[320,1408]{1,0:T(8,128)(2,1)S(1)} %collective-permute-done.30.refs_3_, ...), custom_call_target="tpu_custom_call" | custom-call | flops 5190451200 | bytes 16220160 | tf_op jit(solution)/shard_map/pallas_call | solution.py:135
  178.0 4.2 %collective-permute-done.34.refs_7_ = bf16[640,1408]{1,0:T(8,128)(2,1)S(1)} collective-permute-done((bf16[640,1408]{1,0:T(8,128)(2,1)S(1)}, bf16[640,1408]{1,0:T(8,128)(2,1)S(1)}, u32[]{:S(2)}, u32[]{:S(2)}) %collective-permute-start.34) | collective-permute-done | bytes 1802272 | tf_op jit(solution)/shard_map/ppermute | solution.py:213
  182.1 8.3 %shard_map.42 = f32[640,1408]{1,0:T(8,128)} custom-call(bf16[2,640,1408]{2,1,0:T(8,128)(2,1)S(1)} %get-tuple-element.29.refs_0_, bf16[320,1408]{1,0:T(8,128)(2,1)S(1)} %collective-permute-done.26.refs_1_, bf16[320,1408]{1,0:T(8,128)(2,1)S(1)} %collective-permute-done.27.refs_2_, f32[640,1408]{1,0:T(8,128)} %shard_map.41.refs_3_, ...), custom_call_target="tpu_custom_call", output_to_operand_aliasing={{}: (3, {})} | custom-call | flops 1730150400 | bytes 12615680 | tf_op jit(solution)/shard_map/pallas_call | solution.py:135
  (62 shorter events, 30.3 us)
Async XLA Ops:
  3.7 14.4 %collective-permute-start.4 = (bf16[320,1408]{1,0:T(8,128)(2,1)}, bf16[320,1408]{1,0:T(8,128)(2,1)S(1)}, u32[]{:S(2)}, u32[]{:S(2)}) collective-permute-start(bf16[320,1408]{1,0:T(8,128)(2,1)} %get-tuple-element.26.refs_1_), channel_id=1, source_target_pairs={{0,8},{10,2},{8,16},{18,10},{16,24},{26,18},{24,28},{30,26},{28,20... | collective-permute-start | bytes 2703368 | tf_op jit(solution)/shard_map/ppermute | solution.py:191
  6.8 21.0 %collective-permute-start = (bf16[320,1408]{1,0:T(8,128)(2,1)}, bf16[320,1408]{1,0:T(8,128)(2,1)S(1)}, u32[]{:S(2)}, u32[]{:S(2)}) collective-permute-start(bf16[320,1408]{1,0:T(8,128)(2,1)} %get-tuple-element.27.refs_2_), channel_id=1, source_target_pairs={{0,8},{10,2},{8,16},{18,10},{16,24},{26,18},{24,28},{30,26},{28,20... | collective-permute-start | bytes 2703368 | tf_op jit(solution)/shard_map/ppermute | solution.py:191
  8.3 19.4 %collective-permute-start.2 = (bf16[320,1408]{1,0:T(8,128)(2,1)}, bf16[320,1408]{1,0:T(8,128)(2,1)S(1)}, u32[]{:S(2)}, u32[]{:S(2)}) collective-permute-start(bf16[320,1408]{1,0:T(8,128)(2,1)} %get-tuple-element.26.refs_1_), channel_id=1, source_target_pairs={{0,2},{2,0},{4,6},{6,4},{8,10},{10,8},{12,14},{14,12},{16,18},{18,... | collective-permute-start | bytes 2703368 | tf_op jit(solution)/shard_map/ppermute | solution.py:191
  18.1 19.3 %collective-permute-start.9 = (bf16[320,1408]{1,0:T(8,128)(2,1)S(1)}, bf16[320,1408]{1,0:T(8,128)(2,1)S(1)}, u32[]{:S(2)}, u32[]{:S(2)}) collective-permute-start(bf16[320,1408]{1,0:T(8,128)(2,1)S(1)} %collective-permute-done.4.refs_5_), channel_id=1, source_target_pairs={{0,8},{10,2},{8,16},{18,10},{16,24},{26,18},{24,28},{30,26},{28,20... | collective-permute-start | bytes 2703368 | tf_op jit(solution)/shard_map/ppermute | solution.py:191
  20.2 17.2 %collective-permute-start.3 = (bf16[320,1408]{1,0:T(8,128)(2,1)}, bf16[320,1408]{1,0:T(8,128)(2,1)S(1)}, u32[]{:S(2)}, u32[]{:S(2)}) collective-permute-start(bf16[320,1408]{1,0:T(8,128)(2,1)} %get-tuple-element.27.refs_2_), channel_id=1, source_target_pairs={{0,2},{2,0},{4,6},{6,4},{8,10},{10,8},{12,14},{14,12},{16,18},{18,... | collective-permute-start | bytes 2703368 | tf_op jit(solution)/shard_map/ppermute | solution.py:191
  20.2 19.3 %collective-permute-start.5 = (bf16[320,1408]{1,0:T(8,128)(2,1)S(1)}, bf16[320,1408]{1,0:T(8,128)(2,1)S(1)}, u32[]{:S(2)}, u32[]{:S(2)}) collective-permute-start(bf16[320,1408]{1,0:T(8,128)(2,1)S(1)} %collective-permute-done.4.refs_5_), channel_id=1, source_target_pairs={{0,2},{2,0},{4,6},{6,4},{8,10},{10,8},{12,14},{14,12},{16,18},{18,... | collective-permute-start | bytes 2703368 | tf_op jit(solution)/shard_map/ppermute | solution.py:191
  27.8 11.7 %collective-permute-start.6 = (bf16[320,1408]{1,0:T(8,128)(2,1)S(1)}, bf16[320,1408]{1,0:T(8,128)(2,1)S(1)}, u32[]{:S(2)}, u32[]{:S(2)}) collective-permute-start(bf16[320,1408]{1,0:T(8,128)(2,1)S(1)} %collective-permute-done.refs_7_), channel_id=1, source_target_pairs={{0,2},{2,0},{4,6},{6,4},{8,10},{10,8},{12,14},{14,12},{16,18},{18,... | collective-permute-start | bytes 2703368 | tf_op jit(solution)/shard_map/ppermute | solution.py:191
  27.8 20.8 %collective-permute-start.1 = (bf16[320,1408]{1,0:T(8,128)(2,1)S(1)}, bf16[320,1408]{1,0:T(8,128)(2,1)S(1)}, u32[]{:S(2)}, u32[]{:S(2)}) collective-permute-start(bf16[320,1408]{1,0:T(8,128)(2,1)S(1)} %collective-permute-done.refs_7_), channel_id=1, source_target_pairs={{0,8},{10,2},{8,16},{18,10},{16,24},{26,18},{24,28},{30,26},{28,20... | collective-permute-start | bytes 2703368 | tf_op jit(solution)/shard_map/ppermute | solution.py:191
  37.4 12.9 %collective-permute-start.10 = (bf16[320,1408]{1,0:T(8,128)(2,1)S(1)}, bf16[320,1408]{1,0:T(8,128)(2,1)S(1)}, u32[]{:S(2)}, u32[]{:S(2)}) collective-permute-start(bf16[320,1408]{1,0:T(8,128)(2,1)S(1)} %collective-permute-done.9.refs_1_), channel_id=1, source_target_pairs={{0,2},{2,0},{4,6},{6,4},{8,10},{10,8},{12,14},{14,12},{16,18},{18,... | collective-permute-start | bytes 2703368 | tf_op jit(solution)/shard_map/ppermute | solution.py:191
  37.4 19.3 %collective-permute-start.13 = (bf16[320,1408]{1,0:T(8,128)(2,1)S(1)}, bf16[320,1408]{1,0:T(8,128)(2,1)S(1)}, u32[]{:S(2)}, u32[]{:S(2)}) collective-permute-start(bf16[320,1408]{1,0:T(8,128)(2,1)S(1)} %collective-permute-done.9.refs_1_), channel_id=1, source_target_pairs={{0,8},{10,2},{8,16},{18,10},{16,24},{26,18},{24,28},{30,26},{28,20... | collective-permute-start | bytes 2703368 | tf_op jit(solution)/shard_map/ppermute | solution.py:191
  48.6 10.2 %collective-permute-start.8 = (bf16[320,1408]{1,0:T(8,128)(2,1)S(1)}, bf16[320,1408]{1,0:T(8,128)(2,1)S(1)}, u32[]{:S(2)}, u32[]{:S(2)}) collective-permute-start(bf16[320,1408]{1,0:T(8,128)(2,1)S(1)} %collective-permute-done.1.refs_1_), channel_id=1, source_target_pairs={{0,2},{2,0},{4,6},{6,4},{8,10},{10,8},{12,14},{14,12},{16,18},{18,... | collective-permute-start | bytes 2703368 | tf_op jit(solution)/shard_map/ppermute | solution.py:191
  48.8 17.6 %collective-permute-start.7 = (bf16[320,1408]{1,0:T(8,128)(2,1)S(1)}, bf16[320,1408]{1,0:T(8,128)(2,1)S(1)}, u32[]{:S(2)}, u32[]{:S(2)}) collective-permute-start(bf16[320,1408]{1,0:T(8,128)(2,1)S(1)} %collective-permute-done.1.refs_1_), channel_id=1, source_target_pairs={{0,8},{10,2},{8,16},{18,10},{16,24},{26,18},{24,28},{30,26},{28,20... | collective-permute-start | bytes 2703368 | tf_op jit(solution)/shard_map/ppermute | solution.py:191
  56.7 11.7 %collective-permute-start.14 = (bf16[320,1408]{1,0:T(8,128)(2,1)S(1)}, bf16[320,1408]{1,0:T(8,128)(2,1)S(1)}, u32[]{:S(2)}, u32[]{:S(2)}) collective-permute-start(bf16[320,1408]{1,0:T(8,128)(2,1)S(1)} %collective-permute-done.13.refs_1_), channel_id=1, source_target_pairs={{0,2},{2,0},{4,6},{6,4},{8,10},{10,8},{12,14},{14,12},{16,18},{18,... | collective-permute-start | bytes 2703368 | tf_op jit(solution)/shard_map/ppermute | solution.py:191
  56.7 19.3 %collective-permute-start.17 = (bf16[320,1408]{1,0:T(8,128)(2,1)S(1)}, bf16[320,1408]{1,0:T(8,128)(2,1)S(1)}, u32[]{:S(2)}, u32[]{:S(2)}) collective-permute-start(bf16[320,1408]{1,0:T(8,128)(2,1)S(1)} %collective-permute-done.13.refs_1_), channel_id=1, source_target_pairs={{0,8},{10,2},{8,16},{18,10},{16,24},{26,18},{24,28},{30,26},{28,20... | collective-permute-start | bytes 2703368 | tf_op jit(solution)/shard_map/ppermute | solution.py:191
  66.4 11.7 %collective-permute-start.12 = (bf16[320,1408]{1,0:T(8,128)(2,1)S(1)}, bf16[320,1408]{1,0:T(8,128)(2,1)S(1)}, u32[]{:S(2)}, u32[]{:S(2)}) collective-permute-start(bf16[320,1408]{1,0:T(8,128)(2,1)S(1)} %collective-permute-done.7.refs_1_), channel_id=1, source_target_pairs={{0,2},{2,0},{4,6},{6,4},{8,10},{10,8},{12,14},{14,12},{16,18},{18,... | collective-permute-start | bytes 2703368 | tf_op jit(solution)/shard_map/ppermute | solution.py:191
  66.4 19.3 %collective-permute-start.11 = (bf16[320,1408]{1,0:T(8,128)(2,1)S(1)}, bf16[320,1408]{1,0:T(8,128)(2,1)S(1)}, u32[]{:S(2)}, u32[]{:S(2)}) collective-permute-start(bf16[320,1408]{1,0:T(8,128)(2,1)S(1)} %collective-permute-done.7.refs_1_), channel_id=1, source_target_pairs={{0,8},{10,2},{8,16},{18,10},{16,24},{26,18},{24,28},{30,26},{28,20... | collective-permute-start | bytes 2703368 | tf_op jit(solution)/shard_map/ppermute | solution.py:191
  76.1 11.7 %collective-permute-start.18 = (bf16[320,1408]{1,0:T(8,128)(2,1)S(1)}, bf16[320,1408]{1,0:T(8,128)(2,1)S(1)}, u32[]{:S(2)}, u32[]{:S(2)}) collective-permute-start(bf16[320,1408]{1,0:T(8,128)(2,1)S(1)} %collective-permute-done.17.refs_1_), channel_id=1, source_target_pairs={{0,2},{2,0},{4,6},{6,4},{8,10},{10,8},{12,14},{14,12},{16,18},{18,... | collective-permute-start | bytes 2703368 | tf_op jit(solution)/shard_map/ppermute | solution.py:191
  76.1 19.3 %collective-permute-start.21 = (bf16[320,1408]{1,0:T(8,128)(2,1)S(1)}, bf16[320,1408]{1,0:T(8,128)(2,1)S(1)}, u32[]{:S(2)}, u32[]{:S(2)}) collective-permute-start(bf16[320,1408]{1,0:T(8,128)(2,1)S(1)} %collective-permute-done.17.refs_1_), channel_id=1, source_target_pairs={{0,8},{10,2},{8,16},{18,10},{16,24},{26,18},{24,28},{30,26},{28,20... | collective-permute-start | bytes 2703368 | tf_op jit(solution)/shard_map/ppermute | solution.py:191
  85.7 11.7 %collective-permute-start.16 = (bf16[320,1408]{1,0:T(8,128)(2,1)S(1)}, bf16[320,1408]{1,0:T(8,128)(2,1)S(1)}, u32[]{:S(2)}, u32[]{:S(2)}) collective-permute-start(bf16[320,1408]{1,0:T(8,128)(2,1)S(1)} %collective-permute-done.11.refs_1_), channel_id=1, source_target_pairs={{0,2},{2,0},{4,6},{6,4},{8,10},{10,8},{12,14},{14,12},{16,18},{18,... | collective-permute-start | bytes 2703368 | tf_op jit(solution)/shard_map/ppermute | solution.py:191
  85.7 19.3 %collective-permute-start.15 = (bf16[320,1408]{1,0:T(8,128)(2,1)S(1)}, bf16[320,1408]{1,0:T(8,128)(2,1)S(1)}, u32[]{:S(2)}, u32[]{:S(2)}) collective-permute-start(bf16[320,1408]{1,0:T(8,128)(2,1)S(1)} %collective-permute-done.11.refs_1_), channel_id=1, source_target_pairs={{0,8},{10,2},{8,16},{18,10},{16,24},{26,18},{24,28},{30,26},{28,20... | collective-permute-start | bytes 2703368 | tf_op jit(solution)/shard_map/ppermute | solution.py:191
  95.4 11.7 %collective-permute-start.22 = (bf16[320,1408]{1,0:T(8,128)(2,1)S(1)}, bf16[320,1408]{1,0:T(8,128)(2,1)S(1)}, u32[]{:S(2)}, u32[]{:S(2)}) collective-permute-start(bf16[320,1408]{1,0:T(8,128)(2,1)S(1)} %collective-permute-done.21.refs_1_), channel_id=1, source_target_pairs={{0,2},{2,0},{4,6},{6,4},{8,10},{10,8},{12,14},{14,12},{16,18},{18,... | collective-permute-start | bytes 2703368 | tf_op jit(solution)/shard_map/ppermute | solution.py:191
  95.4 19.3 %collective-permute-start.24 = (bf16[320,1408]{1,0:T(8,128)(2,1)S(1)}, bf16[320,1408]{1,0:T(8,128)(2,1)S(1)}, u32[]{:S(2)}, u32[]{:S(2)}) collective-permute-start(bf16[320,1408]{1,0:T(8,128)(2,1)S(1)} %collective-permute-done.21.refs_1_), channel_id=1, source_target_pairs={{0,8},{10,2},{8,16},{18,10},{16,24},{26,18},{24,28},{30,26},{28,20... | collective-permute-start | bytes 2703368 | tf_op jit(solution)/shard_map/ppermute | solution.py:191
  105.0 19.3 %collective-permute-start.19 = (bf16[320,1408]{1,0:T(8,128)(2,1)S(1)}, bf16[320,1408]{1,0:T(8,128)(2,1)S(1)}, u32[]{:S(2)}, u32[]{:S(2)}) collective-permute-start(bf16[320,1408]{1,0:T(8,128)(2,1)S(1)} %collective-permute-done.15.refs_1_), channel_id=1, source_target_pairs={{0,8},{10,2},{8,16},{18,10},{16,24},{26,18},{24,28},{30,26},{28,20... | collective-permute-start | bytes 2703368 | tf_op jit(solution)/shard_map/ppermute | solution.py:191
  114.7 12.2 %collective-permute-start.25 = (bf16[320,1408]{1,0:T(8,128)(2,1)S(1)}, bf16[320,1408]{1,0:T(8,128)(2,1)S(1)}, u32[]{:S(2)}, u32[]{:S(2)}) collective-permute-start(bf16[320,1408]{1,0:T(8,128)(2,1)S(1)} %collective-permute-done.24.refs_1_), channel_id=1, source_target_pairs={{0,2},{2,0},{4,6},{6,4},{8,10},{10,8},{12,14},{14,12},{16,18},{18,... | collective-permute-start | bytes 2703368 | tf_op jit(solution)/shard_map/ppermute | solution.py:191
  124.6 18.4 %collective-permute-start.28 = (bf16[320,1408]{1,0:T(8,128)(2,1)S(1)}, bf16[320,1408]{1,0:T(8,128)(2,1)S(1)}, u32[]{:S(2)}, u32[]{:S(2)}) collective-permute-start(bf16[320,1408]{1,0:T(8,128)(2,1)S(1)} %bitcast.8), channel_id=1, source_target_pairs={{8,0},{2,10},{16,8},{10,18},{24,16},{18,26},{28,24},{26,30},{20,28... | collective-permute-start | bytes 2703368 | tf_op jit(solution)/shard_map/ppermute | solution.py:191
  136.8 13.3 %collective-permute-start.32 = (bf16[320,1408]{1,0:T(8,128)(2,1)S(1)}, bf16[320,1408]{1,0:T(8,128)(2,1)S(1)}, u32[]{:S(2)}, u32[]{:S(2)}) collective-permute-start(bf16[320,1408]{1,0:T(8,128)(2,1)S(1)} %bitcast.7), channel_id=1, source_target_pairs={{8,0},{2,10},{16,8},{10,18},{24,16},{18,26},{28,24},{26,30},{20,28... | collective-permute-start | bytes 2703368 | tf_op jit(solution)/shard_map/ppermute | solution.py:191
  138.4 21.3 %collective-permute-start.30 = (bf16[320,1408]{1,0:T(8,128)(2,1)S(1)}, bf16[320,1408]{1,0:T(8,128)(2,1)S(1)}, u32[]{:S(2)}, u32[]{:S(2)}) collective-permute-start(bf16[320,1408]{1,0:T(8,128)(2,1)S(1)} %bitcast.6), channel_id=1, source_target_pairs={{8,0},{2,10},{16,8},{10,18},{24,16},{18,26},{28,24},{26,30},{20,28... | collective-permute-start | bytes 2703368 | tf_op jit(solution)/shard_map/ppermute | solution.py:191
  140.0 29.4 %collective-permute-start.26 = (bf16[320,1408]{1,0:T(8,128)(2,1)S(1)}, bf16[320,1408]{1,0:T(8,128)(2,1)S(1)}, u32[]{:S(2)}, u32[]{:S(2)}) collective-permute-start(bf16[320,1408]{1,0:T(8,128)(2,1)S(1)} %bitcast.5), channel_id=1, source_target_pairs={{8,0},{2,10},{16,8},{10,18},{24,16},{18,26},{28,24},{26,30},{20,28... | collective-permute-start | bytes 2703368 | tf_op jit(solution)/shard_map/ppermute | solution.py:191
  141.5 40.6 %collective-permute-start.34 = (bf16[640,1408]{1,0:T(8,128)(2,1)S(1)}, bf16[640,1408]{1,0:T(8,128)(2,1)S(1)}, u32[]{:S(2)}, u32[]{:S(2)}) collective-permute-start(bf16[640,1408]{1,0:T(8,128)(2,1)S(1)} %shard_map.40.refs_6_), channel_id=1, source_target_pairs={{0,1},{1,0},{2,3},{3,2},{4,5},{5,4},{6,7},{7,6},{8,9},{9,8},{10,11... | collective-permute-start | bytes 5406728 | tf_op jit(solution)/shard_map/ppermute | solution.py:213
  143.0 26.3 %collective-permute-start.29 = (bf16[320,1408]{1,0:T(8,128)(2,1)S(1)}, bf16[320,1408]{1,0:T(8,128)(2,1)S(1)}, u32[]{:S(2)}, u32[]{:S(2)}) collective-permute-start(bf16[320,1408]{1,0:T(8,128)(2,1)S(1)} %collective-permute-done.28.refs_1_), channel_id=1, source_target_pairs={{0,2},{2,0},{4,6},{6,4},{8,10},{10,8},{12,14},{14,12},{16,18},{18,... | collective-permute-start | bytes 2703368 | tf_op jit(solution)/shard_map/ppermute | solution.py:191
  150.0 19.3 %collective-permute-start.33 = (bf16[320,1408]{1,0:T(8,128)(2,1)S(1)}, bf16[320,1408]{1,0:T(8,128)(2,1)S(1)}, u32[]{:S(2)}, u32[]{:S(2)}) collective-permute-start(bf16[320,1408]{1,0:T(8,128)(2,1)S(1)} %collective-permute-done.32.refs_5_), channel_id=1, source_target_pairs={{0,2},{2,0},{4,6},{6,4},{8,10},{10,8},{12,14},{14,12},{16,18},{18,... | collective-permute-start | bytes 2703368 | tf_op jit(solution)/shard_map/ppermute | solution.py:191
  159.7 9.7 %collective-permute-start.31 = (bf16[320,1408]{1,0:T(8,128)(2,1)S(1)}, bf16[320,1408]{1,0:T(8,128)(2,1)S(1)}, u32[]{:S(2)}, u32[]{:S(2)}) collective-permute-start(bf16[320,1408]{1,0:T(8,128)(2,1)S(1)} %collective-permute-done.30.refs_3_), channel_id=1, source_target_pairs={{0,2},{2,0},{4,6},{6,4},{8,10},{10,8},{12,14},{14,12},{16,18},{18,... | collective-permute-start | bytes 2703368 | tf_op jit(solution)/shard_map/ppermute | solution.py:191
  (7 other events, 72.0 us)
